TPU v7x, 32 devices: a whole 2x2x4 slice. The times are simulated.
32 devices in a mesh: row: 8 (over z, core), col: 4 (over y, x).
Axes of the slice: x: 2, y: 2, z: 4, core: 2. Of those that a mesh axis runs over, the one named last changes fastest.
Arguments:
- f_blocks: bfloat16 [16384, 2048], P('row', 'col'), may hold values from -0.25 to 0.25
- block_cols: int32 [256, 32], P('row', 'col'), may hold values from 0 to 23, as said below
- block_counts: int32 [256, 4], P('row', 'col'), may hold values from 1 to 8, as said below
- p_matrix: bfloat16 [12288, 2048], P('row', 'col'), may hold values from -6 to 6
Outputs:
- product: bfloat16 [16384, 2048], P('row', 'col')
Inputs may be any that keep to these rules, and one draw needn't show every extreme that they name: `block_cols`: within one block row of one stored tile the 8 listed block columns are distinct, padded slots included. `block_counts`: some block row of every stored tile is full.
All inputs are finite; a program needn't handle non-finite values.
Results may differ from a plain program's by a relative error of at most 0.001.
Values may be sent and summed in bfloat16 or wider, within the bound.
No kernel may reach another device: no remote copies, remote signals or barrier semaphores. Data moves between devices by JAX's collectives and lax.ppermute only.
A program may use at most 64 MiB of HBM per device.

v0:
```python
import jax
import jax.numpy as jnp
from jax import lax
from jax.sharding import PartitionSpec as P


def shifted(block, axis, distance):
    devices = range(lax.axis_size(axis))
    route = [((i - distance) % len(devices), i) for i in devices]
    return lax.ppermute(block, axis, route)


def listed_product(strips, cols, p_tile, depth, edge):
    nrows, slots = cols.shape
    stacked = p_tile.reshape(depth, edge, p_tile.shape[1])
    picked = stacked[cols].reshape(nrows, slots * edge, p_tile.shape[1])
    left = strips.reshape(nrows, edge, slots * edge)
    result = jnp.einsum("rax,rxc->rac", left, picked, preferred_element_type=jnp.float32)
    return result.reshape(nrows * edge, p_tile.shape[1])


def body(f_blocks, block_cols, block_counts, p_matrix):
    nrows, slots = block_cols.shape
    edge = 64
    depth = p_matrix.shape[0] // edge
    live = lax.broadcasted_iota(jnp.int32, (nrows, slots), 1) < block_counts
    p_second = shifted(p_matrix, "row", -1)
    viewed = f_blocks.reshape(nrows, edge, slots, edge)
    masked = jnp.where(live[:, None, :, None], viewed, jnp.zeros((), f_blocks.dtype)).reshape(
        f_blocks.shape
    )
    following = shifted((masked, block_cols), "col", -1)
    total = listed_product(masked, block_cols, p_matrix, depth, edge)
    total = total + listed_product(following[0], following[1], p_second, depth, edge)
    return total.astype(jnp.bfloat16)


def solution(mesh):
    return jax.shard_map(
        body,
        mesh=mesh,
        in_specs=(P("row", "col"), P("row", "col"), P("row", "col"), P("row", "col")),
        out_specs=P("row", "col"),
        check_vma=False,
    )
```

profile of v0, /device:TPU:0, one launch (start us, length us, event | category | flops | bytes accessed | tf_op | source)
XLA Modules:
  0.0 78.0 jit_solution(17289075683362572554)
XLA Ops:
  0.0 0.7 iota_compare_fusion
  0.7 0.6 broadcast_in_dim.34
  1.3 2.8 %broadcast_in_dim.35 = pred[2048,512]{1,0:T(8,128)(4,1)S(1)} reshape(pred[32,64,8,64]{3,2,1,0:T(8,128)(4,1)S(1)} %broadcast_in_dim.34) | data formatting | bytes 2097152 | tf_op jit(solution)/shard_map/jit(_where)/broadcast_in_dim | solution.py:29
  4.1 0.0 copy-start
  4.1 0.0 copy-start.1
  4.2 3.2 %broadcast_select_fusion = bf16[2048,512]{1,0:T(8,128)(2,1)} fusion(pred[2048,512]{1,0:T(8,128)(4,1)S(1)} %broadcast_in_dim.35, bf16[2048,512]{1,0:T(8,128)(2,1)} %param.4), kind=kLoop, calls=%fused_computation.6 | loop fusion | flops 1048576 | bytes 5242880 | tf_op jit(solution)/shard_map/jit(_where)/select_n | solution.py:29
  7.4 3.9 %collective-permute-start = (bf16[2048,512]{1,0:T(8,128)(2,1)}, bf16[2048,512]{1,0:T(8,128)(2,1)}, u32[]{:S(2)}, u32[]{:S(2)}) collective-permute-start(bf16[2048,512]{1,0:T(8,128)(2,1)} %broadcast_select_fusion), channel_id=1, source_target_pairs={{1,0},{2,1},{3,2},{0,3},{5,4},{6,5},{7,6},{4,7},{9,8},{10,9},{11,1... | collective-permute-start | bytes 6291464 | tf_op jit(solution)/shard_map/ppermute | solution.py:10
  11.3 0.0 copy-done
  11.3 2.8 %collective-permute-start.1 = (bf16[1536,512]{1,0:T(8,128)(2,1)S(1)}, bf16[1536,512]{1,0:T(8,128)(2,1)S(1)}, u32[]{:S(2)}, u32[]{:S(2)}) collective-permute-start(bf16[1536,512]{1,0:T(8,128)(2,1)S(1)} %copy-done), channel_id=1, source_target_pairs={{4,0},{8,4},{12,8},{16,12},{20,16},{24,20},{28,24},{0,28},{5,1},{9... | collective-permute-start | bytes 4718600 | tf_op jit(solution)/shard_map/ppermute | solution.py:10
  14.0 0.0 copy-done.1
  14.0 0.5 collective-permute-start.2
  14.6 0.1 broadcast_in_dim.29
  14.7 0.1 broadcast_in_dim.30
  14.8 0.1 copy.5
  14.9 0.1 reshape.53
  15.0 9.7 %gather_fusion = bf16[256,64,512]{2,1,0:T(8,128)(2,1)} fusion(bf16[24,64,512]{2,1,0:T(8,128)(2,1)S(1)} %bitcast.13, s32[1024]{0:T(1024)S(1)} %pad_clamp_fusion.1), kind=kCustom, calls=%fused_computation | custom fusion | bytes 33555456 | tf_op jit(solution)/shard_map/gather | solution.py:16
  24.7 11.3 %fusion = f32[32,64,512]{2,1,0:T(8,128)} fusion(bf16[32,512,512]{2,1,0:T(8,128)(2,1)} %bitcast.16, bf16[32,64,512]{2,1,0:T(8,128)(2,1)} %bitcast.17, pred[32,512]{1,0:T(8,128)(4,1)S(1)} %broadcast_in_dim.30), kind=kOutput, calls=%fused_computation.3 | convolution fusion | flops 1074790400 | bytes 23085056 | tf_op jit(solution)/shard_map/rax,rxc->rac/dot_general | solution.py:18
  36.1 20.5 %collective-permute-done.2 = s32[32,8]{0,1:T(8,128)S(1)} collective-permute-done((s32[32,8]{0,1:T(8,128)S(1)}, s32[32,8]{0,1:T(8,128)S(1)}, u32[]{:S(2)}, u32[]{:S(2)}) %collective-permute-start.2) | collective-permute-done | bytes 1056 | tf_op jit(solution)/shard_map/ppermute | solution.py:10
  56.5 0.1 copy.6
  56.6 0.1 reshape.61
  56.7 0.0 collective-permute-done.1
  56.7 9.7 %gather_fusion.1 = bf16[256,64,512]{2,1,0:T(8,128)(2,1)} fusion(bf16[24,64,512]{2,1,0:T(8,128)(2,1)S(1)} %bitcast.14, s32[1024]{0:T(1024)S(1)} %pad_clamp_fusion), kind=kCustom, calls=%fused_computation.1 | custom fusion | bytes 33555456 | tf_op jit(solution)/shard_map/gather | solution.py:16
  66.5 0.0 collective-permute-done
  66.5 11.6 %add_convert_fusion = bf16[32,64,512]{2,1,0:T(8,128)(2,1)} fusion(f32[32,64,512]{2,1,0:T(8,128)} %fusion, bf16[32,64,512]{2,1,0:T(8,128)(2,1)} %bitcast.4, bf16[32,512,512]{2,1,0:T(8,128)(2,1)} %bitcast.15), kind=kOutput, calls=%fused_computation.2 | convolution fusion | flops 1075838976 | bytes 25165824 | tf_op jit(solution)/shard_map/rax,rxc->rac/dot_general | solution.py:18
  (4 shorter events, 0.0 us)
Async XLA Ops:
  4.1 7.2 %copy-start = (bf16[1536,512]{1,0:T(8,128)(2,1)S(1)}, bf16[1536,512]{1,0:T(8,128)(2,1)}, u32[]{:S(2)}) copy-start(bf16[1536,512]{1,0:T(8,128)(2,1)} %param.7) | copy-start | bytes 4718596
  4.1 9.9 %copy-start.1 = (s32[32,8]{0,1:T(8,128)S(1)}, s32[32,8]{0,1:T(8,128)}, u32[]{:S(2)}) copy-start(s32[32,8]{0,1:T(8,128)} %param.5) | copy-start | bytes 3076
  7.4 59.1 %collective-permute-start = (bf16[2048,512]{1,0:T(8,128)(2,1)}, bf16[2048,512]{1,0:T(8,128)(2,1)}, u32[]{:S(2)}, u32[]{:S(2)}) collective-permute-start(bf16[2048,512]{1,0:T(8,128)(2,1)} %broadcast_select_fusion), channel_id=1, source_target_pairs={{1,0},{2,1},{3,2},{0,3},{5,4},{6,5},{7,6},{4,7},{9,8},{10,9},{11,1... | collective-permute-start | bytes 6291464 | tf_op jit(solution)/shard_map/ppermute | solution.py:10
  11.3 45.4 %collective-permute-start.1 = (bf16[1536,512]{1,0:T(8,128)(2,1)S(1)}, bf16[1536,512]{1,0:T(8,128)(2,1)S(1)}, u32[]{:S(2)}, u32[]{:S(2)}) collective-permute-start(bf16[1536,512]{1,0:T(8,128)(2,1)S(1)} %copy-done), channel_id=1, source_target_pairs={{4,0},{8,4},{12,8},{16,12},{20,16},{24,20},{28,24},{0,28},{5,1},{9... | collective-permute-start | bytes 4718600 | tf_op jit(solution)/shard_map/ppermute | solution.py:10
  14.0 42.5 %collective-permute-start.2 = (s32[32,8]{0,1:T(8,128)S(1)}, s32[32,8]{0,1:T(8,128)S(1)}, u32[]{:S(2)}, u32[]{:S(2)}) collective-permute-start(s32[32,8]{0,1:T(8,128)S(1)} %copy-done.1), channel_id=1, source_target_pairs={{1,0},{2,1},{3,2},{0,3},{5,4},{6,5},{7,6},{4,7},{9,8},{10,9},{11,1... | collective-permute-start | bytes 3080 | tf_op jit(solution)/shard_map/ppermute | solution.py:10
where the time goes:
time: 78.2 us; the launch traced here: 78 us
  local copies, waits for them, and re-layouts  23.4 us (30%)
  matrix products  22.9 us (29%)
  waiting for transfers between devices  20.5 us (26%)
  starting transfers between devices  7.19 us (9%)
  other arithmetic  3.98 us (5%)
    dot_general x2, matrix products, listed_product(): jnp.einsum('rax,rxc->rac', left, picked, preferred_element_type=jnp.float32)  22.9 us
    ppermute x3, waiting for transfers between devices, shifted(): return lax.ppermute(block, axis, route)  20.5 us
    gather x2, local copies, waits for them, and re-layouts, listed_product(): picked = stacked[cols].reshape(nrows, slots * edge, p_tile.shape[1])  19.5 us
    ppermute x3, starting transfers between devices, shifted(): return lax.ppermute(block, axis, route)  7.19 us
    broadcast_in_dim x4, local copies, waits for them, and re-layouts, body(): jnp.where(live[:, None, :, None], viewed, jnp.zeros((), f_blocks.dtype))  3.6 us
    select_n x1, other arithmetic, body(): jnp.where(live[:, None, :, None], viewed, jnp.zeros((), f_blocks.dtype))  3.23 us
  transfers between devices with their start and end apart: 3, of which 1 were waited for; matrix products, arithmetic and copies ran while one was open for 40% of the time, Pallas kernels for 0%

commit v1 on v0

v1 whole, which is shorter than its diff:
```python
import functools

import jax
import jax.numpy as jnp
from jax import lax
from jax.experimental import pallas as pl
from jax.experimental.pallas import tpu as pltpu
from jax.sharding import PartitionSpec as P

LANES = 128
GROUP = 4
CHUNKS = 4


def shifted(block, axis, distance):
    devices = range(lax.axis_size(axis))
    route = [((i - distance) % len(devices), i) for i in devices]
    return lax.ppermute(block, axis, route)


def spread(marked, first_row, strip_ref, dense_refs, edge, slots):
    for dense in dense_refs:
        dense[...] = jnp.zeros_like(dense)
    high = lax.broadcasted_iota(jnp.int32, (edge, LANES), 1) >= edge
    for pair in range(slots // 2):
        for r, dense in enumerate(dense_refs):
            here = strip_ref[pl.ds(r * edge, edge), pl.ds(pair * LANES, LANES)]
            swapped = jnp.concatenate([here[:, edge:], here[:, :edge]], axis=1)
            for half in range(2):
                column = marked[first_row + r, pair * 2 + half]
                odd = column % 2
                value = jnp.where(odd == half, here, swapped)
                tile = pl.ds(pl.multiple_of((column // 2) * LANES, LANES), LANES)
                mine = high == (odd == 1)
                dense[:, tile] = jnp.where(mine, value, dense[:, tile])


def group_product(marked, first_row, strip_ref, p_ref, dense_refs, edge, slots):
    spread(marked, first_row, strip_ref, dense_refs, edge, slots)
    depth = p_ref.shape[0]
    left = jnp.concatenate([dense[:, :depth] for dense in dense_refs], axis=0)
    return jnp.dot(left, p_ref[...], preferred_element_type=jnp.float32)


def first_kernel(edge, slots, marked, strip_ref, p_ref, total_ref, *dense_refs):
    row = pl.program_id(0) * len(dense_refs)
    total_ref[...] = group_product(marked, row, strip_ref, p_ref, dense_refs, edge, slots)


def second_kernel(edge, slots, start, marked, strip_ref, p_ref, total_ref, _, out_ref, *dense_refs):
    row = start + pl.program_id(0) * len(dense_refs)
    product = group_product(marked, row, strip_ref, p_ref, dense_refs, edge, slots)
    out_ref[...] = (total_ref[...] + product).astype(out_ref.dtype)


def dense_scratch(edge, depth):
    return [pltpu.VMEM((edge, depth + LANES), jnp.bfloat16)] * GROUP


def cost(rows, depth, width, extra):
    return pl.CostEstimate(
        flops=2 * rows * depth * width, bytes_accessed=2 * (rows * width + depth * width) + extra, transcendentals=0
    )


def first_product(marked, strips, p_tile):
    nrows, slots = marked.shape
    edge = strips.shape[0] // nrows
    depth, width = p_tile.shape
    tall = GROUP * edge
    return pl.pallas_call(
        functools.partial(first_kernel, edge, slots),
        grid_spec=pltpu.PrefetchScalarGridSpec(
            num_scalar_prefetch=1,
            grid=(nrows // GROUP,),
            in_specs=[
                pl.BlockSpec((tall, strips.shape[1]), lambda g, m: (g, 0)),
                pl.BlockSpec((depth, width), lambda g, m: (0, 0)),
            ],
            out_specs=pl.BlockSpec((tall, width), lambda g, m: (g, 0)),
            scratch_shapes=dense_scratch(edge, depth),
        ),
        out_shape=jax.ShapeDtypeStruct((nrows * edge, width), jnp.float32),
        cost_estimate=cost(nrows * edge, depth, width, 4 * nrows * edge * width),
        compiler_params=pltpu.CompilerParams(vmem_limit_bytes=24 << 20),
        name="first_step",
    )(marked, strips, p_tile)


def second_product(start, marked, part, p_tile, total, out):
    nrows, slots = marked.shape
    edge = total.shape[0] // nrows
    depth, width = p_tile.shape
    tall = GROUP * edge
    offset = start // GROUP
    out_shape = jax.ShapeDtypeStruct((nrows * edge, width), jnp.bfloat16)
    operands = (marked, part, p_tile, total, total if out is None else out)
    return pl.pallas_call(
        functools.partial(second_kernel, edge, slots, start),
        grid_spec=pltpu.PrefetchScalarGridSpec(
            num_scalar_prefetch=1,
            grid=(part.shape[0] // tall,),
            in_specs=[
                pl.BlockSpec((tall, part.shape[1]), lambda g, m: (g, 0)),
                pl.BlockSpec((depth, width), lambda g, m: (0, 0)),
                pl.BlockSpec((tall, width), lambda g, m: (g + offset, 0)),
                pl.BlockSpec(memory_space=pl.ANY),
            ],
            out_specs=pl.BlockSpec((tall, width), lambda g, m: (g + offset, 0)),
            scratch_shapes=dense_scratch(edge, depth),
        ),
        out_shape=out_shape,
        input_output_aliases={} if out is None else {4: 0},
        cost_estimate=cost(part.shape[0], depth, width, 6 * part.shape[0] * width),
        compiler_params=pltpu.CompilerParams(vmem_limit_bytes=24 << 20),
        name="second_step",
    )(*operands)


def body(f_blocks, block_cols, block_counts, p_matrix):
    nrows, slots = block_cols.shape
    edge = f_blocks.shape[0] // nrows
    spare = p_matrix.shape[0] // edge
    live = lax.broadcasted_iota(jnp.int32, (nrows, slots), 1) < block_counts
    marked = jnp.where(live, block_cols, spare)
    marked_next = shifted(marked, "col", -1)
    step = nrows // CHUNKS
    parts = []
    for c in range(CHUNKS):
        parts.append(shifted(f_blocks[c * step * edge : (c + 1) * step * edge], "col", -1))
    p_second = shifted(p_matrix, "row", -1)
    total = first_product(marked, f_blocks, p_matrix)
    out = None
    for c in range(CHUNKS):
        out = second_product(c * step, marked_next, parts[c], p_second, total, out)
    return out


def solution(mesh):
    return jax.shard_map(
        body,
        mesh=mesh,
        in_specs=(P("row", "col"), P("row", "col"), P("row", "col"), P("row", "col")),
        out_specs=P("row", "col"),
        check_vma=False,
    )
```

time: 78.2 us -> 69.2 us (0.88)
  matrix products: 22.9 us -> 0 us
  Pallas kernels: 0 us -> 20.9 us
  local copies, waits for them, and re-layouts: 23.4 us -> 5.98 us
  waiting for transfers between devices: 20.5 us -> 29.2 us
  starting transfers between devices: 7.19 us -> 12.8 us
  other arithmetic: 3.98 us -> 0.07 us
    dot_general x2 -> x0, matrix products: 22.9 us -> none  [listed_product(): jnp.einsum('rax,rxc->rac', left, picked, preferred_element_type=jnp.float32)]
    pallas_call x0 -> x5, Pallas kernels: none -> 20.9 us  [the longest x4 13.2 us: second_product(): pl.pallas_call(functools.partial(second_kernel, edge, slots, start), grid...]
    gather x2 -> x0, local copies, waits for them, and re-layouts: 19.5 us -> none  [listed_product(): picked = stacked[cols].reshape(nrows, slots * edge, p_tile.shape[1])]
    ppermute x3 -> x6, waiting for transfers between devices: 20.5 us -> 29.2 us  [shifted(): return lax.ppermute(block, axis, route)]
    ppermute x3 -> x6, starting transfers between devices: 7.19 us -> 12.8 us  [shifted(): return lax.ppermute(block, axis, route)]
    broadcast_in_dim x6 -> x0, local copies, waits for them, and re-layouts: 3.78 us -> none  [the longest x4 3.6 us: body(): jnp.where(live[:, None, :, None], viewed, jnp.zeros((), f_blocks.dtype))]
    select_n x3 -> x1, other arithmetic: 3.24 us -> 0.07 us  [body(): marked = jnp.where(live, block_cols, spare)]
    unnamed x4 -> x9, local copies, waits for them, and re-layouts: 0.01 us -> 3.08 us
  transfers between devices with their start and end apart: 3 -> 6, of which waited for: 1 -> 1; matrix products, arithmetic and copies ran while one was open for 40% -> 4% of each run, Pallas kernels for 0% -> 25%
where the time goes in v1:
time: 69.2 us; the launch traced here: 69 us
  waiting for transfers between devices  29.2 us (42%)
  Pallas kernels  20.9 us (30%)
  starting transfers between devices  12.8 us (18%)
  local copies, waits for them, and re-layouts  5.98 us (9%)
    ppermute x6, waiting for transfers between devices, shifted(): return lax.ppermute(block, axis, route)  29.2 us
    pallas_call x4, Pallas kernels, second_product(): pl.pallas_call(functools.partial(second_kernel, edge, slots, start), grid...  13.2 us
    ppermute x6, starting transfers between devices, shifted(): return lax.ppermute(block, axis, route)  12.8 us
    pallas_call x1, Pallas kernels, first_product(): pl.pallas_call(functools.partial(first_kernel, edge, slots), grid_spec=pl...  7.72 us
    unnamed x9, local copies, waits for them, and re-layouts  3.08 us
    slice x1, local copies, waits for them, and re-layouts, body(): f_blocks[c * step * edge:(c + 1) * step * edge]  2.9 us
  transfers between devices with their start and end apart: 6, of which 1 were waited for; matrix products, arithmetic and copies ran while one was open for 4% of the time, Pallas kernels for 25%

profile of v1, /device:TPU:0, one launch (start us, length us, event | category | flops | bytes accessed | tf_op | source)
XLA Modules:
  0.0 69.0 jit_solution(3191911624402809648)
XLA Ops:
  0.0 4.5 %collective-permute-start.2 = (bf16[1536,512]{1,0:T(8,128)(2,1)}, bf16[1536,512]{1,0:T(8,128)(2,1)S(1)}, u32[]{:S(2)}, u32[]{:S(2)}) collective-permute-start(bf16[1536,512]{1,0:T(8,128)(2,1)} %p_ref.1), channel_id=1, source_target_pairs={{4,0},{8,4},{12,8},{16,12},{20,16},{24,20},{28,24},{0,28},{5,1},{9... | collective-permute-start | bytes 4718600 | tf_op jit(solution)/shard_map/ppermute | solution.py:18
  4.5 2.9 %fusion.1 = (bf16[512,512]{1,0:T(8,128)(2,1)}, bf16[512,512]{1,0:T(8,128)(2,1)}, bf16[512,512]{1,0:T(8,128)(2,1)}, bf16[512,512]{1,0:T(8,128)(2,1)}) fusion(bf16[2048,512]{1,0:T(8,128)(2,1)} %strip_ref.1), kind=kLoop, calls=%fused_computation.2 | loop fusion | bytes 4194304 | tf_op jit(solution)/shard_map/slice | solution.py:130
  7.4 2.4 %collective-permute-start.5 = (bf16[512,512]{1,0:T(8,128)(2,1)}, bf16[512,512]{1,0:T(8,128)(2,1)S(1)}, u32[]{:S(2)}, u32[]{:S(2)}) collective-permute-start(bf16[512,512]{1,0:T(8,128)(2,1)} %get-tuple-element.5), channel_id=1, source_target_pairs={{1,0},{2,1},{3,2},{0,3},{5,4},{6,5},{7,6},{4,7},{9,8},{10,9},{11,1... | collective-permute-start | bytes 1572872 | tf_op jit(solution)/shard_map/ppermute | solution.py:18
  9.8 0.5 collective-permute-start.3
  10.4 1.4 %collective-permute-start.4 = (bf16[512,512]{1,0:T(8,128)(2,1)}, bf16[512,512]{1,0:T(8,128)(2,1)S(1)}, u32[]{:S(2)}, u32[]{:S(2)}) collective-permute-start(bf16[512,512]{1,0:T(8,128)(2,1)} %get-tuple-element.8), channel_id=1, source_target_pairs={{1,0},{2,1},{3,2},{0,3},{5,4},{6,5},{7,6},{4,7},{9,8},{10,9},{11,1... | collective-permute-start | bytes 1572872 | tf_op jit(solution)/shard_map/ppermute | solution.py:18
  11.8 0.0 copy-done.2
  11.8 0.1 copy.8
  11.9 0.0 copy-done.3
  11.9 0.1 fusion.marked
  12.0 0.5 collective-permute-start
  12.5 29.2 %collective-permute-done.marked = s32[32,8]{1,0:T(8,128)S(1)} collective-permute-done((s32[32,8]{1,0:T(8,128)S(1)}, s32[32,8]{1,0:T(8,128)S(1)}, u32[]{:S(2)}, u32[]{:S(2)}) %collective-permute-start) | collective-permute-done | bytes 1056 | tf_op jit(solution)/shard_map/ppermute | solution.py:18
  41.7 3.4 %collective-permute-start.1 = (bf16[512,512]{1,0:T(8,128)(2,1)}, bf16[512,512]{1,0:T(8,128)(2,1)S(1)}, u32[]{:S(2)}, u32[]{:S(2)}) collective-permute-start(bf16[512,512]{1,0:T(8,128)(2,1)} %get-tuple-element.7), channel_id=1, source_target_pairs={{1,0},{2,1},{3,2},{0,3},{5,4},{6,5},{7,6},{4,7},{9,8},{10,9},{11,1... | collective-permute-start | bytes 1572872 | tf_op jit(solution)/shard_map/ppermute | solution.py:18
  45.1 1.6 %copy-done = bf16[2048,512]{1,0:T(8,128)(2,1)S(1)} copy-done((bf16[2048,512]{1,0:T(8,128)(2,1)S(1)}, bf16[2048,512]{1,0:T(8,128)(2,1)}, u32[]{:S(2)}) %copy-start) | copy-done | bytes 2097176
  46.7 1.4 %copy-done.1 = bf16[1536,512]{1,0:T(8,128)(2,1)S(1)} copy-done((bf16[1536,512]{1,0:T(8,128)(2,1)S(1)}, bf16[1536,512]{1,0:T(8,128)(2,1)}, u32[]{:S(2)}) %copy-start.1) | copy-done | bytes 1572888
  48.1 7.7 %first_step.1.total_ref._ = f32[2048,512]{1,0:T(8,128)S(1)} custom-call(s32[32,8]{1,0:T(8,128)S(1)} %fusion.marked, bf16[2048,512]{1,0:T(8,128)(2,1)S(1)} %copy-done, bf16[1536,512]{1,0:T(8,128)(2,1)S(1)} %copy-done.1), custom_call_target="tpu_custom_call" | custom-call | flops 3221225472 | bytes 7864320 | tf_op jit(solution)/shard_map/first_step/pallas_call | solution.py:71
  55.8 0.0 collective-permute-done.5.strip_ref
  55.8 0.0 collective-permute-done.2.p_ref
  55.8 3.3 %second_step.4._ = bf16[2048,512]{1,0:T(8,128)(2,1)} custom-call(s32[32,8]{1,0:T(8,128)S(1)} %collective-permute-done.marked, bf16[512,512]{1,0:T(8,128)(2,1)S(1)} %collective-permute-done.5.strip_ref, bf16[1536,512]{1,0:T(8,128)(2,1)S(1)} %collective-permute-done.2.p_ref, f32[2048,512]{1,0:T(8,128)S(1)} %first_step.1.total_ref._, ...), custom_call_target="tpu_custom_call" | custom-call | flops 805306368 | bytes 3670016 | tf_op jit(solution)/shard_map/second_step/pallas_call | solution.py:98
  59.1 0.0 collective-permute-done.4.strip_ref
  59.1 3.3 %second_step.5._ = bf16[2048,512]{1,0:T(8,128)(2,1)} custom-call(s32[32,8]{1,0:T(8,128)S(1)} %collective-permute-done.marked, bf16[512,512]{1,0:T(8,128)(2,1)S(1)} %collective-permute-done.4.strip_ref, bf16[1536,512]{1,0:T(8,128)(2,1)S(1)} %collective-permute-done.2.p_ref, f32[2048,512]{1,0:T(8,128)S(1)} %first_step.1.total_ref._, ...), custom_call_target="tpu_custom_call", output_to_operand_aliasing={{}: (4, {})} | custom-call | flops 805306368 | bytes 3670016 | tf_op jit(solution)/shard_map/second_step/pallas_call | solution.py:98
  62.4 0.0 collective-permute-done.3.strip_ref
  62.4 3.3 %second_step.6._ = bf16[2048,512]{1,0:T(8,128)(2,1)} custom-call(s32[32,8]{1,0:T(8,128)S(1)} %collective-permute-done.marked, bf16[512,512]{1,0:T(8,128)(2,1)S(1)} %collective-permute-done.3.strip_ref, bf16[1536,512]{1,0:T(8,128)(2,1)S(1)} %collective-permute-done.2.p_ref, f32[2048,512]{1,0:T(8,128)S(1)} %first_step.1.total_ref._, ...), custom_call_target="tpu_custom_call", output_to_operand_aliasing={{}: (4, {})} | custom-call | flops 805306368 | bytes 3670016 | tf_op jit(solution)/shard_map/second_step/pallas_call | solution.py:98
  65.7 0.0 collective-permute-done.1.strip_ref
  65.7 3.3 %second_step.7 = bf16[2048,512]{1,0:T(8,128)(2,1)} custom-call(s32[32,8]{1,0:T(8,128)S(1)} %collective-permute-done.marked, bf16[512,512]{1,0:T(8,128)(2,1)S(1)} %collective-permute-done.1.strip_ref, bf16[1536,512]{1,0:T(8,128)(2,1)S(1)} %collective-permute-done.2.p_ref, f32[2048,512]{1,0:T(8,128)S(1)} %first_step.1.total_ref._, ...), custom_call_target="tpu_custom_call", output_to_operand_aliasing={{}: (4, {})} | custom-call | flops 805306368 | bytes 3670016 | tf_op jit(solution)/shard_map/second_step/pallas_call | solution.py:98
  (4 shorter events, 0.0 us)
Async XLA Ops:
  0.0 11.8 %copy-start.2 = (s32[32,8]{0,1:T(8,128)S(1)}, s32[32,8]{0,1:T(8,128)}, u32[]{:S(2)}) copy-start(s32[32,8]{0,1:T(8,128)} %param.5) | copy-start | bytes 3076
  0.0 11.9 %copy-start.3 = (s32[32,1]{0,1:T(1,128)S(1)}, s32[32,1]{0,1:T(1,128)}, u32[]{:S(2)}) copy-start(s32[32,1]{0,1:T(1,128)} %param.6) | copy-start | bytes 388
  0.0 55.8 %collective-permute-start.2 = (bf16[1536,512]{1,0:T(8,128)(2,1)}, bf16[1536,512]{1,0:T(8,128)(2,1)S(1)}, u32[]{:S(2)}, u32[]{:S(2)}) collective-permute-start(bf16[1536,512]{1,0:T(8,128)(2,1)} %p_ref.1), channel_id=1, source_target_pairs={{4,0},{8,4},{12,8},{16,12},{20,16},{24,20},{28,24},{0,28},{5,1},{9... | collective-permute-start | bytes 4718600 | tf_op jit(solution)/shard_map/ppermute | solution.py:18
  7.4 48.4 %collective-permute-start.5 = (bf16[512,512]{1,0:T(8,128)(2,1)}, bf16[512,512]{1,0:T(8,128)(2,1)S(1)}, u32[]{:S(2)}, u32[]{:S(2)}) collective-permute-start(bf16[512,512]{1,0:T(8,128)(2,1)} %get-tuple-element.5), channel_id=1, source_target_pairs={{1,0},{2,1},{3,2},{0,3},{5,4},{6,5},{7,6},{4,7},{9,8},{10,9},{11,1... | collective-permute-start | bytes 1572872 | tf_op jit(solution)/shard_map/ppermute | solution.py:18
  9.8 52.6 %collective-permute-start.3 = (bf16[512,512]{1,0:T(8,128)(2,1)}, bf16[512,512]{1,0:T(8,128)(2,1)S(1)}, u32[]{:S(2)}, u32[]{:S(2)}) collective-permute-start(bf16[512,512]{1,0:T(8,128)(2,1)} %get-tuple-element.6), channel_id=1, source_target_pairs={{1,0},{2,1},{3,2},{0,3},{5,4},{6,5},{7,6},{4,7},{9,8},{10,9},{11,1... | collective-permute-start | bytes 1572872 | tf_op jit(solution)/shard_map/ppermute | solution.py:18
  10.4 48.7 %collective-permute-start.4 = (bf16[512,512]{1,0:T(8,128)(2,1)}, bf16[512,512]{1,0:T(8,128)(2,1)S(1)}, u32[]{:S(2)}, u32[]{:S(2)}) collective-permute-start(bf16[512,512]{1,0:T(8,128)(2,1)} %get-tuple-element.8), channel_id=1, source_target_pairs={{1,0},{2,1},{3,2},{0,3},{5,4},{6,5},{7,6},{4,7},{9,8},{10,9},{11,1... | collective-permute-start | bytes 1572872 | tf_op jit(solution)/shard_map/ppermute | solution.py:18
  12.0 29.7 %collective-permute-start = (s32[32,8]{1,0:T(8,128)S(1)}, s32[32,8]{1,0:T(8,128)S(1)}, u32[]{:S(2)}, u32[]{:S(2)}) collective-permute-start(s32[32,8]{1,0:T(8,128)S(1)} %fusion.marked), channel_id=1, source_target_pairs={{1,0},{2,1},{3,2},{0,3},{5,4},{6,5},{7,6},{4,7},{9,8},{10,9},{11,1... | collective-permute-start | bytes 3080 | tf_op jit(solution)/shard_map/ppermute | solution.py:18
  41.7 24.0 %collective-permute-start.1 = (bf16[512,512]{1,0:T(8,128)(2,1)}, bf16[512,512]{1,0:T(8,128)(2,1)S(1)}, u32[]{:S(2)}, u32[]{:S(2)}) collective-permute-start(bf16[512,512]{1,0:T(8,128)(2,1)} %get-tuple-element.7), channel_id=1, source_target_pairs={{1,0},{2,1},{3,2},{0,3},{5,4},{6,5},{7,6},{4,7},{9,8},{10,9},{11,1... | collective-permute-start | bytes 1572872 | tf_op jit(solution)/shard_map/ppermute | solution.py:18
  45.1 1.6 %copy-start = (bf16[2048,512]{1,0:T(8,128)(2,1)S(1)}, bf16[2048,512]{1,0:T(8,128)(2,1)}, u32[]{:S(2)}) copy-start(bf16[2048,512]{1,0:T(8,128)(2,1)} %strip_ref.1) | copy-start | bytes 6291460
  46.7 1.4 %copy-start.1 = (bf16[1536,512]{1,0:T(8,128)(2,1)S(1)}, bf16[1536,512]{1,0:T(8,128)(2,1)}, u32[]{:S(2)}) copy-start(bf16[1536,512]{1,0:T(8,128)(2,1)} %p_ref.1) | copy-start | bytes 4718596

commit v2 on v1

v2 whole, which is shorter than its diff:
```python
import functools

import jax
import jax.numpy as jnp
from jax import lax
from jax.experimental import pallas as pl
from jax.experimental.pallas import tpu as pltpu
from jax.sharding import PartitionSpec as P

GROUP = 4
CHUNKS = 4


def shifted(block, axis, distance):
    devices = range(lax.axis_size(axis))
    route = [((i - distance) % len(devices), i) for i in devices]
    return lax.ppermute(block, axis, route)


def row_product(marked, row, left, p_ref, edge, slots):
    picked = [
        p_ref[pl.ds(pl.multiple_of(marked[row, s] * edge, edge), edge), :] for s in range(slots)
    ]
    return jnp.dot(left, jnp.concatenate(picked, axis=0), preferred_element_type=jnp.float32)


def first_kernel(edge, slots, marked, strip_ref, p_ref, total_ref):
    row = pl.program_id(0) * GROUP
    for r in range(GROUP):
        here = pl.ds(r * edge, edge)
        total_ref[here, :] = row_product(marked, row + r, strip_ref[here, :], p_ref, edge, slots)


def second_kernel(edge, slots, start, marked, strip_ref, p_ref, total_ref, _, out_ref):
    row = start + pl.program_id(0) * GROUP
    for r in range(GROUP):
        here = pl.ds(r * edge, edge)
        product = row_product(marked, row + r, strip_ref[here, :], p_ref, edge, slots)
        out_ref[here, :] = (total_ref[here, :] + product).astype(out_ref.dtype)


def cost(rows, depth, width, extra):
    return pl.CostEstimate(
        flops=2 * rows * depth * width, bytes_accessed=2 * (rows * width + depth * width) + extra, transcendentals=0
    )


def first_product(marked, strips, p_tile):
    nrows, slots = marked.shape
    edge = strips.shape[0] // nrows
    depth, width = p_tile.shape
    tall = GROUP * edge
    return pl.pallas_call(
        functools.partial(first_kernel, edge, slots),
        grid_spec=pltpu.PrefetchScalarGridSpec(
            num_scalar_prefetch=1,
            grid=(nrows // GROUP,),
            in_specs=[
                pl.BlockSpec((tall, strips.shape[1]), lambda g, m: (g, 0)),
                pl.BlockSpec((depth, width), lambda g, m: (0, 0)),
            ],
            out_specs=pl.BlockSpec((tall, width), lambda g, m: (g, 0)),
        ),
        out_shape=jax.ShapeDtypeStruct((nrows * edge, width), jnp.float32),
        cost_estimate=cost(nrows * edge, slots * edge, width, 4 * nrows * edge * width),
        compiler_params=pltpu.CompilerParams(vmem_limit_bytes=24 << 20),
        name="first_step",
    )(marked, strips, p_tile)


def second_product(start, marked, part, p_tile, total, out):
    nrows, slots = marked.shape
    edge = total.shape[0] // nrows
    depth, width = p_tile.shape
    tall = GROUP * edge
    offset = start // GROUP
    out_shape = jax.ShapeDtypeStruct((nrows * edge, width), jnp.bfloat16)
    operands = (marked, part, p_tile, total, total if out is None else out)
    return pl.pallas_call(
        functools.partial(second_kernel, edge, slots, start),
        grid_spec=pltpu.PrefetchScalarGridSpec(
            num_scalar_prefetch=1,
            grid=(part.shape[0] // tall,),
            in_specs=[
                pl.BlockSpec((tall, part.shape[1]), lambda g, m: (g, 0)),
                pl.BlockSpec((depth, width), lambda g, m: (0, 0)),
                pl.BlockSpec((tall, width), lambda g, m: (g + offset, 0)),
                pl.BlockSpec(memory_space=pl.ANY),
            ],
            out_specs=pl.BlockSpec((tall, width), lambda g, m: (g + offset, 0)),
        ),
        out_shape=out_shape,
        input_output_aliases={} if out is None else {4: 0},
        cost_estimate=cost(part.shape[0], slots * edge, width, 6 * part.shape[0] * width),
        compiler_params=pltpu.CompilerParams(vmem_limit_bytes=24 << 20),
        name="second_step",
    )(*operands)


def body(f_blocks, block_cols, block_counts, p_matrix):
    nrows, slots = block_cols.shape
    edge = f_blocks.shape[0] // nrows
    spare = p_matrix.shape[0] // edge
    live = lax.broadcasted_iota(jnp.int32, (nrows, slots), 1) < block_counts
    marked = jnp.where(live, block_cols, spare)
    p_first = jnp.concatenate([p_matrix, jnp.zeros((edge, p_matrix.shape[1]), p_matrix.dtype)], axis=0)
    marked_next = shifted(marked, "col", -1)
    f_blocks, p_first, marked_next = lax.optimization_barrier((f_blocks, p_first, marked_next))
    step = nrows // CHUNKS
    parts = []
    for c in range(CHUNKS):
        parts.append(shifted(f_blocks[c * step * edge : (c + 1) * step * edge], "col", -1))
    p_second = shifted(p_first, "row", -1)
    total = first_product(marked, f_blocks, p_first)
    out = None
    for c in range(CHUNKS):
        out = second_product(c * step, marked_next, parts[c], p_second, total, out)
    return out


def solution(mesh):
    return jax.shard_map(
        body,
        mesh=mesh,
        in_specs=(P("row", "col"), P("row", "col"), P("row", "col"), P("row", "col")),
        out_specs=P("row", "col"),
        check_vma=False,
    )
```

time: 69.2 us -> 58.6 us (0.85)
  Pallas kernels: 20.9 us -> 14.7 us
  local copies, waits for them, and re-layouts: 5.98 us -> 2.56 us
  starting transfers between devices: 12.8 us -> 11.7 us
    pallas_call x4, Pallas kernels: 13.2 us -> 10 us  [second_product(): pl.pallas_call(functools.partial(second_kernel, edge, slots, start), grid...]
    pallas_call x1, Pallas kernels: 7.72 us -> 4.66 us  [first_product(): pl.pallas_call(functools.partial(first_kernel, edge, slots), grid_spec=pl...]
    slice x1, local copies, waits for them, and re-layouts: 2.9 us -> 0.14 us  [body(): f_blocks[c * step * edge:(c + 1) * step * edge]]
    unnamed x9 -> x3, local copies, waits for them, and re-layouts: 3.08 us -> 0.91 us
    concatenate x0 -> x1, local copies, waits for them, and re-layouts: none -> 1.51 us  [body(): jnp.concatenate([p_matrix, jnp.zeros((edge, p_matrix.shape[1]), p_matrix....]
    ppermute x6, starting transfers between devices: 12.8 us -> 11.7 us  [shifted(): return lax.ppermute(block, axis, route)]
  transfers between devices with their start and end apart: 6 -> 6, of which waited for: 1 -> 5; matrix products, arithmetic and copies ran while one was open for 4% -> 3% of each run, Pallas kernels for 25% -> 21%
where the time goes in v2:
time: 58.6 us; the launch traced here: 58.4 us
  waiting for transfers between devices  28.7 us (49%)
  Pallas kernels  14.7 us (25%)
  starting transfers between devices  11.7 us (20%)
  local copies, waits for them, and re-layouts  2.56 us (4%)
  other arithmetic  0.73 us (1%)
    ppermute x6, waiting for transfers between devices, shifted(): return lax.ppermute(block, axis, route)  28.7 us
    ppermute x6, starting transfers between devices, shifted(): return lax.ppermute(block, axis, route)  11.7 us
    pallas_call x4, Pallas kernels, second_product(): pl.pallas_call(functools.partial(second_kernel, edge, slots, start), grid...  10 us
    pallas_call x1, Pallas kernels, first_product(): pl.pallas_call(functools.partial(first_kernel, edge, slots), grid_spec=pl...  4.66 us
    concatenate x1, local copies, waits for them, and re-layouts, body(): jnp.concatenate([p_matrix, jnp.zeros((edge, p_matrix.shape[1]), p_matrix....  1.51 us
  transfers between devices with their start and end apart: 6, of which 5 were waited for; matrix products, arithmetic and copies ran while one was open for 3% of the time, Pallas kernels for 21%

profile of v2, /device:TPU:0, one launch (start us, length us, event | category | flops | bytes accessed | tf_op | source)
XLA Modules:
  0.0 58.4 jit_solution(9634465568136412765)
XLA Ops:
  0.0 0.0 copy-start
  0.0 0.9 %copy.8 = s32[32,8]{1,0:T(8,128)S(1)} copy(s32[32,8]{0,1:T(8,128)} %param.5) | data formatting | bytes 2048 | tf_op args[1]
  0.9 0.7 %fusion.marked = s32[32,8]{1,0:T(8,128)S(1)} fusion(s32[32,8]{1,0:T(8,128)S(1)} %copy.8, s32[32]{0:T(128)} %bitcast.1), kind=kLoop, calls=%fused_computation.1 | loop fusion | flops 512 | bytes 2176 | tf_op jit(solution)/shard_map/jit(_where)/select_n | solution.py:105
  1.6 3.9 %collective-permute-start = (s32[32,8]{1,0:T(8,128)S(1)}, s32[32,8]{1,0:T(8,128)S(1)}, u32[]{:S(2)}, u32[]{:S(2)}) collective-permute-start(s32[32,8]{1,0:T(8,128)S(1)} %fusion.marked), channel_id=1, source_target_pairs={{1,0},{2,1},{3,2},{0,3},{5,4},{6,5},{7,6},{4,7},{9,8},{10,9},{11,1... | collective-permute-start | bytes 3080 | tf_op jit(solution)/shard_map/ppermute | solution.py:17
  5.5 1.5 %concatenate.3.p_ref = bf16[1600,512]{1,0:T(8,128)(2,1)S(1)} pad(bf16[1536,512]{1,0:T(8,128)(2,1)} %param.7, bf16[]{:T(256)} %constant.0.clone.1), padding=0_64x0_0 | pad | bytes 3211266 | tf_op jit(solution)/shard_map/concatenate | solution.py:106
  7.1 0.0 collective-permute-done.marked
  7.1 2.8 %collective-permute-start.2 = (bf16[1600,512]{1,0:T(8,128)(2,1)S(1)}, bf16[1600,512]{1,0:T(8,128)(2,1)S(1)}, u32[]{:S(2)}, u32[]{:S(2)}) collective-permute-start(bf16[1600,512]{1,0:T(8,128)(2,1)S(1)} %concatenate.3.p_ref), channel_id=1, source_target_pairs={{4,0},{8,4},{12,8},{16,12},{20,16},{24,20},{28,24},{0,28},{5,1},{9... | collective-permute-start | bytes 4915208 | tf_op jit(solution)/shard_map/ppermute | solution.py:17
  9.9 0.0 copy-done
  9.9 0.1 fusion.1
  10.0 2.2 %collective-permute-start.5 = (bf16[512,512]{1,0:T(8,128)(2,1)S(1)}, bf16[512,512]{1,0:T(8,128)(2,1)S(1)}, u32[]{:S(2)}, u32[]{:S(2)}) collective-permute-start(bf16[512,512]{1,0:T(8,128)(2,1)S(1)} %get-tuple-element.11), channel_id=1, source_target_pairs={{1,0},{2,1},{3,2},{0,3},{5,4},{6,5},{7,6},{4,7},{9,8},{10,9},{11,1... | collective-permute-start | bytes 1572872 | tf_op jit(solution)/shard_map/ppermute | solution.py:17
  12.3 0.1 collective-permute-start.4
  12.3 1.9 %collective-permute-start.3 = (bf16[512,512]{1,0:T(8,128)(2,1)S(1)}, bf16[512,512]{1,0:T(8,128)(2,1)S(1)}, u32[]{:S(2)}, u32[]{:S(2)}) collective-permute-start(bf16[512,512]{1,0:T(8,128)(2,1)S(1)} %get-tuple-element.13), channel_id=1, source_target_pairs={{1,0},{2,1},{3,2},{0,3},{5,4},{6,5},{7,6},{4,7},{9,8},{10,9},{11,1... | collective-permute-start | bytes 1572872 | tf_op jit(solution)/shard_map/ppermute | solution.py:17
  14.2 0.8 %collective-permute-start.1 = (bf16[512,512]{1,0:T(8,128)(2,1)S(1)}, bf16[512,512]{1,0:T(8,128)(2,1)S(1)}, u32[]{:S(2)}, u32[]{:S(2)}) collective-permute-start(bf16[512,512]{1,0:T(8,128)(2,1)S(1)} %get-tuple-element.14), channel_id=1, source_target_pairs={{1,0},{2,1},{3,2},{0,3},{5,4},{6,5},{7,6},{4,7},{9,8},{10,9},{11,1... | collective-permute-start | bytes 1572872 | tf_op jit(solution)/shard_map/ppermute | solution.py:17
  15.0 4.7 %first_step.1.total_ref._ = f32[2048,512]{1,0:T(8,128)S(1)} custom-call(s32[32,8]{1,0:T(8,128)S(1)} %fusion.marked, bf16[2048,512]{1,0:T(8,128)(2,1)S(1)} %copy-done, bf16[1600,512]{1,0:T(8,128)(2,1)S(1)} %concatenate.3.p_ref), custom_call_target="tpu_custom_call" | custom-call | flops 1073741824 | bytes 6815744 | tf_op jit(solution)/shard_map/first_step/pallas_call | solution.py:53
  19.7 5.2 %collective-permute-done.5.strip_ref = bf16[512,512]{1,0:T(8,128)(2,1)S(1)} collective-permute-done((bf16[512,512]{1,0:T(8,128)(2,1)S(1)}, bf16[512,512]{1,0:T(8,128)(2,1)S(1)}, u32[]{:S(2)}, u32[]{:S(2)}) %collective-permute-start.5) | collective-permute-done | bytes 524320 | tf_op jit(solution)/shard_map/ppermute | solution.py:17
  24.9 3.6 %collective-permute-done.2.p_ref = bf16[1600,512]{1,0:T(8,128)(2,1)S(1)} collective-permute-done((bf16[1600,512]{1,0:T(8,128)(2,1)S(1)}, bf16[1600,512]{1,0:T(8,128)(2,1)S(1)}, u32[]{:S(2)}, u32[]{:S(2)}) %collective-permute-start.2) | collective-permute-done | bytes 1638432 | tf_op jit(solution)/shard_map/ppermute | solution.py:17
  28.5 2.5 %second_step.4._ = bf16[2048,512]{1,0:T(8,128)(2,1)} custom-call(s32[32,8]{1,0:T(8,128)S(1)} %collective-permute-done.marked, bf16[512,512]{1,0:T(8,128)(2,1)S(1)} %collective-permute-done.5.strip_ref, bf16[1600,512]{1,0:T(8,128)(2,1)S(1)} %collective-permute-done.2.p_ref, f32[2048,512]{1,0:T(8,128)S(1)} %first_step.1.total_ref._, ...), custom_call_target="tpu_custom_call" | custom-call | flops 268435456 | bytes 2621440 | tf_op jit(solution)/shard_map/second_step/pallas_call | solution.py:79
  31.0 5.2 %collective-permute-done.4.strip_ref = bf16[512,512]{1,0:T(8,128)(2,1)S(1)} collective-permute-done((bf16[512,512]{1,0:T(8,128)(2,1)S(1)}, bf16[512,512]{1,0:T(8,128)(2,1)S(1)}, u32[]{:S(2)}, u32[]{:S(2)}) %collective-permute-start.4) | collective-permute-done | bytes 524320 | tf_op jit(solution)/shard_map/ppermute | solution.py:17
  36.2 2.5 %second_step.5._ = bf16[2048,512]{1,0:T(8,128)(2,1)} custom-call(s32[32,8]{1,0:T(8,128)S(1)} %collective-permute-done.marked, bf16[512,512]{1,0:T(8,128)(2,1)S(1)} %collective-permute-done.4.strip_ref, bf16[1600,512]{1,0:T(8,128)(2,1)S(1)} %collective-permute-done.2.p_ref, f32[2048,512]{1,0:T(8,128)S(1)} %first_step.1.total_ref._, ...), custom_call_target="tpu_custom_call", output_to_operand_aliasing={{}: (4, {})} | custom-call | flops 268435456 | bytes 2621440 | tf_op jit(solution)/shard_map/second_step/pallas_call | solution.py:79
  38.7 8.7 %collective-permute-done.3.strip_ref = bf16[512,512]{1,0:T(8,128)(2,1)S(1)} collective-permute-done((bf16[512,512]{1,0:T(8,128)(2,1)S(1)}, bf16[512,512]{1,0:T(8,128)(2,1)S(1)}, u32[]{:S(2)}, u32[]{:S(2)}) %collective-permute-start.3) | collective-permute-done | bytes 524320 | tf_op jit(solution)/shard_map/ppermute | solution.py:17
  47.4 2.5 %second_step.6._ = bf16[2048,512]{1,0:T(8,128)(2,1)} custom-call(s32[32,8]{1,0:T(8,128)S(1)} %collective-permute-done.marked, bf16[512,512]{1,0:T(8,128)(2,1)S(1)} %collective-permute-done.3.strip_ref, bf16[1600,512]{1,0:T(8,128)(2,1)S(1)} %collective-permute-done.2.p_ref, f32[2048,512]{1,0:T(8,128)S(1)} %first_step.1.total_ref._, ...), custom_call_target="tpu_custom_call", output_to_operand_aliasing={{}: (4, {})} | custom-call | flops 268435456 | bytes 2621440 | tf_op jit(solution)/shard_map/second_step/pallas_call | solution.py:79
  49.9 6.0 %collective-permute-done.1.strip_ref = bf16[512,512]{1,0:T(8,128)(2,1)S(1)} collective-permute-done((bf16[512,512]{1,0:T(8,128)(2,1)S(1)}, bf16[512,512]{1,0:T(8,128)(2,1)S(1)}, u32[]{:S(2)}, u32[]{:S(2)}) %collective-permute-start.1) | collective-permute-done | bytes 524320 | tf_op jit(solution)/shard_map/ppermute | solution.py:17
  55.9 2.5 %second_step.7 = bf16[2048,512]{1,0:T(8,128)(2,1)} custom-call(s32[32,8]{1,0:T(8,128)S(1)} %collective-permute-done.marked, bf16[512,512]{1,0:T(8,128)(2,1)S(1)} %collective-permute-done.1.strip_ref, bf16[1600,512]{1,0:T(8,128)(2,1)S(1)} %collective-permute-done.2.p_ref, f32[2048,512]{1,0:T(8,128)S(1)} %first_step.1.total_ref._, ...), custom_call_target="tpu_custom_call", output_to_operand_aliasing={{}: (4, {})} | custom-call | flops 268435456 | bytes 2621440 | tf_op jit(solution)/shard_map/second_step/pallas_call | solution.py:79
Async XLA Ops:
  0.0 9.9 %copy-start = (bf16[2048,512]{1,0:T(8,128)(2,1)S(1)}, bf16[2048,512]{1,0:T(8,128)(2,1)}, u32[]{:S(2)}) copy-start(bf16[2048,512]{1,0:T(8,128)(2,1)} %strip_ref) | copy-start | bytes 6291460
  1.6 5.4 %collective-permute-start = (s32[32,8]{1,0:T(8,128)S(1)}, s32[32,8]{1,0:T(8,128)S(1)}, u32[]{:S(2)}, u32[]{:S(2)}) collective-permute-start(s32[32,8]{1,0:T(8,128)S(1)} %fusion.marked), channel_id=1, source_target_pairs={{1,0},{2,1},{3,2},{0,3},{5,4},{6,5},{7,6},{4,7},{9,8},{10,9},{11,1... | collective-permute-start | bytes 3080 | tf_op jit(solution)/shard_map/ppermute | solution.py:17
  7.1 21.5 %collective-permute-start.2 = (bf16[1600,512]{1,0:T(8,128)(2,1)S(1)}, bf16[1600,512]{1,0:T(8,128)(2,1)S(1)}, u32[]{:S(2)}, u32[]{:S(2)}) collective-permute-start(bf16[1600,512]{1,0:T(8,128)(2,1)S(1)} %concatenate.3.p_ref), channel_id=1, source_target_pairs={{4,0},{8,4},{12,8},{16,12},{20,16},{24,20},{28,24},{0,28},{5,1},{9... | collective-permute-start | bytes 4915208 | tf_op jit(solution)/shard_map/ppermute | solution.py:17
  10.0 14.9 %collective-permute-start.5 = (bf16[512,512]{1,0:T(8,128)(2,1)S(1)}, bf16[512,512]{1,0:T(8,128)(2,1)S(1)}, u32[]{:S(2)}, u32[]{:S(2)}) collective-permute-start(bf16[512,512]{1,0:T(8,128)(2,1)S(1)} %get-tuple-element.11), channel_id=1, source_target_pairs={{1,0},{2,1},{3,2},{0,3},{5,4},{6,5},{7,6},{4,7},{9,8},{10,9},{11,1... | collective-permute-start | bytes 1572872 | tf_op jit(solution)/shard_map/ppermute | solution.py:17
  12.3 23.9 %collective-permute-start.4 = (bf16[512,512]{1,0:T(8,128)(2,1)S(1)}, bf16[512,512]{1,0:T(8,128)(2,1)S(1)}, u32[]{:S(2)}, u32[]{:S(2)}) collective-permute-start(bf16[512,512]{1,0:T(8,128)(2,1)S(1)} %get-tuple-element.12), channel_id=1, source_target_pairs={{1,0},{2,1},{3,2},{0,3},{5,4},{6,5},{7,6},{4,7},{9,8},{10,9},{11,1... | collective-permute-start | bytes 1572872 | tf_op jit(solution)/shard_map/ppermute | solution.py:17
  12.3 35.1 %collective-permute-start.3 = (bf16[512,512]{1,0:T(8,128)(2,1)S(1)}, bf16[512,512]{1,0:T(8,128)(2,1)S(1)}, u32[]{:S(2)}, u32[]{:S(2)}) collective-permute-start(bf16[512,512]{1,0:T(8,128)(2,1)S(1)} %get-tuple-element.13), channel_id=1, source_target_pairs={{1,0},{2,1},{3,2},{0,3},{5,4},{6,5},{7,6},{4,7},{9,8},{10,9},{11,1... | collective-permute-start | bytes 1572872 | tf_op jit(solution)/shard_map/ppermute | solution.py:17
  14.2 41.7 %collective-permute-start.1 = (bf16[512,512]{1,0:T(8,128)(2,1)S(1)}, bf16[512,512]{1,0:T(8,128)(2,1)S(1)}, u32[]{:S(2)}, u32[]{:S(2)}) collective-permute-start(bf16[512,512]{1,0:T(8,128)(2,1)S(1)} %get-tuple-element.14), channel_id=1, source_target_pairs={{1,0},{2,1},{3,2},{0,3},{5,4},{6,5},{7,6},{4,7},{9,8},{10,9},{11,1... | collective-permute-start | bytes 1572872 | tf_op jit(solution)/shard_map/ppermute | solution.py:17

commit v3 on v0

v3 whole, which is shorter than its diff:
```python
import functools

import jax
import jax.numpy as jnp
from jax import lax
from jax.experimental import pallas as pl
from jax.experimental.pallas import tpu as pltpu
from jax.sharding import PartitionSpec as P

GROUP = 4
PAIR = 2


def shifted(block, axis, distance):
    devices = range(lax.axis_size(axis))
    route = [((i - distance) % len(devices), i) for i in devices]
    return lax.ppermute(block, axis, route)


def params(mib):
    return pltpu.CompilerParams(vmem_limit_bytes=mib << 20)


def cost(flops, moved):
    return pl.CostEstimate(flops=flops, bytes_accessed=moved, transcendentals=0)


def picked_rows(table, row, p_ref, edge, slots):
    blocks = [p_ref[pl.ds(pl.multiple_of(table[row, s] * edge, edge), edge), :] for s in range(slots)]
    return jnp.concatenate(blocks, axis=0)


def pack_kernel(edge, nrows, slots, table, f_ref, out_ref):
    wide = PAIR * edge
    for r in range(nrows):
        for p in range(slots // PAIR):
            to = pl.multiple_of((table[r, slots] + p) * edge, edge)
            out_ref[pl.ds(to, edge), :] = f_ref[pl.ds(r * edge, edge), pl.ds(p * wide, wide)]


def packed_pieces(table, f_blocks, nrows, slots):
    edge = f_blocks.shape[0] // nrows
    pieces = nrows * slots // PAIR
    shape = (pieces * edge, PAIR * edge)
    return pl.pallas_call(
        functools.partial(pack_kernel, edge, nrows, slots),
        grid_spec=pltpu.PrefetchScalarGridSpec(
            num_scalar_prefetch=1,
            grid=(1,),
            in_specs=[pl.BlockSpec(f_blocks.shape, lambda g, t: (0, 0))],
            out_specs=pl.BlockSpec(shape, lambda g, t: (0, 0)),
        ),
        out_shape=jax.ShapeDtypeStruct(shape, f_blocks.dtype),
        cost_estimate=cost(0, 4 * f_blocks.size),
        compiler_params=params(24),
        name="pack_live_pieces",
    )(table, f_blocks)


def first_kernel(edge, slots, table, strip_ref, p_ref, total_ref):
    row = pl.program_id(0) * GROUP
    for r in range(GROUP):
        here = pl.ds(r * edge, edge)
        picked = picked_rows(table, row + r, p_ref, edge, slots)
        total_ref[here, :] = jnp.dot(strip_ref[here, :], picked, preferred_element_type=jnp.float32)


def first_product(table, slots, strips, p_tile):
    nrows = table.shape[0]
    edge = strips.shape[0] // nrows
    depth, width = p_tile.shape
    tall = GROUP * edge
    return pl.pallas_call(
        functools.partial(first_kernel, edge, slots),
        grid_spec=pltpu.PrefetchScalarGridSpec(
            num_scalar_prefetch=1,
            grid=(nrows // GROUP,),
            in_specs=[
                pl.BlockSpec((tall, strips.shape[1]), lambda g, t: (g, 0)),
                pl.BlockSpec((depth, width), lambda g, t: (0, 0)),
            ],
            out_specs=pl.BlockSpec((tall, width), lambda g, t: (g, 0)),
        ),
        out_shape=jax.ShapeDtypeStruct((nrows * edge, width), jnp.float32),
        cost_estimate=cost(2 * strips.size * width, 8 * nrows * edge * width),
        compiler_params=params(24),
        name="first_step",
    )(table, strips, p_tile)


def add_group(table, slots, edge, group, base, pieces_ref, p_ref, total_ref, out_ref):
    for r in range(GROUP):
        row = group * GROUP + r
        here = pl.ds(r * edge, edge)
        left = [
            pieces_ref[pl.ds(pl.multiple_of((table[row, slots + p] - base) * edge, edge), edge), :]
            for p in range(slots // PAIR)
        ]
        picked = picked_rows(table, row, p_ref, edge, slots)
        product = jnp.dot(jnp.concatenate(left, axis=1), picked, preferred_element_type=jnp.float32)
        out_ref[here, :] = (total_ref[here, :] + product).astype(out_ref.dtype)


def early_kernel(edge, slots, table, done, pieces_ref, p_ref, total_ref, out_ref):
    group = pl.program_id(0)

    @pl.when(group < done[0])
    def _():
        add_group(table, slots, edge, group, 0, pieces_ref, p_ref, total_ref, out_ref)


def late_kernel(edge, slots, early, reach, table, done, early_ref, late_ref, p_ref, total_ref, _, out_ref, held, sems):
    group = pl.program_id(0)
    first = jnp.minimum(done[0], pl.num_programs(0) - 1)
    base = jnp.minimum(early - reach, table[first * GROUP, slots])

    @pl.when(group == 0)
    def _():
        start = pl.multiple_of(base * edge, edge)
        ahead = pltpu.make_async_copy(early_ref.at[pl.ds(start, reach * edge)], held.at[pl.ds(0, reach * edge)], sems.at[0])
        rest = pltpu.make_async_copy(late_ref, held.at[pl.ds(reach * edge, late_ref.shape[0])], sems.at[1])
        ahead.start()
        rest.start()
        ahead.wait()
        rest.wait()

    @pl.when(group >= first)
    def _():
        add_group(table, slots, edge, group, base, held, p_ref, total_ref, out_ref)


def early_product(table, slots, done, pieces, p_tile, total):
    nrows = table.shape[0]
    edge = total.shape[0] // nrows
    depth, width = p_tile.shape
    tall = GROUP * edge

    def block(g, t, done):
        return (jnp.minimum(g, jnp.maximum(done[0] - 1, 0)), 0)

    return pl.pallas_call(
        functools.partial(early_kernel, edge, slots),
        grid_spec=pltpu.PrefetchScalarGridSpec(
            num_scalar_prefetch=2,
            grid=(nrows // GROUP,),
            in_specs=[
                pl.BlockSpec(pieces.shape, lambda g, t, d: (0, 0)),
                pl.BlockSpec((depth, width), lambda g, t, d: (0, 0)),
                pl.BlockSpec((tall, width), block),
            ],
            out_specs=pl.BlockSpec((tall, width), block),
        ),
        out_shape=jax.ShapeDtypeStruct(total.shape, jnp.bfloat16),
        cost_estimate=cost(2 * pieces.size * width, 6 * total.size),
        compiler_params=params(24),
        name="second_step_early",
    )(table, done, pieces, p_tile, total)


def late_product(table, slots, done, early, late, p_tile, total, out):
    nrows = table.shape[0]
    edge = total.shape[0] // nrows
    depth, width = p_tile.shape
    tall = GROUP * edge
    reach = GROUP * slots // PAIR
    last = nrows // GROUP - 1

    def block(g, t, done):
        return (jnp.maximum(g, jnp.minimum(done[0], last)), 0)

    return pl.pallas_call(
        functools.partial(late_kernel, edge, slots, early.shape[0] // edge, reach),
        grid_spec=pltpu.PrefetchScalarGridSpec(
            num_scalar_prefetch=2,
            grid=(nrows // GROUP,),
            in_specs=[
                pl.BlockSpec(memory_space=pl.ANY),
                pl.BlockSpec(memory_space=pl.ANY),
                pl.BlockSpec((depth, width), lambda g, t, d: (0, 0)),
                pl.BlockSpec((tall, width), block),
                pl.BlockSpec(memory_space=pl.ANY),
            ],
            out_specs=pl.BlockSpec((tall, width), block),
            scratch_shapes=[
                pltpu.VMEM((reach * edge + late.shape[0], late.shape[1]), late.dtype),
                pltpu.SemaphoreType.DMA((2,)),
            ],
        ),
        out_shape=jax.ShapeDtypeStruct(total.shape, jnp.bfloat16),
        input_output_aliases={6: 0},
        cost_estimate=cost(2 * late.size * width, 6 * total.size),
        compiler_params=params(24),
        name="second_step_late",
    )(table, done, early, late, p_tile, total, out)


def exchange(room, late_room, slots, table, packed, f_blocks, p_first):
    nrows = table.shape[0]
    edge = f_blocks.shape[0] // nrows
    early_room = room - late_room
    table_next = shifted(table, "col", -1)
    early = shifted(packed[: early_room * edge], "col", -1)
    p_second = shifted(p_first, "row", -1)
    late = shifted(packed[early_room * edge : room * edge], "col", -1)
    total = first_product(table, slots, f_blocks, p_first)
    ends = table_next[GROUP - 1 :: GROUP, -1]
    done = jnp.sum((ends <= early_room).astype(jnp.int32)).reshape(1)
    out = early_product(table_next, slots, done, early, p_second, total)
    return late_product(table_next, slots, done, early, late, p_second, total, out)


def body(f_blocks, block_cols, block_counts, p_matrix):
    nrows, slots = block_cols.shape
    edge = f_blocks.shape[0] // nrows
    spare = p_matrix.shape[0] // edge
    live = lax.broadcasted_iota(jnp.int32, (nrows, slots), 1) < block_counts
    marked = jnp.where(live, block_cols, spare)
    number = (block_counts + (PAIR - 1)) // PAIR
    before = lax.broadcasted_iota(jnp.int32, (nrows, nrows), 1) < lax.broadcasted_iota(jnp.int32, (nrows, nrows), 0)
    offset = jnp.sum(jnp.where(before, number.reshape(1, nrows), 0), axis=1, keepdims=True)
    which = lax.broadcasted_iota(jnp.int32, (nrows, slots // PAIR), 1)
    place = offset + jnp.where(which < number, which, 0)
    table = jnp.concatenate([marked, place, offset + number], axis=1)
    most = lax.pmax(jnp.sum(number), ("row", "col"))
    packed = packed_pieces(table, f_blocks, nrows, slots)
    p_first = jnp.concatenate([p_matrix, jnp.zeros((edge, p_matrix.shape[1]), p_matrix.dtype)], axis=0)
    pieces = nrows * slots // PAIR
    step = max(pieces // 16, 1)
    least = 3 * step * 2
    rooms = list(range(least, pieces + 1, step))
    late_room = 3 * step
    index = jnp.clip((most - least + step - 1) // step, 0, len(rooms) - 1)
    branches = [functools.partial(exchange, room, late_room, slots) for room in rooms]
    return lax.switch(index, branches, table, packed, f_blocks, p_first)


def solution(mesh):
    return jax.shard_map(
        body,
        mesh=mesh,
        in_specs=(P("row", "col"), P("row", "col"), P("row", "col"), P("row", "col")),
        out_specs=P("row", "col"),
        check_vma=False,
    )
```

time: 78.2 us -> 104 us (1.33)
  blocking collectives: 0 us -> 42.2 us
  matrix products: 22.9 us -> 0 us
  Pallas kernels: 0 us -> 19 us
  local copies, waits for them, and re-layouts: 23.4 us -> 7.79 us
  waiting for transfers between devices: 20.5 us -> 25.2 us
  starting transfers between devices: 7.19 us -> 5.34 us
  other arithmetic: 3.98 us -> 2.33 us
    pmax x0 -> x1, blocking collectives: none -> 42.2 us  [body(): most = lax.pmax(jnp.sum(number), ('row', 'col'))]
    dot_general x2 -> x0, matrix products: 22.9 us -> none  [listed_product(): jnp.einsum('rax,rxc->rac', left, picked, preferred_element_type=jnp.float32)]
    gather x2 -> x0, local copies, waits for them, and re-layouts: 19.5 us -> none  [listed_product(): picked = stacked[cols].reshape(nrows, slots * edge, p_tile.shape[1])]
    pallas_call x0 -> x4, Pallas kernels: none -> 19 us  [the longest x1 6.97 us: early_product(): pl.pallas_call(functools.partial(early_kernel, edge, slots), grid_spec=pl...]
    ppermute x3 -> x4, waiting for transfers between devices: 20.5 us -> 25.2 us  [shifted(): return lax.ppermute(block, axis, route)]
    cond x0 -> x4, local copies, waits for them, and re-layouts: none -> 4.16 us
    broadcast_in_dim x6 -> x1, local copies, waits for them, and re-layouts: 3.78 us -> 0.09 us  [body(): jnp.sum(jnp.where(before, number.reshape(1, nrows), 0), axis=1, keepdims=...]
    slice x0 -> x3, local copies, waits for them, and re-layouts: none -> 1.94 us  [the longest x1 1.09 us: exchange(): early = shifted(packed[:early_room * edge], 'col', -1)]
  transfers between devices with their start and end apart: 3 -> 4, of which waited for: 1 -> 1; matrix products, arithmetic and copies ran while one was open for 40% -> 3% of each run, Pallas kernels for 0% -> 11%
where the time goes in v3:
time: 104 us; the launch traced here: 103 us
  blocking collectives  42.2 us (41%)
  waiting for transfers between devices  25.2 us (24%)
  Pallas kernels  19 us (18%)
  local copies, waits for them, and re-layouts  7.79 us (7%)
  starting transfers between devices  5.34 us (5%)
  other arithmetic  2.33 us (2%)
    pmax x1, blocking collectives, body(): most = lax.pmax(jnp.sum(number), ('row', 'col'))  42.2 us
    ppermute x4, waiting for transfers between devices, shifted(): return lax.ppermute(block, axis, route)  25.2 us
    pallas_call x1, Pallas kernels, early_product(): pl.pallas_call(functools.partial(early_kernel, edge, slots), grid_spec=pl...  6.97 us
    ppermute x4, starting transfers between devices, shifted(): return lax.ppermute(block, axis, route)  5.34 us
    pallas_call x1, Pallas kernels, first_product(): pl.pallas_call(functools.partial(first_kernel, edge, slots), grid_spec=pl...  4.66 us
    pallas_call x1, Pallas kernels, late_product(): pl.pallas_call(functools.partial(late_kernel, edge, slots, early.shape[0]...  4.27 us
    cond x4, local copies, waits for them, and re-layouts  4.16 us
    pallas_call x1, Pallas kernels, packed_pieces(): pl.pallas_call(functools.partial(pack_kernel, edge, nrows, slots), grid_s...  3.09 us
  transfers between devices with their start and end apart: 4, of which 1 were waited for; matrix products, arithmetic and copies ran while one was open for 3% of the time, Pallas kernels for 11%

profile of v3, /device:TPU:0, one launch (start us, length us, event | category | flops | bytes accessed | tf_op | source)
XLA Modules:
  0.0 103.2 jit_solution(217830430674824378)
XLA Ops:
  0.0 0.7 copy.44
  0.7 0.6 fusion.4
  1.4 42.2 %pmax.7 = s32[]{:T(128)} all-reduce(s32[]{:T(128)} %get-tuple-element.195), channel_id=1, replica_groups=mesh['row'=8,'col'=4] {'row','col'}, use_global_device_ids=true, to_apply=%region_1.2 | all-reduce | flops 1 | bytes 8 | tf_op jit(solution)/shard_map/pmax | solution.py:224
  44.3 0.1 select_reduce_fusion
  44.4 0.1 copy.46
  44.6 0.8 copy.45
  45.3 0.7 fusion.2
  46.1 3.1 %pack_live_pieces.1 = bf16[8192,128]{1,0:T(8,128)(2,1)S(1)} custom-call(s32[32,13]{1,0:T(8,128)S(1)} %pad_add_fusion.table, bf16[2048,512]{1,0:T(8,128)(2,1)} %f_ref.1), custom_call_target="tpu_custom_call" | custom-call | bytes 4194304 | tf_op jit(solution)/shard_map/pack_live_pieces/pallas_call | solution.py:45
  49.2 53.8 %conditional.1 = (bf16[2048,512]{1,0:T(8,128)(2,1)}) conditional(s32[]{:T(128)} %clamp.3, (s32[32,13]{1,0:T(8,128)S(1)}, bf16[8192,128]{1,0:T(8,128)(2,1)S(1)}, bf16[1536,512]{1,0:T(8,128)(2,1)S(1)}, bf16[2048,512]{1,0:T(8,128)(2,1)S(1)}, ()) %tuple.86, (s32[32,13]{1,0:T(8,128)S(1)}, bf16[8192,128]{1,0:T(8,128)(2,1)S(1)}, ...), branch_computations={%region_3.5_spmd, %region_5.7_spmd, %region_7.9_spmd, %region_9.11... | conditional | flops 2147483648 | bytes 76880712 | solution.py:234
  49.3 0.1 concatenate.14.p_ref
  49.4 1.1 %collective-permute-start.23 = (bf16[1600,512]{1,0:T(8,128)(2,1)S(1)}, bf16[1600,512]{1,0:T(8,128)(2,1)S(1)}, u32[]{:S(2)}, u32[]{:S(2)}) collective-permute-start(bf16[1600,512]{1,0:T(8,128)(2,1)S(1)} %concatenate.14.p_ref), channel_id=1, source_target_pairs={{4,0},{8,4},{12,8},{16,12},{20,16},{24,20},{28,24},{0,28},{5,1},{9... | collective-permute-start | bytes 4915208 | tf_op jit(solution)/shard_map/cond/branch_6_fun/ppermute | solution.py:17
  50.5 1.1 %slice.85 = bf16[4608,128]{1,0:T(8,128)(2,1)} slice(bf16[8192,128]{1,0:T(8,128)(2,1)S(1)} %get-tuple-element.130), slice={[0:4608], [0:128]} | slice | bytes 2359296 | tf_op jit(solution)/shard_map/cond/branch_6_fun/slice | solution.py:202
  51.6 2.3 %collective-permute-start.21 = (bf16[4608,128]{1,0:T(8,128)(2,1)}, bf16[4608,128]{1,0:T(8,128)(2,1)}, u32[]{:S(2)}, u32[]{:S(2)}) collective-permute-start(bf16[4608,128]{1,0:T(8,128)(2,1)} %slice.85), channel_id=1, source_target_pairs={{1,0},{2,1},{3,2},{0,3},{5,4},{6,5},{7,6},{4,7},{9,8},{10,9},{11,1... | collective-permute-start | bytes 3538952 | tf_op jit(solution)/shard_map/cond/branch_6_fun/ppermute | solution.py:17
  53.8 0.8 slice.86
  54.6 0.6 collective-permute-start.22
  55.3 1.3 %collective-permute-start.20 = (s32[32,13]{1,0:T(8,128)S(1)}, s32[32,13]{1,0:T(8,128)S(1)}, u32[]{:S(2)}, u32[]{:S(2)}) collective-permute-start(s32[32,13]{1,0:T(8,128)S(1)} %get-tuple-element.129.table), channel_id=1, source_target_pairs={{1,0},{2,1},{3,2},{0,3},{5,4},{6,5},{7,6},{4,7},{9,8},{10,9},{11,1... | collective-permute-start | bytes 5000 | tf_op jit(solution)/shard_map/cond/branch_6_fun/ppermute | solution.py:17
  56.6 4.7 %first_step.17.total_ref = f32[2048,512]{1,0:T(8,128)S(1)} custom-call(s32[32,13]{1,0:T(8,128)S(1)} %get-tuple-element.129.table, bf16[2048,512]{1,0:T(8,128)(2,1)S(1)} %get-tuple-element.132.strip_ref, bf16[1600,512]{1,0:T(8,128)(2,1)S(1)} %concatenate.14.p_ref), custom_call_target="tpu_custom_call" | custom-call | flops 1073741824 | bytes 8388608 | tf_op jit(solution)/shard_map/cond/branch_6_fun/first_step/pallas_call | solution.py:73
  61.3 2.0 %copy-done.2 = f32[2048,512]{1,0:T(8,128)} copy-done((f32[2048,512]{1,0:T(8,128)}, f32[2048,512]{1,0:T(8,128)S(1)}, u32[]{:S(2)}) %copy-start.2) | copy-done | bytes 4194328 | tf_op jit(solution)/shard_map/cond
  63.2 25.2 %collective-permute-done.20.table = s32[32,13]{1,0:T(8,128)S(1)} collective-permute-done((s32[32,13]{1,0:T(8,128)S(1)}, s32[32,13]{1,0:T(8,128)S(1)}, u32[]{:S(2)}, u32[]{:S(2)}) %collective-permute-start.20) | collective-permute-done | bytes 1696 | tf_op jit(solution)/shard_map/cond/branch_6_fun/ppermute | solution.py:17
  88.4 0.1 slice.84
  88.5 0.7 convert_reduce_fusion.6
  89.2 2.2 %copy-done.3 = f32[2048,512]{1,0:T(8,128)S(1)} copy-done((f32[2048,512]{1,0:T(8,128)S(1)}, f32[2048,512]{1,0:T(8,128)}, u32[]{:S(2)}) %copy-start.3) | copy-done | bytes 4194328 | tf_op jit(solution)/shard_map/cond
  91.4 7.0 %second_step_early.17._ = bf16[2048,512]{1,0:T(8,128)(2,1)} custom-call(s32[32,13]{1,0:T(8,128)S(1)} %collective-permute-done.20.table, s32[1]{0:T(128)} %bitcast.6.done, bf16[4608,128]{1,0:T(8,128)(2,1)} %collective-permute-done.21.pieces_ref.early_ref, bf16[1600,512]{1,0:T(8,128)(2,1)S(1)} %collective-permute-done.23.p_ref, f32[2048,512]{1,0:T(8,128)S(1)} %copy-done.3), custom_call_target="tpu_custom_call" | custom-call | flops 603979776 | bytes 6291456 | tf_op jit(solution)/shard_map/cond/branch_6_fun/second_step_early/pallas_call | solution.py:141
  98.4 4.3 %second_step_late.17 = bf16[2048,512]{1,0:T(8,128)(2,1)} custom-call(s32[32,13]{1,0:T(8,128)S(1)} %collective-permute-done.20.table, s32[1]{0:T(128)} %bitcast.6.done, bf16[4608,128]{1,0:T(8,128)(2,1)} %collective-permute-done.21.pieces_ref.early_ref, bf16[1536,128]{1,0:T(8,128)(2,1)} %collective-permute-done.22.late_ref, ...), custom_call_target="tpu_custom_call", output_to_operand_aliasing={{}: (6, {})} | custom-call | flops 201326592 | bytes 6291456 | tf_op jit(solution)/shard_map/cond/branch_6_fun/second_step_late/pallas_call | solution.py:171
  (12 shorter events, 0.2 us)
Async XLA Ops:
  46.1 3.1 %copy-start.22 = (bf16[2048,512]{1,0:T(8,128)(2,1)S(1)}, bf16[2048,512]{1,0:T(8,128)(2,1)}, u32[]{:S(2)}) copy-start(bf16[2048,512]{1,0:T(8,128)(2,1)} %f_ref.1) | copy-start | bytes 6291460
  46.1 3.1 %copy-start.23 = (bf16[1536,512]{1,0:T(8,128)(2,1)S(1)}, bf16[1536,512]{1,0:T(8,128)(2,1)}, u32[]{:S(2)}) copy-start(bf16[1536,512]{1,0:T(8,128)(2,1)} %param.18) | copy-start | bytes 4718596
  49.4 39.8 %collective-permute-start.23 = (bf16[1600,512]{1,0:T(8,128)(2,1)S(1)}, bf16[1600,512]{1,0:T(8,128)(2,1)S(1)}, u32[]{:S(2)}, u32[]{:S(2)}) collective-permute-start(bf16[1600,512]{1,0:T(8,128)(2,1)S(1)} %concatenate.14.p_ref), channel_id=1, source_target_pairs={{4,0},{8,4},{12,8},{16,12},{20,16},{24,20},{28,24},{0,28},{5,1},{9... | collective-permute-start | bytes 4915208 | tf_op jit(solution)/shard_map/cond/branch_6_fun/ppermute | solution.py:17
  51.6 37.6 %collective-permute-start.21 = (bf16[4608,128]{1,0:T(8,128)(2,1)}, bf16[4608,128]{1,0:T(8,128)(2,1)}, u32[]{:S(2)}, u32[]{:S(2)}) collective-permute-start(bf16[4608,128]{1,0:T(8,128)(2,1)} %slice.85), channel_id=1, source_target_pairs={{1,0},{2,1},{3,2},{0,3},{5,4},{6,5},{7,6},{4,7},{9,8},{10,9},{11,1... | collective-permute-start | bytes 3538952 | tf_op jit(solution)/shard_map/cond/branch_6_fun/ppermute | solution.py:17
  54.6 43.8 %collective-permute-start.22 = (bf16[1536,128]{1,0:T(8,128)(2,1)}, bf16[1536,128]{1,0:T(8,128)(2,1)}, u32[]{:S(2)}, u32[]{:S(2)}) collective-permute-start(bf16[1536,128]{1,0:T(8,128)(2,1)} %slice.86), channel_id=1, source_target_pairs={{1,0},{2,1},{3,2},{0,3},{5,4},{6,5},{7,6},{4,7},{9,8},{10,9},{11,1... | collective-permute-start | bytes 1179656 | tf_op jit(solution)/shard_map/cond/branch_6_fun/ppermute | solution.py:17
  55.3 33.2 %collective-permute-start.20 = (s32[32,13]{1,0:T(8,128)S(1)}, s32[32,13]{1,0:T(8,128)S(1)}, u32[]{:S(2)}, u32[]{:S(2)}) collective-permute-start(s32[32,13]{1,0:T(8,128)S(1)} %get-tuple-element.129.table), channel_id=1, source_target_pairs={{1,0},{2,1},{3,2},{0,3},{5,4},{6,5},{7,6},{4,7},{9,8},{10,9},{11,1... | collective-permute-start | bytes 5000 | tf_op jit(solution)/shard_map/cond/branch_6_fun/ppermute | solution.py:17
  61.3 2.0 %copy-start.2 = (f32[2048,512]{1,0:T(8,128)}, f32[2048,512]{1,0:T(8,128)S(1)}, u32[]{:S(2)}) copy-start(f32[2048,512]{1,0:T(8,128)S(1)} %first_step.17.total_ref) | copy-start | bytes 12582916 | tf_op jit(solution)/shard_map/cond
  89.2 2.2 %copy-start.3 = (f32[2048,512]{1,0:T(8,128)S(1)}, f32[2048,512]{1,0:T(8,128)}, u32[]{:S(2)}) copy-start(f32[2048,512]{1,0:T(8,128)} %copy-done.2) | copy-start | bytes 12582916 | tf_op jit(solution)/shard_map/cond

commit v4 on v0

v4 whole, which is shorter than its diff:
```python
import functools

import jax
import jax.numpy as jnp
from jax import lax
from jax.experimental import pallas as pl
from jax.experimental.pallas import tpu as pltpu
from jax.sharding import PartitionSpec as P

GROUP = 4
PAIR = 2

SMEM = pl.BlockSpec(memory_space=pltpu.SMEM)
ANY = pl.BlockSpec(memory_space=pl.ANY)
HBM = pl.BlockSpec(memory_space=pltpu.HBM)


def shifted(block, axis, distance):
    devices = range(lax.axis_size(axis))
    route = [((i - distance) % len(devices), i) for i in devices]
    return lax.ppermute(block, axis, route)


def in_hbm(x):
    return pltpu.with_memory_space_constraint(x, pltpu.HBM)


def params(mib):
    return pltpu.CompilerParams(vmem_limit_bytes=mib << 20)


def cost(flops, moved):
    return pl.CostEstimate(flops=flops, bytes_accessed=moved, transcendentals=0)


def piece(edge, index, count=1):
    return pl.ds(pl.multiple_of(index * edge, edge), count * edge)


def others_of(count):
    return (count + (PAIR - 1)) // PAIR - 1


def live_half(value, count, slot, edge):
    lane = lax.broadcasted_iota(jnp.int32, value.shape, 1)
    return jnp.where(lane < jnp.where(count > slot + 1, PAIR, 1) * edge, value, jnp.zeros_like(value))


def leading_kernel(edge, counts, f_ref, cols_ref, counts_ref, out_ref):
    slots, nrows = cols_ref.shape
    tall = f_ref.shape[0]
    for r in range(tall // edge):
        here = pl.ds(r * edge, edge)
        out_ref[here, :] = live_half(f_ref[here, :], counts[0, r], 0, edge)
    notes = jnp.concatenate([cols_ref[...], jnp.broadcast_to(counts_ref[...], (slots, nrows))], axis=0)
    out_ref[pl.ds(tall, 2 * slots), pl.ds(0, nrows)] = notes.astype(jnp.float32).astype(out_ref.dtype)


def leading_pieces(rows, f_blocks, cols, counts):
    slots, nrows = cols.shape
    edge = f_blocks.shape[0] // nrows
    shape = (rows * edge + 2 * slots, PAIR * edge)
    f_blocks, cols, counts = (in_hbm(x) for x in (f_blocks, cols, counts))
    return pl.pallas_call(
        functools.partial(leading_kernel, edge),
        grid_spec=pltpu.PrefetchScalarGridSpec(
            num_scalar_prefetch=1,
            grid=(1,),
            in_specs=[
                pl.BlockSpec((rows * edge, PAIR * edge), lambda g, c: (0, 0)),
                pl.BlockSpec(cols.shape, lambda g, c: (0, 0)),
                pl.BlockSpec(counts.shape, lambda g, c: (0, 0)),
            ],
            out_specs=pl.BlockSpec(shape, lambda g, c: (0, 0)),
        ),
        out_shape=jax.ShapeDtypeStruct(shape, f_blocks.dtype),
        cost_estimate=cost(0, 4 * rows * edge * PAIR * edge),
        compiler_params=params(8),
        name="leading_pieces",
    )(counts, f_blocks, cols, counts)


def pack_kernel(edge, slots, notes, f_ref, out_ref, extra_ref, f_here, packed, sems):
    nrows = notes.shape[1]
    parts = slots // PAIR
    fetched = []
    for g in range(nrows // GROUP):
        here = piece(edge, g * GROUP, GROUP)
        fetched.append(pltpu.make_async_copy(f_ref.at[here], f_here.at[here], sems.at[g]))
        fetched[-1].start()
    at = 0
    for r in range(nrows):
        if r % GROUP == 0:
            fetched[r // GROUP].wait()
        count = notes[slots, r]
        for p in range(parts):
            value = f_here[pl.ds(r * edge, edge), pl.ds(p * PAIR * edge, PAIR * edge)]
            to = r if p == 0 else nrows + at + (p - 1)
            packed[piece(edge, to), :] = live_half(value, count, p * PAIR, edge)
        at = at + others_of(count)
    packed[pl.ds(nrows * parts * edge, edge), :] = jnp.zeros((edge, PAIR * edge), packed.dtype)
    copies = [
        pltpu.make_async_copy(packed.at[pl.ds(nrows * edge, extra_ref.shape[0])], extra_ref, sems.at[0]),
        pltpu.make_async_copy(packed, out_ref, sems.at[1]),
    ]
    for copy in copies:
        copy.start()
    for copy in copies:
        copy.wait()


def packed_pieces(notes, slots, always, f_blocks):
    nrows = notes.shape[1]
    edge = f_blocks.shape[0] // nrows
    shape = ((nrows * slots // PAIR + 1) * edge, PAIR * edge)
    return pl.pallas_call(
        functools.partial(pack_kernel, edge, slots),
        in_specs=[SMEM, ANY],
        out_specs=[ANY, ANY],
        scratch_shapes=[
            pltpu.VMEM(f_blocks.shape, f_blocks.dtype),
            pltpu.VMEM(shape, f_blocks.dtype),
            pltpu.SemaphoreType.DMA((nrows // GROUP,)),
        ],
        out_shape=[
            jax.ShapeDtypeStruct(shape, f_blocks.dtype),
            jax.ShapeDtypeStruct((always * edge, PAIR * edge), f_blocks.dtype),
        ],
        cost_estimate=cost(0, 4 * f_blocks.size),
        compiler_params=params(16),
        name="pack_live_pieces",
    )(notes, f_blocks)


def cut_kernel(ranges, packed_ref, *refs):
    *out_refs, sems = refs
    copies = [
        pltpu.make_async_copy(packed_ref.at[pl.ds(low, high - low)], out_ref, sems.at[k])
        for k, ((low, high), out_ref) in enumerate(zip(ranges, out_refs))
    ]
    for copy in copies:
        copy.start()
    for copy in copies:
        copy.wait()


def cut_pieces(ranges, packed):
    edge = packed.shape[1] // PAIR
    rows = [(low * edge, high * edge) for low, high in ranges]
    return pl.pallas_call(
        functools.partial(cut_kernel, rows),
        in_specs=[ANY],
        out_specs=[ANY] * len(rows),
        scratch_shapes=[pltpu.SemaphoreType.DMA((len(rows),))],
        out_shape=[jax.ShapeDtypeStruct((high - low, packed.shape[1]), packed.dtype) for low, high in rows],
        cost_estimate=cost(0, 4 * sum(high - low for low, high in rows) * packed.shape[1]),
        compiler_params=params(2),
        name="cut_pieces",
    )(packed)


def row_product(notes, slots, edge, row, left, p_ref):
    picked = [p_ref[piece(edge, notes[s, row]), :] for s in range(slots)]
    return jnp.dot(
        jnp.concatenate(left, axis=1), jnp.concatenate(picked, axis=0), preferred_element_type=jnp.float32
    )


def left_pieces(notes, slots, edge, row, starts, held):
    nrows = notes.shape[1]
    spare = held.shape[0] // edge - 1
    live = others_of(notes[slots, row])
    left = [held[piece(edge, row), :]]
    for p in range(slots // PAIR - 1):
        left.append(held[piece(edge, jnp.where(p < live, nrows + starts[row] + p, spare)), :])
    return left


def step_kernel(edge, slots, name, leading, places, notes, *refs):
    size = None
    if name == "late":
        size, *refs = refs
    part_refs, refs = refs[: len(places)], refs[len(places) :]
    p_ref, *refs = refs
    total_ref = None
    if name != "first":
        total_ref, *refs = refs
    if name == "late":
        _, *refs = refs
    out_ref, starts, held, p_here, stage, sems, out_sems, *refs = refs
    nrows = notes.shape[1]
    groups = nrows // GROUP

    copies = [(None, pltpu.make_async_copy(p_ref, p_here, sems.at[0]))]
    for k, ((which, at, rows), part) in enumerate(zip(places, part_refs)):
        copy = pltpu.make_async_copy(part.at[pl.ds(0, rows * edge)], held.at[piece(edge, at, rows)], sems.at[k + 1])
        copies.append((None if which is None else size[0] == which, copy))

    def each(act):
        for needed, copy in copies:
            if needed is None:
                act(copy)
            else:
                pl.when(needed)(functools.partial(act, copy))

    each(lambda copy: copy.start())

    at = jnp.int32(0)
    for r in range(nrows):
        starts[r] = at
        at = at + others_of(notes[slots, r])
    starts[nrows] = at
    low, high = 0, groups
    if name != "first":
        room = places[-1][2] if name == "early" else places[2][2]
        done = jnp.int32(0)
        for g in range(leading // GROUP):
            done = done + (starts[(g + 1) * GROUP] <= room).astype(jnp.int32)
        low, high = (0, done) if name == "early" else (done, groups)

    def total_copy(g):
        here = piece(edge, g * GROUP, GROUP)
        return pltpu.make_async_copy(total_ref.at[here], refs[0].at[here], refs[1].at[g])

    def out_copy(g):
        here = piece(edge, g * GROUP, GROUP)
        return pltpu.make_async_copy(stage.at[here], out_ref.at[here], out_sems.at[g])

    def over(act):
        def step(g, carry):
            act(g)
            return carry

        lax.fori_loop(low, high, step, 0)

    if name != "first":
        over(lambda g: total_copy(g).start())
    if name != "first":
        held[pl.ds(held.shape[0] - edge, edge), :] = jnp.zeros((edge, held.shape[1]), held.dtype)
    each(lambda copy: copy.wait())

    def group(g):
        if name != "first":
            total_copy(g).wait()
        for r in range(GROUP):
            row = g * GROUP + r
            here = piece(edge, row)
            left = left_pieces(notes, slots, edge, row, starts, held)
            value = row_product(notes, slots, edge, row, left, p_here)
            if name != "first":
                value = refs[0][here, :] + value
            stage[here, :] = value.astype(stage.dtype)
        out_copy(g).start()

    over(group)
    over(lambda g: out_copy(g).wait())


def step_product(name, notes, slots, leading, places, parts, p_tile, total=None, size=None, out=None):
    nrows = notes.shape[1]
    depth, width = p_tile.shape
    edge = parts[0].shape[1] // PAIR
    groups = nrows // GROUP
    room = max(at + rows for _, at, rows in places)
    dtype = jnp.float32 if name == "first" else jnp.bfloat16
    tall = nrows * edge
    later = name != "first"
    late = name == "late"
    return pl.pallas_call(
        functools.partial(step_kernel, edge, slots, name, leading, places),
        in_specs=[SMEM] * (1 + late) + [ANY] * (len(parts) + 1 + later) + [HBM] * late,
        out_specs=HBM if later else ANY,
        scratch_shapes=[
            pltpu.SMEM((nrows + 1,), jnp.int32),
            pltpu.VMEM(((room + later) * edge, PAIR * edge), p_tile.dtype),
            pltpu.VMEM(p_tile.shape, p_tile.dtype),
            pltpu.VMEM((tall, width), dtype),
            pltpu.SemaphoreType.DMA((len(parts) + 1,)),
            pltpu.SemaphoreType.DMA((groups,)),
        ]
        + [pltpu.VMEM((tall, width), jnp.float32), pltpu.SemaphoreType.DMA((groups,))] * later,
        out_shape=(pltpu.HBM if later else jax.ShapeDtypeStruct)((tall, width), dtype),
        input_output_aliases={4 + len(parts): 0} if late else {},
        cost_estimate=cost(tall * width * slots * edge, 4 * tall * width),
        compiler_params=params(16),
        name="step_" + name,
    )(
        notes,
        *([size] if late else []),
        *parts,
        p_tile,
        *([total] if later else []),
        *([in_hbm(out)] if late else []),
    )


def remainder(k, slots, leading, places, rests, notes, lead, extra, p_second, total):
    rest = [shifted(part, "col", -1) if k == n else part for n, part in enumerate(rests)]
    return step_product("early", notes, slots, leading, places, (lead, extra), p_second, total), rest


def body(f_blocks, block_cols, block_counts, p_matrix):
    nrows, slots = block_cols.shape
    edge = f_blocks.shape[0] // nrows
    cols, counts = block_cols.T, block_counts.T
    groups = nrows // GROUP
    leading = (groups - groups * 3 // 8) * GROUP
    others = nrows * (slots // PAIR - 1)
    unit = others // 24
    always = 10 * unit
    ends = [always + k * unit for k in (2, 3, 4, 5, 6, 7, 9)] + [others]

    lead = shifted(leading_pieces(leading, f_blocks, cols, counts), "col", -1)
    p_second = shifted(p_matrix, "row", -1)
    notes = jnp.concatenate([cols, jnp.broadcast_to(counts, (slots, nrows))], axis=0)
    packed, extra = packed_pieces(notes, slots, always, f_blocks)
    extra = shifted(extra, "col", -1)
    later, *rests = cut_pieces([(leading, nrows)] + [(nrows + always, nrows + end) for end in ends], packed)
    every = packed.shape[0] // edge
    total = step_product("first", notes, slots, leading, [(None, 0, every)], (packed,), p_matrix)
    later, total = lax.optimization_barrier((later, total))
    later = shifted(later, "col", -1)

    notes_next = lead[leading * edge :, :nrows].astype(jnp.float32).astype(jnp.int32)
    most = jnp.maximum(jnp.sum(others_of(counts)), jnp.sum(others_of(notes_next[slots])))
    distance = 2
    while distance < lax.axis_size("col"):
        most = jnp.maximum(most, shifted(most, "col", -distance))
        distance *= 2
    size = sum((most > end).astype(jnp.int32) for end in ends[:-1])
    early = [(None, 0, leading), (None, nrows, always)]
    late = [early[0], (None, leading, nrows - leading), early[1]]
    late += [(k, nrows + always, end - always) for k, end in enumerate(ends)]
    branches = [functools.partial(remainder, k, slots, leading, early) for k in range(len(ends))]
    out, rest = lax.switch(size, branches, rests, notes_next, lead, extra, p_second, total)
    parts = (lead, later, extra, *rest)
    return step_product("late", notes_next, slots, leading, late, parts, p_second, total, size.reshape(1), out)


def solution(mesh):
    return jax.shard_map(
        body,
        mesh=mesh,
        in_specs=(P("row", "col"), P("row", "col"), P("row", "col"), P("row", "col")),
        out_specs=P("row", "col"),
        check_vma=False,
    )
```

time: 78.2 us -> 46.3 us (0.59)
  matrix products: 22.9 us -> 0 us
  Pallas kernels: 0 us -> 22.1 us
  local copies, waits for them, and re-layouts: 23.4 us -> 1.56 us
  waiting for transfers between devices: 20.5 us -> 3.99 us
  starting transfers between devices: 7.19 us -> 15.4 us
  other arithmetic: 3.98 us -> 1.37 us
  between operations: 0.07 us -> 2.12 us
    dot_general x2 -> x0, matrix products: 22.9 us -> none  [listed_product(): jnp.einsum('rax,rxc->rac', left, picked, preferred_element_type=jnp.float32)]
    pallas_call x0 -> x6, Pallas kernels: none -> 22.1 us  [the longest x3 16.3 us: step_product(): pl.pallas_call(functools.partial(step_kernel, edge, slots, name, leading,...]
    gather x2 -> x0, local copies, waits for them, and re-layouts: 19.5 us -> none  [listed_product(): picked = stacked[cols].reshape(nrows, slots * edge, p_tile.shape[1])]
    ppermute x3 -> x6, waiting for transfers between devices: 20.5 us -> 3.99 us  [shifted(): return lax.ppermute(block, axis, route)]
    ppermute x3 -> x6, starting transfers between devices: 7.19 us -> 15.4 us  [shifted(): return lax.ppermute(block, axis, route)]
    broadcast_in_dim x6 -> x1, local copies, waits for them, and re-layouts: 3.78 us -> 0.01 us  [body(): jnp.broadcast_to(counts, (slots, nrows))]
    select_n x3 -> x0, other arithmetic: 3.24 us -> none  [the longest x1 3.23 us: body(): jnp.where(live[:, None, :, None], viewed, jnp.zeros((), f_blocks.dtype))]
    reduce_sum x0 -> x2, other arithmetic: none -> 1.36 us  [the longest x1 0.72 us: body(): jnp.sum(others_of(notes_next[slots]))]
  transfers between devices with their start and end apart: 3 -> 6, of which waited for: 1 -> 3; matrix products, arithmetic and copies ran while one was open for 40% -> 5% of each run, Pallas kernels for 0% -> 37%
where the time goes in v4:
time: 46.3 us; the launch traced here: 46.5 us
  Pallas kernels  22.1 us (48%)
  starting transfers between devices  15.4 us (33%)
  waiting for transfers between devices  3.99 us (9%)
  between operations  2.12 us (5%)
  local copies, waits for them, and re-layouts  1.56 us (3%)
  other arithmetic  1.37 us (3%)
    pallas_call x3, Pallas kernels, step_product(): pl.pallas_call(functools.partial(step_kernel, edge, slots, name, leading,...  16.3 us
    ppermute x6, starting transfers between devices, shifted(): return lax.ppermute(block, axis, route)  15.4 us
    ppermute x6, waiting for transfers between devices, shifted(): return lax.ppermute(block, axis, route)  3.99 us
    pallas_call x1, Pallas kernels, cut_pieces(): pl.pallas_call(functools.partial(cut_kernel, rows), in_specs=[ANY], out_s...  2.13 us
    pallas_call x1, Pallas kernels, packed_pieces(): pl.pallas_call(functools.partial(pack_kernel, edge, slots), in_specs=[SME...  1.95 us
    pallas_call x1, Pallas kernels, leading_pieces(): pl.pallas_call(functools.partial(leading_kernel, edge), grid_spec=pltpu.P...  1.73 us
  transfers between devices with their start and end apart: 6, of which 3 were waited for; matrix products, arithmetic and copies ran while one was open for 5% of the time, Pallas kernels for 37%

profile of v4, /device:TPU:0, one launch (start us, length us, event | category | flops | bytes accessed | tf_op | source)
XLA Modules:
  0.0 46.5 jit_solution(15784278151768928162)
XLA Ops:
  0.0 4.5 %collective-permute-start.12 = (bf16[1536,512]{1,0:T(8,128)(2,1)}, bf16[1536,512]{1,0:T(8,128)(2,1)S(1)}, u32[]{:S(2)}, u32[]{:S(2)}) collective-permute-start(bf16[1536,512]{1,0:T(8,128)(2,1)} %refs_1_.1), channel_id=1, source_target_pairs={{4,0},{8,4},{12,8},{16,12},{20,16},{24,20},{28,24},{0,28},{5,1},{9... | collective-permute-start | bytes 4718600 | tf_op jit(solution)/shard_map/ppermute | solution.py:21
  4.6 1.7 %leading_pieces.1 = bf16[1296,128]{1,0:T(8,128)(2,1)S(1)} custom-call(s32[1,32]{1,0:T(1,128)} %bitcast.13, bf16[2048,512]{1,0:T(8,128)(2,1)} %f_ref.3, s32[8,32]{1,0:T(8,128)} %bitcast.11, s32[1,32]{1,0:T(1,128)} %bitcast.14), custom_call_target="tpu_custom_call" | custom-call | bytes 655360 | tf_op jit(solution)/shard_map/leading_pieces/pallas_call | solution.py:64
  6.3 2.5 %collective-permute-start.8 = (bf16[1296,128]{1,0:T(8,128)(2,1)S(1)}, bf16[1296,128]{1,0:T(8,128)(2,1)S(1)}, u32[]{:S(2)}, u32[]{:S(2)}) collective-permute-start(bf16[1296,128]{1,0:T(8,128)(2,1)S(1)} %leading_pieces.1), channel_id=1, source_target_pairs={{1,0},{2,1},{3,2},{0,3},{5,4},{6,5},{7,6},{4,7},{9,8},{10,9},{11,1... | collective-permute-start | bytes 995336 | tf_op jit(solution)/shard_map/ppermute | solution.py:21
  8.8 0.0 copy-start.1
  8.8 1.9 %pack_live_pieces.1 = (bf16[8256,128]{1,0:T(8,128)(2,1)S(1)}, bf16[2560,128]{1,0:T(8,128)(2,1)S(1)}) custom-call(s32[16,32]{1,0:T(8,128)S(1)} %pad_add_fusion.notes, bf16[2048,512]{1,0:T(8,128)(2,1)S(1)} %copy-done), custom_call_target="tpu_custom_call" | custom-call | bytes 4194304 | tf_op jit(solution)/shard_map/pack_live_pieces/pallas_call | solution.py:116
  10.8 0.6 %collective-permute-start.11 = (bf16[2560,128]{1,0:T(8,128)(2,1)S(1)}, bf16[2560,128]{1,0:T(8,128)(2,1)S(1)}, u32[]{:S(2)}, u32[]{:S(2)}) collective-permute-start(bf16[2560,128]{1,0:T(8,128)(2,1)S(1)} %get-tuple-element.342), channel_id=1, source_target_pairs={{1,0},{2,1},{3,2},{0,3},{5,4},{6,5},{7,6},{4,7},{9,8},{10,9},{11,1... | collective-permute-start | bytes 1966088 | tf_op jit(solution)/shard_map/ppermute | solution.py:21
  11.4 2.1 %cut_pieces.1 = (bf16[768,128]{1,0:T(8,128)(2,1)S(1)}, bf16[512,128]{1,0:T(8,128)(2,1)S(1)}, bf16[768,128]{1,0:T(8,128)(2,1)}, bf16[1024,128]{1,0:T(8,128)(2,1)}...) custom-call(bf16[8256,128]{1,0:T(8,128)(2,1)S(1)} %get-tuple-element, ...), custom_call_target="tpu_custom_call" | custom-call | bytes 6946816 | tf_op jit(solution)/shard_map/cut_pieces/pallas_call | solution.py:150
  13.5 5.8 %step_first.1.refs_13_ = f32[2048,512]{1,0:T(8,128)} custom-call(s32[16,32]{1,0:T(8,128)S(1)} %pad_add_fusion.notes, bf16[8256,128]{1,0:T(8,128)(2,1)S(1)} %get-tuple-element.339.packed_ref.refs_0_, bf16[1536,512]{1,0:T(8,128)(2,1)S(1)} %copy-done.1), custom_call_target="tpu_custom_call" | custom-call | flops 536870912 | bytes 4194304 | tf_op jit(solution)/shard_map/step_first/pallas_call | solution.py:269
  19.3 1.5 %collective-permute-start.10 = (bf16[768,128]{1,0:T(8,128)(2,1)S(1)}, bf16[768,128]{1,0:T(8,128)(2,1)S(1)}, u32[]{:S(2)}, u32[]{:S(2)}) collective-permute-start(bf16[768,128]{1,0:T(8,128)(2,1)S(1)} %get-tuple-element.341), channel_id=1, source_target_pairs={{1,0},{2,1},{3,2},{0,3},{5,4},{6,5},{7,6},{4,7},{9,8},{10,9},{11,1... | collective-permute-start | bytes 589832 | tf_op jit(solution)/shard_map/ppermute | solution.py:21
  20.8 0.6 %add_reduce_fusion.1 = s32[]{:T(128)} fusion(s32[32,1]{0,1:T(1,128)S(1)} %copy-done.4), kind=kLoop, calls=%fused_computation.13 | loop fusion | flops 575 | bytes 132 | tf_op jit(solution)/shard_map/reduce_sum | solution.py:325
  21.5 0.0 collective-permute-done.8.refs_1_
  21.5 0.7 %copy-done.2 = bf16[1296,128]{1,0:T(8,128)(2,1)} copy-done((bf16[1296,128]{1,0:T(8,128)(2,1)}, bf16[1296,128]{1,0:T(8,128)(2,1)S(1)}, u32[]{:S(2)}) %copy-start.2) | copy-done | bytes 331800
  22.2 0.7 %add_reduce_fusion = s32[]{:T(128)} fusion(s32[16,32]{1,0:T(8,128)S(1)} %convert_convert_fusion.notes), kind=kLoop, calls=%fused_computation.12 | loop fusion | flops 575 | bytes 132 | tf_op jit(solution)/shard_map/reduce_sum | solution.py:325
  24.3 2.9 %collective-permute-start.9 = (s32[]{:T(128)}, s32[]{:T(128)}, u32[]{:S(2)}, u32[]{:S(2)}) collective-permute-start(s32[]{:T(128)} %max.6), channel_id=1, source_target_pairs={{2,0},{3,1},{0,2},{1,3},{6,4},{7,5},{4,6},{5,7},{10,8},{11,9},{8,1... | collective-permute-start | bytes 20 | tf_op jit(solution)/shard_map/ppermute | solution.py:21
  27.2 0.7 %collective-permute-done.9 = s32[]{:T(128)} collective-permute-done((s32[]{:T(128)}, s32[]{:T(128)}, u32[]{:S(2)}, u32[]{:S(2)}) %collective-permute-start.9) | collective-permute-done | bytes 36 | tf_op jit(solution)/shard_map/ppermute | solution.py:21
  28.6 2.5 %collective-permute-done.11.refs_3_ = bf16[2560,128]{1,0:T(8,128)(2,1)S(1)} collective-permute-done((bf16[2560,128]{1,0:T(8,128)(2,1)S(1)}, bf16[2560,128]{1,0:T(8,128)(2,1)S(1)}, u32[]{:S(2)}, u32[]{:S(2)}) %collective-permute-start.11) | collective-permute-done | bytes 655392 | tf_op jit(solution)/shard_map/ppermute | solution.py:21
  31.1 0.0 collective-permute-done.12.refs_12_
  31.1 10.5 %conditional.1 = (bf16[2048,512]{1,0:T(8,128)(2,1)}, bf16[512,128]{1,0:T(8,128)(2,1)S(1)}, bf16[768,128]{1,0:T(8,128)(2,1)}, bf16[1024,128]{1,0:T(8,128)(2,1)}, ...) conditional(s32[]{:T(128)} %clamp.3, (s32[16,32]{1,0:T(8,128)S(1)}, ...), branch_computations={%region_2.3_spmd, %region_3.4_spmd, %region_4.5_spmd, %region_5.6_... | conditional | flops 536870912 | bytes 9961584 | solution.py:335
  31.1 3.4 %collective-permute-start.5 = (bf16[1792,128]{1,0:T(8,128)(2,1)}, bf16[1792,128]{1,0:T(8,128)(2,1)S(1)}, u32[]{:S(2)}, u32[]{:S(2)}) collective-permute-start(bf16[1792,128]{1,0:T(8,128)(2,1)} %get-tuple-element.288), channel_id=1, source_target_pairs={{1,0},{2,1},{3,2},{0,3},{5,4},{6,5},{7,6},{4,7},{9,8},{10,9},{11,1... | collective-permute-start | bytes 1376264 | tf_op jit(solution)/shard_map/cond/branch_5_fun/ppermute | solution.py:21
  34.5 5.5 %step_early.13 = bf16[2048,512]{1,0:T(8,128)(2,1)} custom-call(s32[16,32]{1,0:T(8,128)S(1)} %get-tuple-element.278.notes, bf16[1296,128]{1,0:T(8,128)(2,1)} %get-tuple-element.279.refs_0_, bf16[2560,128]{1,0:T(8,128)(2,1)S(1)} %get-tuple-element.280.refs_1_, bf16[1536,512]{1,0:T(8,128)(2,1)S(1)} %get-tuple-element.281.refs_2_, ...), custom_call_target="tpu_custom_call" | custom-call | flops 536870912 | bytes 4194304 | tf_op jit(solution)/shard_map/cond/branch_5_fun/step_early/pallas_call | solution.py:269
  40.0 0.8 %collective-permute-done.5 = bf16[1792,128]{1,0:T(8,128)(2,1)S(1)} collective-permute-done((bf16[1792,128]{1,0:T(8,128)(2,1)}, bf16[1792,128]{1,0:T(8,128)(2,1)S(1)}, u32[]{:S(2)}, u32[]{:S(2)}) %collective-permute-start.5) | collective-permute-done | bytes 458784 | tf_op jit(solution)/shard_map/cond/branch_5_fun/ppermute | solution.py:21
  40.8 0.8 %copy.57 = bf16[1792,128]{1,0:T(8,128)(2,1)} copy(bf16[1792,128]{1,0:T(8,128)(2,1)S(1)} %collective-permute-done.5) | data formatting | bytes 917504 | tf_op jit(solution)/shard_map/cond
  41.6 0.0 collective-permute-done.10.refs_2_
  41.6 4.9 %step_late.1 = bf16[2048,512]{1,0:T(8,128)(2,1)} custom-call(s32[16,32]{1,0:T(8,128)S(1)} %convert_convert_fusion.notes, s32[1]{0:T(128)} %bitcast.3.refs_0_, bf16[1296,128]{1,0:T(8,128)(2,1)} %copy-done.2, bf16[768,128]{1,0:T(8,128)(2,1)S(1)} %collective-permute-done.10.refs_2_, ...), custom_call_target="tpu_custom_call", output_to_operand_aliasing={{}: (15, {})} | custom-call | flops 536870912 | bytes 4194304 | tf_op jit(solution)/shard_map/step_late/pallas_call | solution.py:269
  (12 shorter events, 0.0 us)
Async XLA Ops:
  0.0 8.8 %copy-start = (bf16[2048,512]{1,0:T(8,128)(2,1)S(1)}, bf16[2048,512]{1,0:T(8,128)(2,1)}, u32[]{:S(2)}) copy-start(bf16[2048,512]{1,0:T(8,128)(2,1)} %f_ref.3) | copy-start | bytes 6291460
  0.0 8.8 %copy-start.4 = (s32[32,1]{0,1:T(1,128)S(1)}, s32[32,1]{0,1:T(1,128)}, u32[]{:S(2)}) copy-start(s32[32,1]{0,1:T(1,128)} %param.14) | copy-start | bytes 388
  0.0 8.8 %copy-start.3 = (s32[32,8]{0,1:T(8,128)S(1)}, s32[32,8]{0,1:T(8,128)}, u32[]{:S(2)}) copy-start(s32[32,8]{0,1:T(8,128)} %param.13) | copy-start | bytes 3076
  0.0 31.1 %collective-permute-start.12 = (bf16[1536,512]{1,0:T(8,128)(2,1)}, bf16[1536,512]{1,0:T(8,128)(2,1)S(1)}, u32[]{:S(2)}, u32[]{:S(2)}) collective-permute-start(bf16[1536,512]{1,0:T(8,128)(2,1)} %refs_1_.1), channel_id=1, source_target_pairs={{4,0},{8,4},{12,8},{16,12},{20,16},{24,20},{28,24},{0,28},{5,1},{9... | collective-permute-start | bytes 4718600 | tf_op jit(solution)/shard_map/ppermute | solution.py:21
  6.3 15.2 %collective-permute-start.8 = (bf16[1296,128]{1,0:T(8,128)(2,1)S(1)}, bf16[1296,128]{1,0:T(8,128)(2,1)S(1)}, u32[]{:S(2)}, u32[]{:S(2)}) collective-permute-start(bf16[1296,128]{1,0:T(8,128)(2,1)S(1)} %leading_pieces.1), channel_id=1, source_target_pairs={{1,0},{2,1},{3,2},{0,3},{5,4},{6,5},{7,6},{4,7},{9,8},{10,9},{11,1... | collective-permute-start | bytes 995336 | tf_op jit(solution)/shard_map/ppermute | solution.py:21
  8.8 4.7 %copy-start.1 = (bf16[1536,512]{1,0:T(8,128)(2,1)S(1)}, bf16[1536,512]{1,0:T(8,128)(2,1)}, u32[]{:S(2)}) copy-start(bf16[1536,512]{1,0:T(8,128)(2,1)} %refs_1_.1) | copy-start | bytes 4718596
  10.8 20.3 %collective-permute-start.11 = (bf16[2560,128]{1,0:T(8,128)(2,1)S(1)}, bf16[2560,128]{1,0:T(8,128)(2,1)S(1)}, u32[]{:S(2)}, u32[]{:S(2)}) collective-permute-start(bf16[2560,128]{1,0:T(8,128)(2,1)S(1)} %get-tuple-element.342), channel_id=1, source_target_pairs={{1,0},{2,1},{3,2},{0,3},{5,4},{6,5},{7,6},{4,7},{9,8},{10,9},{11,1... | collective-permute-start | bytes 1966088 | tf_op jit(solution)/shard_map/ppermute | solution.py:21
  19.3 22.2 %collective-permute-start.10 = (bf16[768,128]{1,0:T(8,128)(2,1)S(1)}, bf16[768,128]{1,0:T(8,128)(2,1)S(1)}, u32[]{:S(2)}, u32[]{:S(2)}) collective-permute-start(bf16[768,128]{1,0:T(8,128)(2,1)S(1)} %get-tuple-element.341), channel_id=1, source_target_pairs={{1,0},{2,1},{3,2},{0,3},{5,4},{6,5},{7,6},{4,7},{9,8},{10,9},{11,1... | collective-permute-start | bytes 589832 | tf_op jit(solution)/shard_map/ppermute | solution.py:21
  21.5 0.7 %copy-start.2 = (bf16[1296,128]{1,0:T(8,128)(2,1)}, bf16[1296,128]{1,0:T(8,128)(2,1)S(1)}, u32[]{:S(2)}) copy-start(bf16[1296,128]{1,0:T(8,128)(2,1)S(1)} %collective-permute-done.8.refs_1_) | copy-start | bytes 995332
  24.3 3.6 %collective-permute-start.9 = (s32[]{:T(128)}, s32[]{:T(128)}, u32[]{:S(2)}, u32[]{:S(2)}) collective-permute-start(s32[]{:T(128)} %max.6), channel_id=1, source_target_pairs={{2,0},{3,1},{0,2},{1,3},{6,4},{7,5},{4,6},{5,7},{10,8},{11,9},{8,1... | collective-permute-start | bytes 20 | tf_op jit(solution)/shard_map/ppermute | solution.py:21
  31.1 9.7 %collective-permute-start.5 = (bf16[1792,128]{1,0:T(8,128)(2,1)}, bf16[1792,128]{1,0:T(8,128)(2,1)S(1)}, u32[]{:S(2)}, u32[]{:S(2)}) collective-permute-start(bf16[1792,128]{1,0:T(8,128)(2,1)} %get-tuple-element.288), channel_id=1, source_target_pairs={{1,0},{2,1},{3,2},{0,3},{5,4},{6,5},{7,6},{4,7},{9,8},{10,9},{11,1... | collective-permute-start | bytes 1376264 | tf_op jit(solution)/shard_map/cond/branch_5_fun/ppermute | solution.py:21

commit v5 on v4

--- a/solution.py
+++ b/solution.py
@@ -133,7 +133,7 @@
 
 
 def cut_kernel(ranges, packed_ref, *refs):
-    *out_refs, sems = refs
+    out_refs, sems = refs[: len(ranges)], refs[-1]
     copies = [
         pltpu.make_async_copy(packed_ref.at[pl.ds(low, high - low)], out_ref, sems.at[k])
         for k, ((low, high), out_ref) in enumerate(zip(ranges, out_refs))
@@ -150,9 +150,9 @@
     return pl.pallas_call(
         functools.partial(cut_kernel, rows),
         in_specs=[ANY],
-        out_specs=[ANY] * len(rows),
+        out_specs=[ANY] * (2 * len(rows)),
         scratch_shapes=[pltpu.SemaphoreType.DMA((len(rows),))],
-        out_shape=[jax.ShapeDtypeStruct((high - low, packed.shape[1]), packed.dtype) for low, high in rows],
+        out_shape=[jax.ShapeDtypeStruct((high - low, packed.shape[1]), packed.dtype) for low, high in rows] * 2,
         cost_estimate=cost(0, 4 * sum(high - low for low, high in rows) * packed.shape[1]),
         compiler_params=params(2),
         name="cut_pieces",
@@ -191,19 +191,8 @@
     nrows = notes.shape[1]
     groups = nrows // GROUP
 
-    copies = [(None, pltpu.make_async_copy(p_ref, p_here, sems.at[0]))]
-    for k, ((which, at, rows), part) in enumerate(zip(places, part_refs)):
-        copy = pltpu.make_async_copy(part.at[pl.ds(0, rows * edge)], held.at[piece(edge, at, rows)], sems.at[k + 1])
-        copies.append((None if which is None else size[0] == which, copy))
-
-    def each(act):
-        for needed, copy in copies:
-            if needed is None:
-                act(copy)
-            else:
-                pl.when(needed)(functools.partial(act, copy))
-
-    each(lambda copy: copy.start())
+    p_copy = pltpu.make_async_copy(p_ref, p_here, sems.at[0])
+    p_copy.start()
 
     at = jnp.int32(0)
     for r in range(nrows):
@@ -212,11 +201,38 @@
     starts[nrows] = at
     low, high = 0, groups
     if name != "first":
-        room = places[-1][2] if name == "early" else places[2][2]
+        room = [count for kind, _, count in places if kind == "second"][0]
         done = jnp.int32(0)
         for g in range(leading // GROUP):
             done = done + (starts[(g + 1) * GROUP] <= room).astype(jnp.int32)
         low, high = (0, done) if name == "early" else (done, groups)
+
+    copies = []
+    for (kind, at, count), part in zip(places, part_refs):
+        step = count
+        if name == "late" and kind == "second":
+            step = -(-count // 4)
+        for first in range(0, count, step):
+            needed = None
+            if name == "late" and kind == "first":
+                needed = low < leading // GROUP
+            elif name == "late" and kind == "second":
+                needed = starts[low * GROUP] < first + step
+            elif not isinstance(kind, str):
+                needed = size[0] == kind
+            tall = min(step, count - first) * edge
+            source = part.at[pl.ds(first * edge, tall)]
+            target = held.at[pl.ds((at + first) * edge, tall)]
+            copies.append((needed, pltpu.make_async_copy(source, target, sems.at[1 + len(copies)])))
+
+    def each(act):
+        for needed, copy in copies:
+            if needed is None:
+                act(copy)
+            else:
+                pl.when(needed)(functools.partial(act, copy))
+
+    each(lambda copy: copy.start())
 
     def total_copy(g):
         here = piece(edge, g * GROUP, GROUP)
@@ -238,6 +254,7 @@
     if name != "first":
         held[pl.ds(held.shape[0] - edge, edge), :] = jnp.zeros((edge, held.shape[1]), held.dtype)
     each(lambda copy: copy.wait())
+    p_copy.wait()
 
     def group(g):
         if name != "first":
@@ -275,7 +292,7 @@
             pltpu.VMEM(((room + later) * edge, PAIR * edge), p_tile.dtype),
             pltpu.VMEM(p_tile.shape, p_tile.dtype),
             pltpu.VMEM((tall, width), dtype),
-            pltpu.SemaphoreType.DMA((len(parts) + 1,)),
+            pltpu.SemaphoreType.DMA((len(parts) + 8,)),
             pltpu.SemaphoreType.DMA((groups,)),
         ]
         + [pltpu.VMEM((tall, width), jnp.float32), pltpu.SemaphoreType.DMA((groups,))] * later,
@@ -294,8 +311,8 @@
     )
 
 
-def remainder(k, slots, leading, places, rests, notes, lead, extra, p_second, total):
-    rest = [shifted(part, "col", -1) if k == n else part for n, part in enumerate(rests)]
+def remainder(k, slots, leading, places, rests, unused, notes, lead, extra, p_second, total):
+    rest = [shifted(part, "col", -1) if k == n else other for n, (part, other) in enumerate(zip(rests, unused))]
     return step_product("early", notes, slots, leading, places, (lead, extra), p_second, total), rest
 
 
@@ -304,20 +321,22 @@
     edge = f_blocks.shape[0] // nrows
     cols, counts = block_cols.T, block_counts.T
     groups = nrows // GROUP
-    leading = (groups - groups * 3 // 8) * GROUP
+    leading = (groups - groups // 4) * GROUP
     others = nrows * (slots // PAIR - 1)
     unit = others // 24
-    always = 10 * unit
-    ends = [always + k * unit for k in (2, 3, 4, 5, 6, 7, 9)] + [others]
-
-    lead = shifted(leading_pieces(leading, f_blocks, cols, counts), "col", -1)
-    p_second = shifted(p_matrix, "row", -1)
+    always = 11 * unit
+    ends = [always + k * unit for k in (1, 2, 3, 4, 5, 6, 8)] + [others]
+
+    lead, p_second = lax.optimization_barrier((leading_pieces(leading, f_blocks, cols, counts), p_matrix))
+    lead = shifted(lead, "col", -1)
     notes = jnp.concatenate([cols, jnp.broadcast_to(counts, (slots, nrows))], axis=0)
     packed, extra = packed_pieces(notes, slots, always, f_blocks)
     extra = shifted(extra, "col", -1)
-    later, *rests = cut_pieces([(leading, nrows)] + [(nrows + always, nrows + end) for end in ends], packed)
+    p_second = shifted(p_second, "row", -1)
+    rests = cut_pieces([(nrows + always, nrows + end) for end in ends] + [(leading, nrows)], packed)
+    rests, later, unused = rests[: len(ends)], rests[len(ends)], rests[len(ends) + 1 : -1]
     every = packed.shape[0] // edge
-    total = step_product("first", notes, slots, leading, [(None, 0, every)], (packed,), p_matrix)
+    total = step_product("first", notes, slots, leading, [("all", 0, every)], (packed,), p_matrix)
     later, total = lax.optimization_barrier((later, total))
     later = shifted(later, "col", -1)
 
@@ -328,11 +347,11 @@
         most = jnp.maximum(most, shifted(most, "col", -distance))
         distance *= 2
     size = sum((most > end).astype(jnp.int32) for end in ends[:-1])
-    early = [(None, 0, leading), (None, nrows, always)]
-    late = [early[0], (None, leading, nrows - leading), early[1]]
+    early = [("first", 0, leading), ("second", nrows, always)]
+    late = [early[0], ("later", leading, nrows - leading), early[1]]
     late += [(k, nrows + always, end - always) for k, end in enumerate(ends)]
     branches = [functools.partial(remainder, k, slots, leading, early) for k in range(len(ends))]
-    out, rest = lax.switch(size, branches, rests, notes_next, lead, extra, p_second, total)
+    out, rest = lax.switch(size, branches, rests, unused, notes_next, lead, extra, p_second, total)
     parts = (lead, later, extra, *rest)
     return step_product("late", notes_next, slots, leading, late, parts, p_second, total, size.reshape(1), out)
 

time: 46.3 us -> 47.3 us (1.022)
  waiting for transfers between devices: 3.99 us -> 5.54 us
  local copies, waits for them, and re-layouts: 1.56 us -> 0.76 us
    ppermute x6, waiting for transfers between devices: 3.99 us -> 5.54 us  [shifted(): return lax.ppermute(block, axis, route)]
    cond x2 -> x1, local copies, waits for them, and re-layouts: 0.79 us -> 0.01 us
  transfers between devices with their start and end apart: 6 -> 6, of which waited for: 3 -> 2; matrix products, arithmetic and copies ran while one was open for 5% -> 3% of each run, Pallas kernels for 37% -> 34%
where the time goes in v5:
time: 47.3 us; the launch traced here: 47.1 us
  Pallas kernels  22.3 us (47%)
  starting transfers between devices  15.3 us (32%)
  waiting for transfers between devices  5.54 us (12%)
  between operations  1.85 us (4%)
  other arithmetic  1.26 us (3%)
  local copies, waits for them, and re-layouts  0.76 us (2%)
    pallas_call x3, Pallas kernels, step_product(): pl.pallas_call(functools.partial(step_kernel, edge, slots, name, leading,...  16.5 us
    ppermute x6, starting transfers between devices, shifted(): return lax.ppermute(block, axis, route)  15.3 us
    ppermute x6, waiting for transfers between devices, shifted(): return lax.ppermute(block, axis, route)  5.54 us
    pallas_call x1, Pallas kernels, packed_pieces(): pl.pallas_call(functools.partial(pack_kernel, edge, slots), in_specs=[SME...  2.03 us
    pallas_call x1, Pallas kernels, leading_pieces(): pl.pallas_call(functools.partial(leading_kernel, edge), grid_spec=pltpu.P...  1.9 us
    pallas_call x1, Pallas kernels, cut_pieces(): pl.pallas_call(functools.partial(cut_kernel, rows), in_specs=[ANY], out_s...  1.79 us
  transfers between devices with their start and end apart: 6, of which 2 were waited for; matrix products, arithmetic and copies ran while one was open for 3% of the time, Pallas kernels for 34%

profile of v5, /device:TPU:0, one launch (start us, length us, event | category | flops | bytes accessed | tf_op | source)
XLA Modules:
  0.0 47.1 jit_solution(1774023286109766663)
XLA Ops:
  0.0 1.9 %leading_pieces.1 = bf16[1552,128]{1,0:T(8,128)(2,1)S(1)} custom-call(s32[1,32]{1,0:T(1,128)} %bitcast.13, bf16[2048,512]{1,0:T(8,128)(2,1)} %f_ref.3, s32[8,32]{1,0:T(8,128)} %bitcast.11, s32[1,32]{1,0:T(1,128)} %bitcast.14), custom_call_target="tpu_custom_call" | custom-call | bytes 786432 | tf_op jit(solution)/shard_map/leading_pieces/pallas_call | solution.py:64
  1.9 4.5 %collective-permute-start.12 = (bf16[1536,512]{1,0:T(8,128)(2,1)}, bf16[1536,512]{1,0:T(8,128)(2,1)S(1)}, u32[]{:S(2)}, u32[]{:S(2)}) collective-permute-start(bf16[1536,512]{1,0:T(8,128)(2,1)} %refs_1_.1), channel_id=1, source_target_pairs={{4,0},{8,4},{12,8},{16,12},{20,16},{24,20},{28,24},{0,28},{5,1},{9... | collective-permute-start | bytes 4718600 | tf_op jit(solution)/shard_map/ppermute | solution.py:21
  6.5 2.4 %collective-permute-start.8 = (bf16[1552,128]{1,0:T(8,128)(2,1)S(1)}, bf16[1552,128]{1,0:T(8,128)(2,1)S(1)}, u32[]{:S(2)}, u32[]{:S(2)}) collective-permute-start(bf16[1552,128]{1,0:T(8,128)(2,1)S(1)} %leading_pieces.1), channel_id=1, source_target_pairs={{1,0},{2,1},{3,2},{0,3},{5,4},{6,5},{7,6},{4,7},{9,8},{10,9},{11,1... | collective-permute-start | bytes 1191944 | tf_op jit(solution)/shard_map/ppermute | solution.py:21
  8.9 0.0 copy-done.8
  8.9 0.0 copy-start.1
  8.9 2.0 %pack_live_pieces.1 = (bf16[8256,128]{1,0:T(8,128)(2,1)S(1)}, bf16[2816,128]{1,0:T(8,128)(2,1)S(1)}) custom-call(s32[16,32]{1,0:T(8,128)S(1)} %pad_add_fusion.notes, bf16[2048,512]{1,0:T(8,128)(2,1)S(1)} %copy-done), custom_call_target="tpu_custom_call" | custom-call | bytes 4194304 | tf_op jit(solution)/shard_map/pack_live_pieces/pallas_call | solution.py:116
  11.0 0.6 %collective-permute-start.11 = (bf16[2816,128]{1,0:T(8,128)(2,1)S(1)}, bf16[2816,128]{1,0:T(8,128)(2,1)S(1)}, u32[]{:S(2)}, u32[]{:S(2)}) collective-permute-start(bf16[2816,128]{1,0:T(8,128)(2,1)S(1)} %get-tuple-element.353), channel_id=1, source_target_pairs={{1,0},{2,1},{3,2},{0,3},{5,4},{6,5},{7,6},{4,7},{9,8},{10,9},{11,1... | collective-permute-start | bytes 2162696 | tf_op jit(solution)/shard_map/ppermute | solution.py:21
  11.6 1.8 %cut_pieces.1 = (bf16[256,128]{1,0:T(8,128)(2,1)}, bf16[512,128]{1,0:T(8,128)(2,1)}, bf16[768,128]{1,0:T(8,128)(2,1)S(1)}, bf16[1024,128]{1,0:T(8,128)(2,1)}, bf...) custom-call(bf16[8256,128]{1,0:T(8,128)(2,1)S(1)} %get-tuple-element, ...), custom_call_target="tpu_custom_call" | custom-call | bytes 5767168 | tf_op jit(solution)/shard_map/cut_pieces/pallas_call | solution.py:150
  13.4 5.9 %step_first.1.refs_13_ = f32[2048,512]{1,0:T(8,128)} custom-call(s32[16,32]{1,0:T(8,128)S(1)} %pad_add_fusion.notes, bf16[8256,128]{1,0:T(8,128)(2,1)S(1)} %get-tuple-element.350.packed_ref.refs_0_, bf16[1536,512]{1,0:T(8,128)(2,1)S(1)} %copy-done.1), custom_call_target="tpu_custom_call" | custom-call | flops 536870912 | bytes 4194304 | tf_op jit(solution)/shard_map/step_first/pallas_call | solution.py:286
  19.3 1.5 %collective-permute-start.10 = (bf16[512,128]{1,0:T(8,128)(2,1)S(1)}, bf16[512,128]{1,0:T(8,128)(2,1)S(1)}, u32[]{:S(2)}, u32[]{:S(2)}) collective-permute-start(bf16[512,128]{1,0:T(8,128)(2,1)S(1)} %get-tuple-element.352), channel_id=1, source_target_pairs={{1,0},{2,1},{3,2},{0,3},{5,4},{6,5},{7,6},{4,7},{9,8},{10,9},{11,1... | collective-permute-start | bytes 393224 | tf_op jit(solution)/shard_map/ppermute | solution.py:21
  20.8 0.6 %add_reduce_fusion.1 = s32[]{:T(128)} fusion(s32[32,1]{0,1:T(1,128)S(1)} %copy-done.9), kind=kLoop, calls=%fused_computation.13 | loop fusion | flops 575 | bytes 132 | tf_op jit(solution)/shard_map/reduce_sum | solution.py:344
  21.4 0.0 collective-permute-done.8.refs_1_
  21.4 0.7 %copy-done.2 = bf16[1552,128]{1,0:T(8,128)(2,1)} copy-done((bf16[1552,128]{1,0:T(8,128)(2,1)}, bf16[1552,128]{1,0:T(8,128)(2,1)S(1)}, u32[]{:S(2)}) %copy-start.2) | copy-done | bytes 397336
  22.1 0.6 %add_reduce_fusion = s32[]{:T(128)} fusion(s32[16,32]{1,0:T(8,128)S(1)} %convert_convert_fusion.notes), kind=kLoop, calls=%fused_computation.12 | loop fusion | flops 575 | bytes 132 | tf_op jit(solution)/shard_map/reduce_sum | solution.py:344
  24.0 2.9 %collective-permute-start.9 = (s32[]{:T(128)}, s32[]{:T(128)}, u32[]{:S(2)}, u32[]{:S(2)}) collective-permute-start(s32[]{:T(128)} %max.6), channel_id=1, source_target_pairs={{2,0},{3,1},{0,2},{1,3},{6,4},{7,5},{4,6},{5,7},{10,8},{11,9},{8,1... | collective-permute-start | bytes 20 | tf_op jit(solution)/shard_map/ppermute | solution.py:21
  26.8 0.8 %collective-permute-done.9 = s32[]{:T(128)} collective-permute-done((s32[]{:T(128)}, s32[]{:T(128)}, u32[]{:S(2)}, u32[]{:S(2)}) %collective-permute-start.9) | collective-permute-done | bytes 36 | tf_op jit(solution)/shard_map/ppermute | solution.py:21
  28.2 4.7 %collective-permute-done.11.refs_3_ = bf16[2816,128]{1,0:T(8,128)(2,1)S(1)} collective-permute-done((bf16[2816,128]{1,0:T(8,128)(2,1)S(1)}, bf16[2816,128]{1,0:T(8,128)(2,1)S(1)}, u32[]{:S(2)}, u32[]{:S(2)}) %collective-permute-start.11) | collective-permute-done | bytes 720928 | tf_op jit(solution)/shard_map/ppermute | solution.py:21
  32.9 0.0 collective-permute-done.12.refs_12_
  32.9 9.6 %conditional.1 = (bf16[2048,512]{1,0:T(8,128)(2,1)}, bf16[256,128]{1,0:T(8,128)(2,1)S(1)}, bf16[512,128]{1,0:T(8,128)(2,1)}, bf16[768,128]{1,0:T(8,128)(2,1)}, b...) conditional(s32[]{:T(128)} %clamp.3, (s32[16,32]{1,0:T(8,128)S(1)}, ...), branch_computations={%region_2.3_spmd, %region_3.4_spmd, %region_4.5_spmd, %region_5.6_... | conditional | flops 536870912 | bytes 11141260 | solution.py:354
  32.9 3.4 %collective-permute-start.2 = (bf16[768,128]{1,0:T(8,128)(2,1)S(1)}, bf16[768,128]{1,0:T(8,128)(2,1)}, u32[]{:S(2)}, u32[]{:S(2)}) collective-permute-start(bf16[768,128]{1,0:T(8,128)(2,1)S(1)} %get-tuple-element.246), channel_id=1, source_target_pairs={{1,0},{2,1},{3,2},{0,3},{5,4},{6,5},{7,6},{4,7},{9,8},{10,9},{11,1... | collective-permute-start | bytes 589832 | tf_op jit(solution)/shard_map/cond/branch_2_fun/ppermute | solution.py:21
  36.3 6.1 %step_early.10 = bf16[2048,512]{1,0:T(8,128)(2,1)} custom-call(s32[16,32]{1,0:T(8,128)S(1)} %get-tuple-element.239.notes, bf16[1552,128]{1,0:T(8,128)(2,1)} %get-tuple-element.240.refs_0_, bf16[2816,128]{1,0:T(8,128)(2,1)S(1)} %get-tuple-element.241.refs_1_, bf16[1536,512]{1,0:T(8,128)(2,1)S(1)} %get-tuple-element.242.refs_2_, ...), custom_call_target="tpu_custom_call" | custom-call | flops 536870912 | bytes 4194304 | tf_op jit(solution)/shard_map/cond/branch_2_fun/step_early/pallas_call | solution.py:286
  42.5 0.0 collective-permute-done.2
  42.5 0.0 collective-permute-done.10.refs_2_
  42.5 4.5 %step_late.1 = bf16[2048,512]{1,0:T(8,128)(2,1)} custom-call(s32[16,32]{1,0:T(8,128)S(1)} %convert_convert_fusion.notes, s32[1]{0:T(128)} %bitcast.3.refs_0_, bf16[1552,128]{1,0:T(8,128)(2,1)} %copy-done.2, bf16[512,128]{1,0:T(8,128)(2,1)S(1)} %collective-permute-done.10.refs_2_, ...), custom_call_target="tpu_custom_call", output_to_operand_aliasing={{}: (15, {})} | custom-call | flops 536870912 | bytes 4194304 | tf_op jit(solution)/shard_map/step_late/pallas_call | solution.py:286
  (11 shorter events, 0.0 us)
Async XLA Ops:
  0.0 8.9 %copy-start = (bf16[2048,512]{1,0:T(8,128)(2,1)S(1)}, bf16[2048,512]{1,0:T(8,128)(2,1)}, u32[]{:S(2)}) copy-start(bf16[2048,512]{1,0:T(8,128)(2,1)} %f_ref.3) | copy-start | bytes 6291460
  0.0 8.9 %copy-start.9 = (s32[32,1]{0,1:T(1,128)S(1)}, s32[32,1]{0,1:T(1,128)}, u32[]{:S(2)}) copy-start(s32[32,1]{0,1:T(1,128)} %param.14) | copy-start | bytes 388
  0.0 8.9 %copy-start.8 = (s32[32,8]{0,1:T(8,128)S(1)}, s32[32,8]{0,1:T(8,128)}, u32[]{:S(2)}) copy-start(s32[32,8]{0,1:T(8,128)} %param.13) | copy-start | bytes 3076
  1.9 31.0 %collective-permute-start.12 = (bf16[1536,512]{1,0:T(8,128)(2,1)}, bf16[1536,512]{1,0:T(8,128)(2,1)S(1)}, u32[]{:S(2)}, u32[]{:S(2)}) collective-permute-start(bf16[1536,512]{1,0:T(8,128)(2,1)} %refs_1_.1), channel_id=1, source_target_pairs={{4,0},{8,4},{12,8},{16,12},{20,16},{24,20},{28,24},{0,28},{5,1},{9... | collective-permute-start | bytes 4718600 | tf_op jit(solution)/shard_map/ppermute | solution.py:21
  6.5 14.9 %collective-permute-start.8 = (bf16[1552,128]{1,0:T(8,128)(2,1)S(1)}, bf16[1552,128]{1,0:T(8,128)(2,1)S(1)}, u32[]{:S(2)}, u32[]{:S(2)}) collective-permute-start(bf16[1552,128]{1,0:T(8,128)(2,1)S(1)} %leading_pieces.1), channel_id=1, source_target_pairs={{1,0},{2,1},{3,2},{0,3},{5,4},{6,5},{7,6},{4,7},{9,8},{10,9},{11,1... | collective-permute-start | bytes 1191944 | tf_op jit(solution)/shard_map/ppermute | solution.py:21
  8.9 4.4 %copy-start.1 = (bf16[1536,512]{1,0:T(8,128)(2,1)S(1)}, bf16[1536,512]{1,0:T(8,128)(2,1)}, u32[]{:S(2)}) copy-start(bf16[1536,512]{1,0:T(8,128)(2,1)} %refs_1_.1) | copy-start | bytes 4718596
  11.0 22.0 %collective-permute-start.11 = (bf16[2816,128]{1,0:T(8,128)(2,1)S(1)}, bf16[2816,128]{1,0:T(8,128)(2,1)S(1)}, u32[]{:S(2)}, u32[]{:S(2)}) collective-permute-start(bf16[2816,128]{1,0:T(8,128)(2,1)S(1)} %get-tuple-element.353), channel_id=1, source_target_pairs={{1,0},{2,1},{3,2},{0,3},{5,4},{6,5},{7,6},{4,7},{9,8},{10,9},{11,1... | collective-permute-start | bytes 2162696 | tf_op jit(solution)/shard_map/ppermute | solution.py:21
  19.3 23.3 %collective-permute-start.10 = (bf16[512,128]{1,0:T(8,128)(2,1)S(1)}, bf16[512,128]{1,0:T(8,128)(2,1)S(1)}, u32[]{:S(2)}, u32[]{:S(2)}) collective-permute-start(bf16[512,128]{1,0:T(8,128)(2,1)S(1)} %get-tuple-element.352), channel_id=1, source_target_pairs={{1,0},{2,1},{3,2},{0,3},{5,4},{6,5},{7,6},{4,7},{9,8},{10,9},{11,1... | collective-permute-start | bytes 393224 | tf_op jit(solution)/shard_map/ppermute | solution.py:21
  21.4 0.7 %copy-start.2 = (bf16[1552,128]{1,0:T(8,128)(2,1)}, bf16[1552,128]{1,0:T(8,128)(2,1)S(1)}, u32[]{:S(2)}) copy-start(bf16[1552,128]{1,0:T(8,128)(2,1)S(1)} %collective-permute-done.8.refs_1_) | copy-start | bytes 1191940
  24.0 3.7 %collective-permute-start.9 = (s32[]{:T(128)}, s32[]{:T(128)}, u32[]{:S(2)}, u32[]{:S(2)}) collective-permute-start(s32[]{:T(128)} %max.6), channel_id=1, source_target_pairs={{2,0},{3,1},{0,2},{1,3},{6,4},{7,5},{4,6},{5,7},{10,8},{11,9},{8,1... | collective-permute-start | bytes 20 | tf_op jit(solution)/shard_map/ppermute | solution.py:21
  32.9 9.6 %collective-permute-start.2 = (bf16[768,128]{1,0:T(8,128)(2,1)S(1)}, bf16[768,128]{1,0:T(8,128)(2,1)}, u32[]{:S(2)}, u32[]{:S(2)}) collective-permute-start(bf16[768,128]{1,0:T(8,128)(2,1)S(1)} %get-tuple-element.246), channel_id=1, source_target_pairs={{1,0},{2,1},{3,2},{0,3},{5,4},{6,5},{7,6},{4,7},{9,8},{10,9},{11,1... | collective-permute-start | bytes 589832 | tf_op jit(solution)/shard_map/cond/branch_2_fun/ppermute | solution.py:21

commit v6 on v5

--- a/solution.py
+++ b/solution.py
@@ -285,8 +285,8 @@
     late = name == "late"
     return pl.pallas_call(
         functools.partial(step_kernel, edge, slots, name, leading, places),
-        in_specs=[SMEM] * (1 + late) + [ANY] * (len(parts) + 1 + later) + [HBM] * late,
-        out_specs=HBM if later else ANY,
+        in_specs=[SMEM] * (1 + late) + [ANY] * len(parts) + [HBM] * (1 + later + late),
+        out_specs=HBM,
         scratch_shapes=[
             pltpu.SMEM((nrows + 1,), jnp.int32),
             pltpu.VMEM(((room + later) * edge, PAIR * edge), p_tile.dtype),
@@ -296,17 +296,17 @@
             pltpu.SemaphoreType.DMA((groups,)),
         ]
         + [pltpu.VMEM((tall, width), jnp.float32), pltpu.SemaphoreType.DMA((groups,))] * later,
-        out_shape=(pltpu.HBM if later else jax.ShapeDtypeStruct)((tall, width), dtype),
+        out_shape=pltpu.HBM((tall, width), dtype),
         input_output_aliases={4 + len(parts): 0} if late else {},
-        cost_estimate=cost(tall * width * slots * edge, 4 * tall * width),
+        cost_estimate=cost((1 if later else 20) * tall * width * slots * edge, 4 * tall * width),
         compiler_params=params(16),
         name="step_" + name,
     )(
         notes,
         *([size] if late else []),
         *parts,
-        p_tile,
-        *([total] if later else []),
+        in_hbm(p_tile),
+        *([in_hbm(total)] if later else []),
         *([in_hbm(out)] if late else []),
     )
 
@@ -327,20 +327,21 @@
     always = 11 * unit
     ends = [always + k * unit for k in (1, 2, 3, 4, 5, 6, 8)] + [others]
 
-    lead, p_second = lax.optimization_barrier((leading_pieces(leading, f_blocks, cols, counts), p_matrix))
-    lead = shifted(lead, "col", -1)
+    lead = shifted(leading_pieces(leading, f_blocks, cols, counts), "col", -1)
     notes = jnp.concatenate([cols, jnp.broadcast_to(counts, (slots, nrows))], axis=0)
     packed, extra = packed_pieces(notes, slots, always, f_blocks)
     extra = shifted(extra, "col", -1)
+    p_second, packed = lax.optimization_barrier((p_matrix, packed))
     p_second = shifted(p_second, "row", -1)
     rests = cut_pieces([(nrows + always, nrows + end) for end in ends] + [(leading, nrows)], packed)
     rests, later, unused = rests[: len(ends)], rests[len(ends)], rests[len(ends) + 1 : -1]
     every = packed.shape[0] // edge
+    notes_next = lead[leading * edge :, :nrows].astype(jnp.float32).astype(jnp.int32)
+    packed, notes_next = lax.optimization_barrier((packed, notes_next))
     total = step_product("first", notes, slots, leading, [("all", 0, every)], (packed,), p_matrix)
     later, total = lax.optimization_barrier((later, total))
     later = shifted(later, "col", -1)
 
-    notes_next = lead[leading * edge :, :nrows].astype(jnp.float32).astype(jnp.int32)
     most = jnp.maximum(jnp.sum(others_of(counts)), jnp.sum(others_of(notes_next[slots])))
     distance = 2
     while distance < lax.axis_size("col"):

time: 47.3 us -> 45.5 us (0.962)
  starting transfers between devices: 15.3 us -> 14.3 us
  waiting for transfers between devices: 5.54 us -> 4.71 us
  local copies, waits for them, and re-layouts: 0.76 us -> 0.02 us
  Pallas kernels: 22.3 us -> 22.8 us
    pallas_call x3, Pallas kernels: 16.5 us -> 17.7 us  [step_product(): pl.pallas_call(functools.partial(step_kernel, edge, slots, name, leading,...]
    ppermute x6, starting transfers between devices: 15.3 us -> 14.3 us  [shifted(): return lax.ppermute(block, axis, route)]
    ppermute x6, waiting for transfers between devices: 5.54 us -> 4.71 us  [shifted(): return lax.ppermute(block, axis, route)]
    unnamed x10 -> x6, local copies, waits for them, and re-layouts: 0.76 us -> 0.01 us
    pallas_call x1, Pallas kernels: 1.79 us -> 1.18 us  [cut_pieces(): pl.pallas_call(functools.partial(cut_kernel, rows), in_specs=[ANY], out_s...]
  transfers between devices with their start and end apart: 6 -> 6, of which waited for: 2 -> 2; matrix products, arithmetic and copies ran while one was open for 3% -> 3% of each run, Pallas kernels for 34% -> 36%
where the time goes in v6:
time: 45.5 us; the launch traced here: 45.2 us
  Pallas kernels  22.8 us (50%)
  starting transfers between devices  14.3 us (31%)
  waiting for transfers between devices  4.71 us (10%)
  between operations  2.03 us (4%)
  other arithmetic  1.35 us (3%)
    pallas_call x3, Pallas kernels, step_product(): pl.pallas_call(functools.partial(step_kernel, edge, slots, name, leading,...  17.7 us
    ppermute x6, starting transfers between devices, shifted(): return lax.ppermute(block, axis, route)  14.3 us
    ppermute x6, waiting for transfers between devices, shifted(): return lax.ppermute(block, axis, route)  4.71 us
    pallas_call x1, Pallas kernels, packed_pieces(): pl.pallas_call(functools.partial(pack_kernel, edge, slots), in_specs=[SME...  2.03 us
    pallas_call x1, Pallas kernels, leading_pieces(): pl.pallas_call(functools.partial(leading_kernel, edge), grid_spec=pltpu.P...  1.9 us
    pallas_call x1, Pallas kernels, cut_pieces(): pl.pallas_call(functools.partial(cut_kernel, rows), in_specs=[ANY], out_s...  1.18 us
  transfers between devices with their start and end apart: 6, of which 2 were waited for; matrix products, arithmetic and copies ran while one was open for 3% of the time, Pallas kernels for 36%

profile of v6, /device:TPU:0, one launch (start us, length us, event | category | flops | bytes accessed | tf_op | source)
XLA Modules:
  0.0 45.2 jit_solution(14604454000614233388)
XLA Ops:
  0.0 1.9 %leading_pieces.1 = bf16[1552,128]{1,0:T(8,128)(2,1)S(1)} custom-call(s32[1,32]{1,0:T(1,128)} %bitcast.17, bf16[2048,512]{1,0:T(8,128)(2,1)} %f_ref.3, s32[8,32]{1,0:T(8,128)} %bitcast.15, s32[1,32]{1,0:T(1,128)} %bitcast.18), custom_call_target="tpu_custom_call" | custom-call | bytes 786432 | tf_op jit(solution)/shard_map/leading_pieces/pallas_call | solution.py:64
  1.9 4.0 %collective-permute-start.8 = (bf16[1552,128]{1,0:T(8,128)(2,1)S(1)}, bf16[1552,128]{1,0:T(8,128)(2,1)S(1)}, u32[]{:S(2)}, u32[]{:S(2)}) collective-permute-start(bf16[1552,128]{1,0:T(8,128)(2,1)S(1)} %leading_pieces.1), channel_id=1, source_target_pairs={{1,0},{2,1},{3,2},{0,3},{5,4},{6,5},{7,6},{4,7},{9,8},{10,9},{11,1... | collective-permute-start | bytes 1191944 | tf_op jit(solution)/shard_map/ppermute | solution.py:21
  5.9 0.0 copy-done.2
  5.9 0.0 copy-done.1
  5.9 0.0 copy-done
  5.9 2.0 %pack_live_pieces.1 = (bf16[8256,128]{1,0:T(8,128)(2,1)S(1)}, bf16[2816,128]{1,0:T(8,128)(2,1)S(1)}) custom-call(s32[16,32]{1,0:T(8,128)S(1)} %pad_add_fusion.notes, bf16[2048,512]{1,0:T(8,128)(2,1)S(1)} %copy-done), custom_call_target="tpu_custom_call" | custom-call | bytes 4194304 | tf_op jit(solution)/shard_map/pack_live_pieces/pallas_call | solution.py:116
  7.9 2.8 %collective-permute-start.12 = (bf16[1536,512]{1,0:T(8,128)(2,1)}, bf16[1536,512]{1,0:T(8,128)(2,1)}, u32[]{:S(2)}, u32[]{:S(2)}) collective-permute-start(bf16[1536,512]{1,0:T(8,128)(2,1)} %refs_1_.1), channel_id=1, source_target_pairs={{4,0},{8,4},{12,8},{16,12},{20,16},{24,20},{28,24},{0,28},{5,1},{9... | collective-permute-start | bytes 4718600 | tf_op jit(solution)/shard_map/ppermute | solution.py:21
  10.7 0.5 %collective-permute-start.11 = (bf16[2816,128]{1,0:T(8,128)(2,1)S(1)}, bf16[2816,128]{1,0:T(8,128)(2,1)S(1)}, u32[]{:S(2)}, u32[]{:S(2)}) collective-permute-start(bf16[2816,128]{1,0:T(8,128)(2,1)S(1)} %get-tuple-element.357), channel_id=1, source_target_pairs={{1,0},{2,1},{3,2},{0,3},{5,4},{6,5},{7,6},{4,7},{9,8},{10,9},{11,1... | collective-permute-start | bytes 2162696 | tf_op jit(solution)/shard_map/ppermute | solution.py:21
  11.3 1.2 %cut_pieces.1 = (bf16[256,128]{1,0:T(8,128)(2,1)}, bf16[512,128]{1,0:T(8,128)(2,1)}, bf16[768,128]{1,0:T(8,128)(2,1)}, bf16[1024,128]{1,0:T(8,128)(2,1)}, bf16[1...) custom-call(bf16[8256,128]{1,0:T(8,128)(2,1)S(1)} %get-tuple-element, ...), custom_call_target="tpu_custom_call" | custom-call | bytes 5767168 | tf_op jit(solution)/shard_map/cut_pieces/pallas_call | solution.py:150
  12.5 3.0 %collective-permute-done.8.refs_1_ = bf16[1552,128]{1,0:T(8,128)(2,1)S(1)} collective-permute-done((bf16[1552,128]{1,0:T(8,128)(2,1)S(1)}, bf16[1552,128]{1,0:T(8,128)(2,1)S(1)}, u32[]{:S(2)}, u32[]{:S(2)}) %collective-permute-start.8) | collective-permute-done | bytes 397344 | tf_op jit(solution)/shard_map/ppermute | solution.py:21
  15.5 6.8 %step_first.1.refs_13_ = f32[2048,512]{1,0:T(8,128)} custom-call(s32[16,32]{1,0:T(8,128)S(1)} %pad_add_fusion.notes, bf16[8256,128]{1,0:T(8,128)(2,1)S(1)} %get-tuple-element.355.packed_ref.refs_0_, bf16[1536,512]{1,0:T(8,128)(2,1)} %refs_1_.1), custom_call_target="tpu_custom_call" | custom-call | flops 10737418240 | bytes 4194304 | tf_op jit(solution)/shard_map/step_first/pallas_call | solution.py:286
  22.3 3.4 %collective-permute-start.10 = (bf16[512,128]{1,0:T(8,128)(2,1)S(1)}, bf16[512,128]{1,0:T(8,128)(2,1)S(1)}, u32[]{:S(2)}, u32[]{:S(2)}) collective-permute-start(bf16[512,128]{1,0:T(8,128)(2,1)S(1)} %get-tuple-element.356), channel_id=1, source_target_pairs={{1,0},{2,1},{3,2},{0,3},{5,4},{6,5},{7,6},{4,7},{9,8},{10,9},{11,1... | collective-permute-start | bytes 393224 | tf_op jit(solution)/shard_map/ppermute | solution.py:21
  25.8 0.6 %add_reduce_fusion.1 = s32[]{:T(128)} fusion(s32[32,1]{0,1:T(1,128)S(1)} %copy-done.2), kind=kLoop, calls=%fused_computation.12 | loop fusion | flops 575 | bytes 132 | tf_op jit(solution)/shard_map/reduce_sum | solution.py:345
  26.4 0.7 %add_reduce_fusion = s32[]{:T(128)} fusion(s32[16,32]{1,0:T(8,128)S(1)} %convert_convert_fusion.notes), kind=kLoop, calls=%fused_computation.11 | loop fusion | flops 575 | bytes 132 | tf_op jit(solution)/shard_map/reduce_sum | solution.py:345
  28.4 1.9 %collective-permute-start.9 = (s32[]{:T(128)}, s32[]{:T(128)}, u32[]{:S(2)}, u32[]{:S(2)}) collective-permute-start(s32[]{:T(128)} %max.6), channel_id=1, source_target_pairs={{2,0},{3,1},{0,2},{1,3},{6,4},{7,5},{4,6},{5,7},{10,8},{11,9},{8,1... | collective-permute-start | bytes 20 | tf_op jit(solution)/shard_map/ppermute | solution.py:21
  30.2 1.7 %collective-permute-done.9 = s32[]{:T(128)} collective-permute-done((s32[]{:T(128)}, s32[]{:T(128)}, u32[]{:S(2)}, u32[]{:S(2)}) %collective-permute-start.9) | collective-permute-done | bytes 36 | tf_op jit(solution)/shard_map/ppermute | solution.py:21
  32.6 0.0 collective-permute-done.11.refs_3_
  32.6 0.0 collective-permute-done.12.refs_12_
  32.6 8.0 %conditional.1 = (bf16[2048,512]{1,0:T(8,128)(2,1)}, bf16[256,128]{1,0:T(8,128)(2,1)S(1)}, bf16[512,128]{1,0:T(8,128)(2,1)}, bf16[768,128]{1,0:T(8,128)(2,1)}, b...) conditional(s32[]{:T(128)} %clamp.3, (s32[16,32]{1,0:T(8,128)S(1)}, ...), branch_computations={%region_2.3_spmd, %region_3.4_spmd, %region_4.5_spmd, %region_5.6_... | conditional | flops 536870912 | bytes 7733360 | solution.py:355
  32.7 1.7 %collective-permute-start.3 = (bf16[1024,128]{1,0:T(8,128)(2,1)}, bf16[1024,128]{1,0:T(8,128)(2,1)}, u32[]{:S(2)}, u32[]{:S(2)}) collective-permute-start(bf16[1024,128]{1,0:T(8,128)(2,1)} %get-tuple-element.260), channel_id=1, source_target_pairs={{1,0},{2,1},{3,2},{0,3},{5,4},{6,5},{7,6},{4,7},{9,8},{10,9},{11,1... | collective-permute-start | bytes 786440 | tf_op jit(solution)/shard_map/cond/branch_3_fun/ppermute | solution.py:21
  34.3 6.3 %step_early.11 = bf16[2048,512]{1,0:T(8,128)(2,1)} custom-call(s32[16,32]{1,0:T(8,128)S(1)} %get-tuple-element.252.notes, bf16[1552,128]{1,0:T(8,128)(2,1)S(1)} %get-tuple-element.253.refs_0_, bf16[2816,128]{1,0:T(8,128)(2,1)S(1)} %get-tuple-element.254.refs_1_, bf16[1536,512]{1,0:T(8,128)(2,1)} %get-tuple-element.255.refs_2_, ...), custom_call_target="tpu_custom_call" | custom-call | flops 536870912 | bytes 4194304 | tf_op jit(solution)/shard_map/cond/branch_3_fun/step_early/pallas_call | solution.py:286
  40.6 0.0 collective-permute-done.3
  40.7 0.0 collective-permute-done.10.refs_2_
  40.7 4.5 %step_late.1 = bf16[2048,512]{1,0:T(8,128)(2,1)} custom-call(s32[16,32]{1,0:T(8,128)S(1)} %convert_convert_fusion.notes, s32[1]{0:T(128)} %bitcast.4.refs_0_, bf16[1552,128]{1,0:T(8,128)(2,1)S(1)} %collective-permute-done.8.refs_1_, bf16[512,128]{1,0:T(8,128)(2,1)S(1)} %collective-permute-done.10.refs_2_, ...), custom_call_target="tpu_custom_call", output_to_operand_aliasing={{}: (15, {})} | custom-call | flops 536870912 | bytes 4194304 | tf_op jit(solution)/shard_map/step_late/pallas_call | solution.py:286
  (7 shorter events, 0.0 us)
Async XLA Ops:
  0.0 5.9 %copy-start = (bf16[2048,512]{1,0:T(8,128)(2,1)S(1)}, bf16[2048,512]{1,0:T(8,128)(2,1)}, u32[]{:S(2)}) copy-start(bf16[2048,512]{1,0:T(8,128)(2,1)} %f_ref.3) | copy-start | bytes 6291460
  0.0 5.9 %copy-start.2 = (s32[32,1]{0,1:T(1,128)S(1)}, s32[32,1]{0,1:T(1,128)}, u32[]{:S(2)}) copy-start(s32[32,1]{0,1:T(1,128)} %param.14) | copy-start | bytes 388
  0.0 5.9 %copy-start.1 = (s32[32,8]{0,1:T(8,128)S(1)}, s32[32,8]{0,1:T(8,128)}, u32[]{:S(2)}) copy-start(s32[32,8]{0,1:T(8,128)} %param.13) | copy-start | bytes 3076
  1.9 13.6 %collective-permute-start.8 = (bf16[1552,128]{1,0:T(8,128)(2,1)S(1)}, bf16[1552,128]{1,0:T(8,128)(2,1)S(1)}, u32[]{:S(2)}, u32[]{:S(2)}) collective-permute-start(bf16[1552,128]{1,0:T(8,128)(2,1)S(1)} %leading_pieces.1), channel_id=1, source_target_pairs={{1,0},{2,1},{3,2},{0,3},{5,4},{6,5},{7,6},{4,7},{9,8},{10,9},{11,1... | collective-permute-start | bytes 1191944 | tf_op jit(solution)/shard_map/ppermute | solution.py:21
  7.9 24.7 %collective-permute-start.12 = (bf16[1536,512]{1,0:T(8,128)(2,1)}, bf16[1536,512]{1,0:T(8,128)(2,1)}, u32[]{:S(2)}, u32[]{:S(2)}) collective-permute-start(bf16[1536,512]{1,0:T(8,128)(2,1)} %refs_1_.1), channel_id=1, source_target_pairs={{4,0},{8,4},{12,8},{16,12},{20,16},{24,20},{28,24},{0,28},{5,1},{9... | collective-permute-start | bytes 4718600 | tf_op jit(solution)/shard_map/ppermute | solution.py:21
  10.7 21.9 %collective-permute-start.11 = (bf16[2816,128]{1,0:T(8,128)(2,1)S(1)}, bf16[2816,128]{1,0:T(8,128)(2,1)S(1)}, u32[]{:S(2)}, u32[]{:S(2)}) collective-permute-start(bf16[2816,128]{1,0:T(8,128)(2,1)S(1)} %get-tuple-element.357), channel_id=1, source_target_pairs={{1,0},{2,1},{3,2},{0,3},{5,4},{6,5},{7,6},{4,7},{9,8},{10,9},{11,1... | collective-permute-start | bytes 2162696 | tf_op jit(solution)/shard_map/ppermute | solution.py:21
  22.3 18.3 %collective-permute-start.10 = (bf16[512,128]{1,0:T(8,128)(2,1)S(1)}, bf16[512,128]{1,0:T(8,128)(2,1)S(1)}, u32[]{:S(2)}, u32[]{:S(2)}) collective-permute-start(bf16[512,128]{1,0:T(8,128)(2,1)S(1)} %get-tuple-element.356), channel_id=1, source_target_pairs={{1,0},{2,1},{3,2},{0,3},{5,4},{6,5},{7,6},{4,7},{9,8},{10,9},{11,1... | collective-permute-start | bytes 393224 | tf_op jit(solution)/shard_map/ppermute | solution.py:21
  28.4 3.6 %collective-permute-start.9 = (s32[]{:T(128)}, s32[]{:T(128)}, u32[]{:S(2)}, u32[]{:S(2)}) collective-permute-start(s32[]{:T(128)} %max.6), channel_id=1, source_target_pairs={{2,0},{3,1},{0,2},{1,3},{6,4},{7,5},{4,6},{5,7},{10,8},{11,9},{8,1... | collective-permute-start | bytes 20 | tf_op jit(solution)/shard_map/ppermute | solution.py:21
  32.7 8.0 %collective-permute-start.3 = (bf16[1024,128]{1,0:T(8,128)(2,1)}, bf16[1024,128]{1,0:T(8,128)(2,1)}, u32[]{:S(2)}, u32[]{:S(2)}) collective-permute-start(bf16[1024,128]{1,0:T(8,128)(2,1)} %get-tuple-element.260), channel_id=1, source_target_pairs={{1,0},{2,1},{3,2},{0,3},{5,4},{6,5},{7,6},{4,7},{9,8},{10,9},{11,1... | collective-permute-start | bytes 786440 | tf_op jit(solution)/shard_map/cond/branch_3_fun/ppermute | solution.py:21

commit v7 on v5

--- a/solution.py
+++ b/solution.py
@@ -9,6 +9,8 @@
 
 GROUP = 4
 PAIR = 2
+SIDE = 256
+UNITS = 2
 
 SMEM = pl.BlockSpec(memory_space=pltpu.SMEM)
 ANY = pl.BlockSpec(memory_space=pl.ANY)
@@ -159,11 +161,16 @@
     )(packed)
 
 
-def row_product(notes, slots, edge, row, left, p_ref):
-    picked = [p_ref[piece(edge, notes[s, row]), :] for s in range(slots)]
-    return jnp.dot(
-        jnp.concatenate(left, axis=1), jnp.concatenate(picked, axis=0), preferred_element_type=jnp.float32
-    )
+def row_start(notes, slots, edge, row, left, p_ref, sums):
+    step = SIDE // edge
+    for k in range(slots // step):
+        here = jnp.concatenate(left[k * step // PAIR : (k + 1) * step // PAIR], axis=1)
+        for n, acc in enumerate(sums):
+            picked = [
+                p_ref[piece(edge, notes[s, row]), pl.ds(n * SIDE, SIDE)] for s in range(k * step, (k + 1) * step)
+            ]
+            pltpu.matmul_push_rhs(jnp.concatenate(picked, axis=0), k % 2, n % UNITS)
+            pltpu.matmul_acc_lhs(acc, here, load_staged_rhs=k % 2)
 
 
 def left_pieces(notes, slots, edge, row, starts, held):
@@ -190,6 +197,7 @@
     out_ref, starts, held, p_here, stage, sems, out_sems, *refs = refs
     nrows = notes.shape[1]
     groups = nrows // GROUP
+    across = p_here.shape[1] // SIDE
 
     p_copy = pltpu.make_async_copy(p_ref, p_here, sems.at[0])
     p_copy.start()
@@ -256,20 +264,27 @@
     each(lambda copy: copy.wait())
     p_copy.wait()
 
-    def group(g):
+    def group(g, *accs):
+        sums = [accs[:across], accs[across:]]
         if name != "first":
             total_copy(g).wait()
-        for r in range(GROUP):
-            row = g * GROUP + r
-            here = piece(edge, row)
-            left = left_pieces(notes, slots, edge, row, starts, held)
-            value = row_product(notes, slots, edge, row, left, p_here)
-            if name != "first":
-                value = refs[0][here, :] + value
-            stage[here, :] = value.astype(stage.dtype)
+        for r in range(GROUP + 1):
+            if r < GROUP:
+                row = g * GROUP + r
+                left = left_pieces(notes, slots, edge, row, starts, held)
+                row_start(notes, slots, edge, row, left, p_here, sums[r % 2])
+            if r > 0:
+                here = piece(edge, g * GROUP + r - 1)
+                for n, acc in enumerate(sums[(r - 1) % 2]):
+                    there = pl.ds(n * SIDE, SIDE)
+                    value = pltpu.matmul_pop(acc)
+                    if name != "first":
+                        value = refs[0][here, there] + value
+                    stage[here, there] = value.astype(stage.dtype)
         out_copy(g).start()
 
-    over(group)
+    spaces = [pltpu.ACC(n % UNITS)((edge, SIDE), jnp.float32) for n in range(across)] * 2
+    pl.run_scoped(lambda *accs: over(lambda g: group(g, *accs)), *spaces)
     over(lambda g: out_copy(g).wait())
 
 
@@ -298,7 +313,7 @@
         + [pltpu.VMEM((tall, width), jnp.float32), pltpu.SemaphoreType.DMA((groups,))] * later,
         out_shape=(pltpu.HBM if later else jax.ShapeDtypeStruct)((tall, width), dtype),
         input_output_aliases={4 + len(parts): 0} if late else {},
-        cost_estimate=cost(tall * width * slots * edge, 4 * tall * width),
+        cost_estimate=cost((1 if later else 20) * tall * width * slots * edge, 4 * tall * width),
         compiler_params=params(16),
         name="step_" + name,
     )(
@@ -327,20 +342,21 @@
     always = 11 * unit
     ends = [always + k * unit for k in (1, 2, 3, 4, 5, 6, 8)] + [others]
 
-    lead, p_second = lax.optimization_barrier((leading_pieces(leading, f_blocks, cols, counts), p_matrix))
-    lead = shifted(lead, "col", -1)
+    lead = shifted(leading_pieces(leading, f_blocks, cols, counts), "col", -1)
     notes = jnp.concatenate([cols, jnp.broadcast_to(counts, (slots, nrows))], axis=0)
     packed, extra = packed_pieces(notes, slots, always, f_blocks)
     extra = shifted(extra, "col", -1)
+    p_second, packed = lax.optimization_barrier((p_matrix, packed))
     p_second = shifted(p_second, "row", -1)
     rests = cut_pieces([(nrows + always, nrows + end) for end in ends] + [(leading, nrows)], packed)
     rests, later, unused = rests[: len(ends)], rests[len(ends)], rests[len(ends) + 1 : -1]
     every = packed.shape[0] // edge
+    notes_next = lead[leading * edge :, :nrows].astype(jnp.float32).astype(jnp.int32)
+    packed, notes_next = lax.optimization_barrier((packed, notes_next))
     total = step_product("first", notes, slots, leading, [("all", 0, every)], (packed,), p_matrix)
     later, total = lax.optimization_barrier((later, total))
     later = shifted(later, "col", -1)
 
-    notes_next = lead[leading * edge :, :nrows].astype(jnp.float32).astype(jnp.int32)
     most = jnp.maximum(jnp.sum(others_of(counts)), jnp.sum(others_of(notes_next[slots])))
     distance = 2
     while distance < lax.axis_size("col"):

time: 47.3 us -> 45.7 us (0.966)
  waiting for transfers between devices: 5.54 us -> 4.25 us
  local copies, waits for them, and re-layouts: 0.76 us -> 0.02 us
  Pallas kernels: 22.3 us -> 22.9 us
    ppermute x6, waiting for transfers between devices: 5.54 us -> 4.25 us  [shifted(): return lax.ppermute(block, axis, route)]
    unnamed x10, local copies, waits for them, and re-layouts: 0.76 us -> 0.02 us
  transfers between devices with their start and end apart: 6 -> 6, of which waited for: 2 -> 2; matrix products, arithmetic and copies ran while one was open for 3% -> 3% of each run, Pallas kernels for 34% -> 35%
where the time goes in v7:
time: 45.7 us
  Pallas kernels  22.9 us (50%)
  starting transfers between devices  15.1 us (33%)
  waiting for transfers between devices  4.25 us (9%)
  between operations  2.05 us (4%)
  other arithmetic  1.31 us (3%)
    pallas_call x3, Pallas kernels, step_product(): pl.pallas_call(functools.partial(step_kernel, edge, slots, name, leading,...  16.9 us
    ppermute x6, starting transfers between devices, shifted(): return lax.ppermute(block, axis, route)  15.1 us
    ppermute x6, waiting for transfers between devices, shifted(): return lax.ppermute(block, axis, route)  4.25 us
    pallas_call x1, Pallas kernels, leading_pieces(): pl.pallas_call(functools.partial(leading_kernel, edge), grid_spec=pltpu.P...  2.24 us
    pallas_call x1, Pallas kernels, packed_pieces(): pl.pallas_call(functools.partial(pack_kernel, edge, slots), in_specs=[SME...  2.03 us
    pallas_call x1, Pallas kernels, cut_pieces(): pl.pallas_call(functools.partial(cut_kernel, rows), in_specs=[ANY], out_s...  1.78 us
  transfers between devices with their start and end apart: 6, of which 2 were waited for; matrix products, arithmetic and copies ran while one was open for 3% of the time, Pallas kernels for 35%

profile of v7, /device:TPU:0, one launch (start us, length us, event | category | flops | bytes accessed | tf_op | source)
XLA Modules:
  0.0 45.7 jit_solution(16791936066205772883)
XLA Ops:
  0.0 2.2 %leading_pieces.1 = bf16[1552,128]{1,0:T(8,128)(2,1)S(1)} custom-call(s32[1,32]{1,0:T(1,128)} %bitcast.17, bf16[2048,512]{1,0:T(8,128)(2,1)} %f_ref.3, s32[8,32]{1,0:T(8,128)} %bitcast.15, s32[1,32]{1,0:T(1,128)} %bitcast.18), custom_call_target="tpu_custom_call" | custom-call | bytes 786432 | tf_op jit(solution)/shard_map/leading_pieces/pallas_call | solution.py:66
  2.2 3.9 %collective-permute-start.8 = (bf16[1552,128]{1,0:T(8,128)(2,1)S(1)}, bf16[1552,128]{1,0:T(8,128)(2,1)S(1)}, u32[]{:S(2)}, u32[]{:S(2)}) collective-permute-start(bf16[1552,128]{1,0:T(8,128)(2,1)S(1)} %leading_pieces.1), channel_id=1, source_target_pairs={{1,0},{2,1},{3,2},{0,3},{5,4},{6,5},{7,6},{4,7},{9,8},{10,9},{11,1... | collective-permute-start | bytes 1191944 | tf_op jit(solution)/shard_map/ppermute | solution.py:23
  6.2 0.0 copy-done.9
  6.2 0.0 copy-done.8
  6.2 0.0 copy-done
  6.2 2.0 %pack_live_pieces.1 = (bf16[8256,128]{1,0:T(8,128)(2,1)S(1)}, bf16[2816,128]{1,0:T(8,128)(2,1)S(1)}) custom-call(s32[16,32]{1,0:T(8,128)S(1)} %pad_add_fusion.notes, bf16[2048,512]{1,0:T(8,128)(2,1)S(1)} %copy-done), custom_call_target="tpu_custom_call" | custom-call | bytes 4194304 | tf_op jit(solution)/shard_map/pack_live_pieces/pallas_call | solution.py:118
  8.3 2.8 %collective-permute-start.12 = (bf16[1536,512]{1,0:T(8,128)(2,1)S(1)}, bf16[1536,512]{1,0:T(8,128)(2,1)}, u32[]{:S(2)}, u32[]{:S(2)}) collective-permute-start(bf16[1536,512]{1,0:T(8,128)(2,1)S(1)} %copy-done.1), channel_id=1, source_target_pairs={{4,0},{8,4},{12,8},{16,12},{20,16},{24,20},{28,24},{0,28},{5,1},{9... | collective-permute-start | bytes 4718600 | tf_op jit(solution)/shard_map/ppermute | solution.py:23
  11.1 0.5 %collective-permute-start.11 = (bf16[2816,128]{1,0:T(8,128)(2,1)S(1)}, bf16[2816,128]{1,0:T(8,128)(2,1)S(1)}, u32[]{:S(2)}, u32[]{:S(2)}) collective-permute-start(bf16[2816,128]{1,0:T(8,128)(2,1)S(1)} %get-tuple-element.357), channel_id=1, source_target_pairs={{1,0},{2,1},{3,2},{0,3},{5,4},{6,5},{7,6},{4,7},{9,8},{10,9},{11,1... | collective-permute-start | bytes 2162696 | tf_op jit(solution)/shard_map/ppermute | solution.py:23
  11.6 1.8 %cut_pieces.1 = (bf16[256,128]{1,0:T(8,128)(2,1)}, bf16[512,128]{1,0:T(8,128)(2,1)}, bf16[768,128]{1,0:T(8,128)(2,1)S(1)}, bf16[1024,128]{1,0:T(8,128)(2,1)}, bf...) custom-call(bf16[8256,128]{1,0:T(8,128)(2,1)S(1)} %get-tuple-element, ...), custom_call_target="tpu_custom_call" | custom-call | bytes 5767168 | tf_op jit(solution)/shard_map/cut_pieces/pallas_call | solution.py:152
  13.4 2.4 %collective-permute-done.8.refs_1_ = bf16[1552,128]{1,0:T(8,128)(2,1)S(1)} collective-permute-done((bf16[1552,128]{1,0:T(8,128)(2,1)S(1)}, bf16[1552,128]{1,0:T(8,128)(2,1)S(1)}, u32[]{:S(2)}, u32[]{:S(2)}) %collective-permute-start.8) | collective-permute-done | bytes 397344 | tf_op jit(solution)/shard_map/ppermute | solution.py:23
  15.8 5.9 %step_first.1.refs_13_ = f32[2048,512]{1,0:T(8,128)} custom-call(s32[16,32]{1,0:T(8,128)S(1)} %pad_add_fusion.notes, bf16[8256,128]{1,0:T(8,128)(2,1)S(1)} %get-tuple-element.355.packed_ref.refs_0_, bf16[1536,512]{1,0:T(8,128)(2,1)S(1)} %copy-done.1), custom_call_target="tpu_custom_call" | custom-call | flops 10737418240 | bytes 4194304 | tf_op jit(solution)/shard_map/step_first/pallas_call | solution.py:301
  21.7 3.4 %collective-permute-start.10 = (bf16[512,128]{1,0:T(8,128)(2,1)S(1)}, bf16[512,128]{1,0:T(8,128)(2,1)S(1)}, u32[]{:S(2)}, u32[]{:S(2)}) collective-permute-start(bf16[512,128]{1,0:T(8,128)(2,1)S(1)} %get-tuple-element.356), channel_id=1, source_target_pairs={{1,0},{2,1},{3,2},{0,3},{5,4},{6,5},{7,6},{4,7},{9,8},{10,9},{11,1... | collective-permute-start | bytes 393224 | tf_op jit(solution)/shard_map/ppermute | solution.py:23
  25.2 0.6 %add_reduce_fusion.1 = s32[]{:T(128)} fusion(s32[32,1]{0,1:T(1,128)S(1)} %copy-done.9), kind=kLoop, calls=%fused_computation.12 | loop fusion | flops 575 | bytes 132 | tf_op jit(solution)/shard_map/reduce_sum | solution.py:360
  25.8 0.7 %add_reduce_fusion = s32[]{:T(128)} fusion(s32[16,32]{1,0:T(8,128)S(1)} %convert_convert_fusion.notes), kind=kLoop, calls=%fused_computation.11 | loop fusion | flops 575 | bytes 132 | tf_op jit(solution)/shard_map/reduce_sum | solution.py:360
  27.7 1.9 %collective-permute-start.9 = (s32[]{:T(128)}, s32[]{:T(128)}, u32[]{:S(2)}, u32[]{:S(2)}) collective-permute-start(s32[]{:T(128)} %max.6), channel_id=1, source_target_pairs={{2,0},{3,1},{0,2},{1,3},{6,4},{7,5},{4,6},{5,7},{10,8},{11,9},{8,1... | collective-permute-start | bytes 20 | tf_op jit(solution)/shard_map/ppermute | solution.py:23
  29.6 1.8 %collective-permute-done.9 = s32[]{:T(128)} collective-permute-done((s32[]{:T(128)}, s32[]{:T(128)}, u32[]{:S(2)}, u32[]{:S(2)}) %collective-permute-start.9) | collective-permute-done | bytes 36 | tf_op jit(solution)/shard_map/ppermute | solution.py:23
  32.1 0.0 collective-permute-done.11.refs_3_
  32.1 0.0 collective-permute-done.12.refs_12_
  32.1 8.8 %conditional.1 = (bf16[2048,512]{1,0:T(8,128)(2,1)}, bf16[256,128]{1,0:T(8,128)(2,1)S(1)}, bf16[512,128]{1,0:T(8,128)(2,1)}, bf16[768,128]{1,0:T(8,128)(2,1)}, b...) conditional(s32[]{:T(128)} %clamp.3, (s32[16,32]{1,0:T(8,128)S(1)}, ...), branch_computations={%region_2.3_spmd, %region_3.4_spmd, %region_4.5_spmd, %region_5.6_... | conditional | flops 536870912 | bytes 11141260 | solution.py:370
  32.2 2.5 %collective-permute-start = (bf16[256,128]{1,0:T(8,128)(2,1)}, bf16[256,128]{1,0:T(8,128)(2,1)S(1)}, u32[]{:S(2)}, u32[]{:S(2)}) collective-permute-start(bf16[256,128]{1,0:T(8,128)(2,1)} %get-tuple-element.218), channel_id=1, source_target_pairs={{1,0},{2,1},{3,2},{0,3},{5,4},{6,5},{7,6},{4,7},{9,8},{10,9},{11,1... | collective-permute-start | bytes 196616 | tf_op jit(solution)/shard_map/cond/branch_0_fun/ppermute | solution.py:23
  34.6 6.2 %step_early.8 = bf16[2048,512]{1,0:T(8,128)(2,1)} custom-call(s32[16,32]{1,0:T(8,128)S(1)} %get-tuple-element.213.notes, bf16[1552,128]{1,0:T(8,128)(2,1)} %get-tuple-element.214.refs_0_, bf16[2816,128]{1,0:T(8,128)(2,1)S(1)} %get-tuple-element.215.refs_1_, bf16[1536,512]{1,0:T(8,128)(2,1)} %get-tuple-element.216.refs_2_, f32[2048,512]{1,0:T(8,128)} %get-tuple-element.217.refs_3_), custom_call_target="tpu_custom_call" | custom-call | flops 536870912 | bytes 4194304 | tf_op jit(solution)/shard_map/cond/branch_0_fun/step_early/pallas_call | solution.py:301
  40.9 0.0 collective-permute-done
  40.9 0.0 collective-permute-done.10.refs_2_
  40.9 4.7 %step_late.1 = bf16[2048,512]{1,0:T(8,128)(2,1)} custom-call(s32[16,32]{1,0:T(8,128)S(1)} %convert_convert_fusion.notes, s32[1]{0:T(128)} %bitcast.4.refs_0_, bf16[1552,128]{1,0:T(8,128)(2,1)} %copy-done.2, bf16[512,128]{1,0:T(8,128)(2,1)S(1)} %collective-permute-done.10.refs_2_, ...), custom_call_target="tpu_custom_call", output_to_operand_aliasing={{}: (15, {})} | custom-call | flops 536870912 | bytes 4194304 | tf_op jit(solution)/shard_map/step_late/pallas_call | solution.py:301
  (10 shorter events, 0.0 us)
Async XLA Ops:
  0.0 6.2 %copy-start = (bf16[2048,512]{1,0:T(8,128)(2,1)S(1)}, bf16[2048,512]{1,0:T(8,128)(2,1)}, u32[]{:S(2)}) copy-start(bf16[2048,512]{1,0:T(8,128)(2,1)} %f_ref.3) | copy-start | bytes 6291460
  0.0 6.2 %copy-start.9 = (s32[32,1]{0,1:T(1,128)S(1)}, s32[32,1]{0,1:T(1,128)}, u32[]{:S(2)}) copy-start(s32[32,1]{0,1:T(1,128)} %param.14) | copy-start | bytes 388
  0.0 6.2 %copy-start.8 = (s32[32,8]{0,1:T(8,128)S(1)}, s32[32,8]{0,1:T(8,128)}, u32[]{:S(2)}) copy-start(s32[32,8]{0,1:T(8,128)} %param.13) | copy-start | bytes 3076
  0.0 8.3 %copy-start.1 = (bf16[1536,512]{1,0:T(8,128)(2,1)S(1)}, bf16[1536,512]{1,0:T(8,128)(2,1)}, u32[]{:S(2)}) copy-start(bf16[1536,512]{1,0:T(8,128)(2,1)} %refs_1_.1) | copy-start | bytes 4718596
  2.2 13.6 %collective-permute-start.8 = (bf16[1552,128]{1,0:T(8,128)(2,1)S(1)}, bf16[1552,128]{1,0:T(8,128)(2,1)S(1)}, u32[]{:S(2)}, u32[]{:S(2)}) collective-permute-start(bf16[1552,128]{1,0:T(8,128)(2,1)S(1)} %leading_pieces.1), channel_id=1, source_target_pairs={{1,0},{2,1},{3,2},{0,3},{5,4},{6,5},{7,6},{4,7},{9,8},{10,9},{11,1... | collective-permute-start | bytes 1191944 | tf_op jit(solution)/shard_map/ppermute | solution.py:23
  8.3 23.9 %collective-permute-start.12 = (bf16[1536,512]{1,0:T(8,128)(2,1)S(1)}, bf16[1536,512]{1,0:T(8,128)(2,1)}, u32[]{:S(2)}, u32[]{:S(2)}) collective-permute-start(bf16[1536,512]{1,0:T(8,128)(2,1)S(1)} %copy-done.1), channel_id=1, source_target_pairs={{4,0},{8,4},{12,8},{16,12},{20,16},{24,20},{28,24},{0,28},{5,1},{9... | collective-permute-start | bytes 4718600 | tf_op jit(solution)/shard_map/ppermute | solution.py:23
  11.1 21.0 %collective-permute-start.11 = (bf16[2816,128]{1,0:T(8,128)(2,1)S(1)}, bf16[2816,128]{1,0:T(8,128)(2,1)S(1)}, u32[]{:S(2)}, u32[]{:S(2)}) collective-permute-start(bf16[2816,128]{1,0:T(8,128)(2,1)S(1)} %get-tuple-element.357), channel_id=1, source_target_pairs={{1,0},{2,1},{3,2},{0,3},{5,4},{6,5},{7,6},{4,7},{9,8},{10,9},{11,1... | collective-permute-start | bytes 2162696 | tf_op jit(solution)/shard_map/ppermute | solution.py:23
  15.8 5.9 %copy-start.2 = (bf16[1552,128]{1,0:T(8,128)(2,1)}, bf16[1552,128]{1,0:T(8,128)(2,1)S(1)}, u32[]{:S(2)}) copy-start(bf16[1552,128]{1,0:T(8,128)(2,1)S(1)} %collective-permute-done.8.refs_1_) | copy-start | bytes 1191940
  21.7 19.2 %collective-permute-start.10 = (bf16[512,128]{1,0:T(8,128)(2,1)S(1)}, bf16[512,128]{1,0:T(8,128)(2,1)S(1)}, u32[]{:S(2)}, u32[]{:S(2)}) collective-permute-start(bf16[512,128]{1,0:T(8,128)(2,1)S(1)} %get-tuple-element.356), channel_id=1, source_target_pairs={{1,0},{2,1},{3,2},{0,3},{5,4},{6,5},{7,6},{4,7},{9,8},{10,9},{11,1... | collective-permute-start | bytes 393224 | tf_op jit(solution)/shard_map/ppermute | solution.py:23
  27.7 3.7 %collective-permute-start.9 = (s32[]{:T(128)}, s32[]{:T(128)}, u32[]{:S(2)}, u32[]{:S(2)}) collective-permute-start(s32[]{:T(128)} %max.6), channel_id=1, source_target_pairs={{2,0},{3,1},{0,2},{1,3},{6,4},{7,5},{4,6},{5,7},{10,8},{11,9},{8,1... | collective-permute-start | bytes 20 | tf_op jit(solution)/shard_map/ppermute | solution.py:23
  32.2 8.7 %collective-permute-start = (bf16[256,128]{1,0:T(8,128)(2,1)}, bf16[256,128]{1,0:T(8,128)(2,1)S(1)}, u32[]{:S(2)}, u32[]{:S(2)}) collective-permute-start(bf16[256,128]{1,0:T(8,128)(2,1)} %get-tuple-element.218), channel_id=1, source_target_pairs={{1,0},{2,1},{3,2},{0,3},{5,4},{6,5},{7,6},{4,7},{9,8},{10,9},{11,1... | collective-permute-start | bytes 196616 | tf_op jit(solution)/shard_map/cond/branch_0_fun/ppermute | solution.py:23

commit v8 on v6

--- a/solution.py
+++ b/solution.py
@@ -37,21 +37,33 @@
     return pl.ds(pl.multiple_of(index * edge, edge), count * edge)
 
 
-def others_of(count):
-    return (count + (PAIR - 1)) // PAIR - 1
-
-
-def live_half(value, count, slot, edge):
-    lane = lax.broadcasted_iota(jnp.int32, value.shape, 1)
-    return jnp.where(lane < jnp.where(count > slot + 1, PAIR, 1) * edge, value, jnp.zeros_like(value))
-
-
-def leading_kernel(edge, counts, f_ref, cols_ref, counts_ref, out_ref):
+def beyond(count):
+    more = jnp.maximum(count - PAIR, 0)
+    return more // PAIR, more % PAIR
+
+
+def pieces_of(counts):
+    full, single = beyond(counts)
+    return jnp.sum(full) + (jnp.sum(single) + 1) // PAIR
+
+
+def walk(counts, full_at, single_at, row_done):
+    at, opened = jnp.int32(0), jnp.int32(-1)
+    for r in range(len(counts)):
+        full, single = beyond(counts[r])
+        full_at(r, at)
+        shares = jnp.logical_and(single == 1, opened >= 0)
+        opens = jnp.logical_and(single == 1, opened < 0)
+        single_at(r, jnp.where(shares, opened, at + full), shares)
+        opened = jnp.where(opens, at + full, jnp.where(shares, -1, opened))
+        at = at + full + opens.astype(jnp.int32)
+        row_done(r, at, opened)
+
+
+def leading_kernel(f_ref, cols_ref, counts_ref, out_ref):
     slots, nrows = cols_ref.shape
     tall = f_ref.shape[0]
-    for r in range(tall // edge):
-        here = pl.ds(r * edge, edge)
-        out_ref[here, :] = live_half(f_ref[here, :], counts[0, r], 0, edge)
+    out_ref[pl.ds(0, tall), :] = f_ref[...]
     notes = jnp.concatenate([cols_ref[...], jnp.broadcast_to(counts_ref[...], (slots, nrows))], axis=0)
     out_ref[pl.ds(tall, 2 * slots), pl.ds(0, nrows)] = notes.astype(jnp.float32).astype(out_ref.dtype)
 
@@ -62,22 +74,19 @@
     shape = (rows * edge + 2 * slots, PAIR * edge)
     f_blocks, cols, counts = (in_hbm(x) for x in (f_blocks, cols, counts))
     return pl.pallas_call(
-        functools.partial(leading_kernel, edge),
-        grid_spec=pltpu.PrefetchScalarGridSpec(
-            num_scalar_prefetch=1,
-            grid=(1,),
-            in_specs=[
-                pl.BlockSpec((rows * edge, PAIR * edge), lambda g, c: (0, 0)),
-                pl.BlockSpec(cols.shape, lambda g, c: (0, 0)),
-                pl.BlockSpec(counts.shape, lambda g, c: (0, 0)),
-            ],
-            out_specs=pl.BlockSpec(shape, lambda g, c: (0, 0)),
-        ),
+        leading_kernel,
+        grid=(1,),
+        in_specs=[
+            pl.BlockSpec((rows * edge, PAIR * edge), lambda g: (0, 0)),
+            pl.BlockSpec(cols.shape, lambda g: (0, 0)),
+            pl.BlockSpec(counts.shape, lambda g: (0, 0)),
+        ],
+        out_specs=pl.BlockSpec(shape, lambda g: (0, 0)),
         out_shape=jax.ShapeDtypeStruct(shape, f_blocks.dtype),
         cost_estimate=cost(0, 4 * rows * edge * PAIR * edge),
         compiler_params=params(8),
         name="leading_pieces",
-    )(counts, f_blocks, cols, counts)
+    )(f_blocks, cols, counts)
 
 
 def pack_kernel(edge, slots, notes, f_ref, out_ref, extra_ref, f_here, packed, sems):
@@ -88,17 +97,28 @@
         here = piece(edge, g * GROUP, GROUP)
         fetched.append(pltpu.make_async_copy(f_ref.at[here], f_here.at[here], sems.at[g]))
         fetched[-1].start()
-    at = 0
-    for r in range(nrows):
+    wide = PAIR * edge
+
+    def strip(r, p):
+        return f_here[pl.ds(r * edge, edge), pl.ds(pl.multiple_of(p * wide, wide), wide)]
+
+    def full_at(r, at):
         if r % GROUP == 0:
             fetched[r // GROUP].wait()
-        count = notes[slots, r]
-        for p in range(parts):
-            value = f_here[pl.ds(r * edge, edge), pl.ds(p * PAIR * edge, PAIR * edge)]
-            to = r if p == 0 else nrows + at + (p - 1)
-            packed[piece(edge, to), :] = live_half(value, count, p * PAIR, edge)
-        at = at + others_of(count)
-    packed[pl.ds(nrows * parts * edge, edge), :] = jnp.zeros((edge, PAIR * edge), packed.dtype)
+        packed[pl.ds(r * edge, edge), :] = strip(r, 0)
+        for p in range(1, parts):
+            packed[piece(edge, nrows + at + (p - 1)), :] = strip(r, p)
+
+    def single_at(r, at, shares):
+        @pl.when(shares)
+        def _():
+            value = strip(r, 1 + beyond(notes[slots, r])[0])
+            here = piece(edge, nrows + at)
+            moved = jnp.concatenate([value[:, edge:], value[:, :edge]], axis=1)
+            low = lax.broadcasted_iota(jnp.int32, value.shape, 1) < edge
+            packed[here, :] = jnp.where(low, packed[here, :], moved)
+
+    walk([notes[slots, r] for r in range(nrows)], full_at, single_at, lambda *_: None)
     copies = [
         pltpu.make_async_copy(packed.at[pl.ds(nrows * edge, extra_ref.shape[0])], extra_ref, sems.at[0]),
         pltpu.make_async_copy(packed, out_ref, sems.at[1]),
@@ -112,7 +132,7 @@
 def packed_pieces(notes, slots, always, f_blocks):
     nrows = notes.shape[1]
     edge = f_blocks.shape[0] // nrows
-    shape = ((nrows * slots // PAIR + 1) * edge, PAIR * edge)
+    shape = (nrows * slots // PAIR * edge, PAIR * edge)
     return pl.pallas_call(
         functools.partial(pack_kernel, edge, slots),
         in_specs=[SMEM, ANY],
@@ -159,21 +179,26 @@
     )(packed)
 
 
-def row_product(notes, slots, edge, row, left, p_ref):
-    picked = [p_ref[piece(edge, notes[s, row]), :] for s in range(slots)]
+def row_product(notes, slots, edge, row, starts, singles, held, p_ref):
+    nrows = notes.shape[1]
+    zero = p_ref.shape[0] // edge - 1
+    count = notes[slots, row]
+    full, single = beyond(count)
+    code = singles[row]
+    second = code % 2
+    left = [held[piece(edge, row), :]]
+    picks = [notes[0, row], jnp.where(count > 1, notes[1, row], zero)]
+    for p in range(slots // PAIR - 1):
+        alone = jnp.logical_and(p == full, single == 1)
+        at = jnp.where(p < full, nrows + starts[row] + p, jnp.where(alone, nrows + code // 2, row))
+        left.append(held[piece(edge, at), :])
+        even, odd = notes[PAIR * (p + 1), row], notes[PAIR * (p + 1) + 1, row]
+        picks.append(jnp.where(jnp.logical_or(p < full, jnp.logical_and(alone, second == 0)), even, zero))
+        picks.append(jnp.where(p < full, odd, jnp.where(jnp.logical_and(alone, second == 1), even, zero)))
+    picked = [p_ref[piece(edge, pick), :] for pick in picks]
     return jnp.dot(
         jnp.concatenate(left, axis=1), jnp.concatenate(picked, axis=0), preferred_element_type=jnp.float32
     )
-
-
-def left_pieces(notes, slots, edge, row, starts, held):
-    nrows = notes.shape[1]
-    spare = held.shape[0] // edge - 1
-    live = others_of(notes[slots, row])
-    left = [held[piece(edge, row), :]]
-    for p in range(slots // PAIR - 1):
-        left.append(held[piece(edge, jnp.where(p < live, nrows + starts[row] + p, spare)), :])
-    return left
 
 
 def step_kernel(edge, slots, name, leading, places, notes, *refs):
@@ -187,18 +212,27 @@
         total_ref, *refs = refs
     if name == "late":
         _, *refs = refs
-    out_ref, starts, held, p_here, stage, sems, out_sems, *refs = refs
+    out_ref, starts, singles, opened, held, p_here, stage, sems, out_sems, *refs = refs
     nrows = notes.shape[1]
     groups = nrows // GROUP
 
-    p_copy = pltpu.make_async_copy(p_ref, p_here, sems.at[0])
+    depth = p_ref.shape[0]
+    p_copy = pltpu.make_async_copy(p_ref, p_here.at[pl.ds(0, depth)], sems.at[0])
     p_copy.start()
-
-    at = jnp.int32(0)
-    for r in range(nrows):
+    p_here[pl.ds(depth, edge), :] = jnp.zeros((edge, p_here.shape[1]), p_here.dtype)
+
+    def full_at(r, at):
         starts[r] = at
-        at = at + others_of(notes[slots, r])
-    starts[nrows] = at
+
+    def single_at(r, at, shares):
+        singles[r] = at * 2 + shares.astype(jnp.int32)
+
+    def row_done(r, at, still):
+        starts[r + 1] = at
+        opened[r + 1] = jnp.where(still < 0, at, still)
+
+    opened[0] = jnp.int32(0)
+    walk([notes[slots, r] for r in range(nrows)], full_at, single_at, row_done)
     low, high = 0, groups
     if name != "first":
         room = [count for kind, _, count in places if kind == "second"][0]
@@ -217,7 +251,7 @@
             if name == "late" and kind == "first":
                 needed = low < leading // GROUP
             elif name == "late" and kind == "second":
-                needed = starts[low * GROUP] < first + step
+                needed = opened[low * GROUP] < first + step
             elif not isinstance(kind, str):
                 needed = size[0] == kind
             tall = min(step, count - first) * edge
@@ -251,8 +285,6 @@
 
     if name != "first":
         over(lambda g: total_copy(g).start())
-    if name != "first":
-        held[pl.ds(held.shape[0] - edge, edge), :] = jnp.zeros((edge, held.shape[1]), held.dtype)
     each(lambda copy: copy.wait())
     p_copy.wait()
 
@@ -262,8 +294,7 @@
         for r in range(GROUP):
             row = g * GROUP + r
             here = piece(edge, row)
-            left = left_pieces(notes, slots, edge, row, starts, held)
-            value = row_product(notes, slots, edge, row, left, p_here)
+            value = row_product(notes, slots, edge, row, starts, singles, held, p_here)
             if name != "first":
                 value = refs[0][here, :] + value
             stage[here, :] = value.astype(stage.dtype)
@@ -289,8 +320,10 @@
         out_specs=HBM,
         scratch_shapes=[
             pltpu.SMEM((nrows + 1,), jnp.int32),
-            pltpu.VMEM(((room + later) * edge, PAIR * edge), p_tile.dtype),
-            pltpu.VMEM(p_tile.shape, p_tile.dtype),
+            pltpu.SMEM((nrows,), jnp.int32),
+            pltpu.SMEM((nrows + 1,), jnp.int32),
+            pltpu.VMEM((room * edge, PAIR * edge), p_tile.dtype),
+            pltpu.VMEM((depth + edge, width), p_tile.dtype),
             pltpu.VMEM((tall, width), dtype),
             pltpu.SemaphoreType.DMA((len(parts) + 8,)),
             pltpu.SemaphoreType.DMA((groups,)),
@@ -324,7 +357,7 @@
     leading = (groups - groups // 4) * GROUP
     others = nrows * (slots // PAIR - 1)
     unit = others // 24
-    always = 11 * unit
+    always = 10 * unit
     ends = [always + k * unit for k in (1, 2, 3, 4, 5, 6, 8)] + [others]
 
     lead = shifted(leading_pieces(leading, f_blocks, cols, counts), "col", -1)
@@ -342,7 +375,7 @@
     later, total = lax.optimization_barrier((later, total))
     later = shifted(later, "col", -1)
 
-    most = jnp.maximum(jnp.sum(others_of(counts)), jnp.sum(others_of(notes_next[slots])))
+    most = jnp.maximum(pieces_of(counts), pieces_of(notes_next[slots]))
     distance = 2
     while distance < lax.axis_size("col"):
         most = jnp.maximum(most, shifted(most, "col", -distance))

time: 45.5 us -> 44.9 us (0.987)
  starting transfers between devices: 14.3 us -> 12.9 us
  between operations: 2.03 us -> 3.36 us
    ppermute x6, starting transfers between devices: 14.3 us -> 12.9 us  [shifted(): return lax.ppermute(block, axis, route)]
    pallas_call x1, Pallas kernels: 1.9 us -> 1.19 us  [leading_pieces(): pl.pallas_call(leading_kernel, grid=(1,), in_specs=[pl.BlockSpec((rows *...]
    pallas_call x3, Pallas kernels: 17.7 us -> 18.1 us  [step_product(): pl.pallas_call(functools.partial(step_kernel, edge, slots, name, leading,...]
  transfers between devices with their start and end apart: 6 -> 6, of which waited for: 2 -> 2; matrix products, arithmetic and copies ran while one was open for 3% -> 3% of each run, Pallas kernels for 36% -> 37%
where the time goes in v8:
time: 44.9 us; the launch traced here: 44.8 us
  Pallas kernels  22.7 us (51%)
  starting transfers between devices  12.9 us (29%)
  waiting for transfers between devices  4.26 us (9%)
  between operations  3.36 us (7%)
  other arithmetic  1.42 us (3%)
    pallas_call x3, Pallas kernels, step_product(): pl.pallas_call(functools.partial(step_kernel, edge, slots, name, leading,...  18.1 us
    ppermute x6, starting transfers between devices, shifted(): return lax.ppermute(block, axis, route)  12.9 us
    ppermute x6, waiting for transfers between devices, shifted(): return lax.ppermute(block, axis, route)  4.26 us
    pallas_call x1, Pallas kernels, packed_pieces(): pl.pallas_call(functools.partial(pack_kernel, edge, slots), in_specs=[SME...  2.23 us
    reduce_sum x2, other arithmetic, pieces_of(): return jnp.sum(full) + (jnp.sum(single) + 1) // PAIR  1.41 us
    pallas_call x1, Pallas kernels, leading_pieces(): pl.pallas_call(leading_kernel, grid=(1,), in_specs=[pl.BlockSpec((rows *...  1.19 us
    pallas_call x1, Pallas kernels, cut_pieces(): pl.pallas_call(functools.partial(cut_kernel, rows), in_specs=[ANY], out_s...  1.18 us
  transfers between devices with their start and end apart: 6, of which 2 were waited for; matrix products, arithmetic and copies ran while one was open for 3% of the time, Pallas kernels for 37%

profile of v8, /device:TPU:0, one launch (start us, length us, event | category | flops | bytes accessed | tf_op | source)
XLA Modules:
  0.0 44.8 jit_solution(1260975196149985762)
XLA Ops:
  0.0 1.2 %leading_pieces.1 = bf16[1552,128]{1,0:T(8,128)(2,1)S(1)} custom-call(bf16[2048,512]{1,0:T(8,128)(2,1)} %f_ref.3, s32[8,32]{1,0:T(8,128)} %bitcast.21, s32[1,32]{1,0:T(1,128)} %bitcast.23), custom_call_target="tpu_custom_call" | custom-call | bytes 786432 | tf_op jit(solution)/shard_map/leading_pieces/pallas_call | solution.py:76
  1.2 4.0 %collective-permute-start.8 = (bf16[1552,128]{1,0:T(8,128)(2,1)S(1)}, bf16[1552,128]{1,0:T(8,128)(2,1)S(1)}, u32[]{:S(2)}, u32[]{:S(2)}) collective-permute-start(bf16[1552,128]{1,0:T(8,128)(2,1)S(1)} %leading_pieces.1), channel_id=1, source_target_pairs={{1,0},{2,1},{3,2},{0,3},{5,4},{6,5},{7,6},{4,7},{9,8},{10,9},{11,1... | collective-permute-start | bytes 1191944 | tf_op jit(solution)/shard_map/ppermute | solution.py:21
  5.2 0.0 copy-done.2
  5.2 0.0 copy-done.1
  5.2 0.0 copy-done
  5.2 2.2 %pack_live_pieces.1 = (bf16[8192,128]{1,0:T(8,128)(2,1)S(1)}, bf16[2560,128]{1,0:T(8,128)(2,1)S(1)}) custom-call(s32[16,32]{1,0:T(8,128)S(1)} %pad_add_fusion.notes, bf16[2048,512]{1,0:T(8,128)(2,1)S(1)} %copy-done), custom_call_target="tpu_custom_call" | custom-call | bytes 4194304 | tf_op jit(solution)/shard_map/pack_live_pieces/pallas_call | solution.py:136
  7.4 2.8 %collective-permute-start.12 = (bf16[1536,512]{1,0:T(8,128)(2,1)}, bf16[1536,512]{1,0:T(8,128)(2,1)}, u32[]{:S(2)}, u32[]{:S(2)}) collective-permute-start(bf16[1536,512]{1,0:T(8,128)(2,1)} %refs_1_.1), channel_id=1, source_target_pairs={{4,0},{8,4},{12,8},{16,12},{20,16},{24,20},{28,24},{0,28},{5,1},{9... | collective-permute-start | bytes 4718600 | tf_op jit(solution)/shard_map/ppermute | solution.py:21
  10.2 0.8 %collective-permute-start.11 = (bf16[2560,128]{1,0:T(8,128)(2,1)S(1)}, bf16[2560,128]{1,0:T(8,128)(2,1)S(1)}, u32[]{:S(2)}, u32[]{:S(2)}) collective-permute-start(bf16[2560,128]{1,0:T(8,128)(2,1)S(1)} %get-tuple-element.357), channel_id=1, source_target_pairs={{1,0},{2,1},{3,2},{0,3},{5,4},{6,5},{7,6},{4,7},{9,8},{10,9},{11,1... | collective-permute-start | bytes 1966088 | tf_op jit(solution)/shard_map/ppermute | solution.py:21
  11.0 1.2 %cut_pieces.1 = (bf16[256,128]{1,0:T(8,128)(2,1)}, bf16[512,128]{1,0:T(8,128)(2,1)}, bf16[768,128]{1,0:T(8,128)(2,1)}, bf16[1024,128]{1,0:T(8,128)(2,1)}, bf16[1...) custom-call(bf16[8192,128]{1,0:T(8,128)(2,1)S(1)} %get-tuple-element, ...), custom_call_target="tpu_custom_call" | custom-call | bytes 5898240 | tf_op jit(solution)/shard_map/cut_pieces/pallas_call | solution.py:170
  12.2 2.6 %collective-permute-done.8.refs_1_ = bf16[1552,128]{1,0:T(8,128)(2,1)S(1)} collective-permute-done((bf16[1552,128]{1,0:T(8,128)(2,1)S(1)}, bf16[1552,128]{1,0:T(8,128)(2,1)S(1)}, u32[]{:S(2)}, u32[]{:S(2)}) %collective-permute-start.8) | collective-permute-done | bytes 397344 | tf_op jit(solution)/shard_map/ppermute | solution.py:21
  14.8 6.9 %step_first.1.refs_13_ = f32[2048,512]{1,0:T(8,128)} custom-call(s32[16,32]{1,0:T(8,128)S(1)} %pad_add_fusion.notes, bf16[8192,128]{1,0:T(8,128)(2,1)S(1)} %get-tuple-element.355.packed_ref.refs_0_, bf16[1536,512]{1,0:T(8,128)(2,1)} %refs_1_.1), custom_call_target="tpu_custom_call" | custom-call | flops 10737418240 | bytes 4194304 | tf_op jit(solution)/shard_map/step_first/pallas_call | solution.py:317
  21.6 3.4 %collective-permute-start.10 = (bf16[512,128]{1,0:T(8,128)(2,1)S(1)}, bf16[512,128]{1,0:T(8,128)(2,1)S(1)}, u32[]{:S(2)}, u32[]{:S(2)}) collective-permute-start(bf16[512,128]{1,0:T(8,128)(2,1)S(1)} %get-tuple-element.356), channel_id=1, source_target_pairs={{1,0},{2,1},{3,2},{0,3},{5,4},{6,5},{7,6},{4,7},{9,8},{10,9},{11,1... | collective-permute-start | bytes 393224 | tf_op jit(solution)/shard_map/ppermute | solution.py:21
  25.1 0.7 %fusion.1 = (s32[]{:T(128)}, s32[]{:T(128)}) fusion(s32[32,1]{0,1:T(1,128)S(1)} %copy-done.2), kind=kLoop, calls=%fused_computation.7 | loop fusion | flops 510 | bytes 136 | tf_op jit(solution)/shard_map/reduce_sum | solution.py:47
  27.1 0.7 %fusion.2 = (s32[]{:T(128)}, s32[]{:T(128)}) fusion(s32[16,32]{1,0:T(8,128)S(1)} %convert_convert_fusion.notes), kind=kLoop, calls=%fused_computation.8 | loop fusion | flops 510 | bytes 136 | tf_op jit(solution)/shard_map/reduce_sum | solution.py:47
  29.1 1.9 %collective-permute-start.9 = (s32[]{:T(128)}, s32[]{:T(128)}, u32[]{:S(2)}, u32[]{:S(2)}) collective-permute-start(s32[]{:T(128)} %max.35), channel_id=1, source_target_pairs={{2,0},{3,1},{0,2},{1,3},{6,4},{7,5},{4,6},{5,7},{10,8},{11,9},{8,1... | collective-permute-start | bytes 20 | tf_op jit(solution)/shard_map/ppermute | solution.py:21
  31.0 1.7 %collective-permute-done.9 = s32[]{:T(128)} collective-permute-done((s32[]{:T(128)}, s32[]{:T(128)}, u32[]{:S(2)}, u32[]{:S(2)}) %collective-permute-start.9) | collective-permute-done | bytes 36 | tf_op jit(solution)/shard_map/ppermute | solution.py:21
  33.3 0.0 collective-permute-done.11.refs_3_
  33.3 0.0 collective-permute-done.12.refs_12_
  33.3 6.5 %conditional.1 = (bf16[2048,512]{1,0:T(8,128)(2,1)}, bf16[256,128]{1,0:T(8,128)(2,1)S(1)}, bf16[512,128]{1,0:T(8,128)(2,1)}, bf16[768,128]{1,0:T(8,128)(2,1)}, b...) conditional(s32[]{:T(128)} %clamp.3, (s32[16,32]{1,0:T(8,128)S(1)}, ...), branch_computations={%region_4.5_spmd, %region_5.6_spmd, %region_6.7_spmd, %region_7.8_... | conditional | flops 536870912 | bytes 7995504 | solution.py:388
  33.4 0.1 collective-permute-start.2
  33.4 6.4 %step_early.10 = bf16[2048,512]{1,0:T(8,128)(2,1)} custom-call(s32[16,32]{1,0:T(8,128)S(1)} %get-tuple-element.239.notes, bf16[1552,128]{1,0:T(8,128)(2,1)S(1)} %get-tuple-element.240.refs_0_, bf16[2560,128]{1,0:T(8,128)(2,1)S(1)} %get-tuple-element.241.refs_1_, bf16[1536,512]{1,0:T(8,128)(2,1)} %get-tuple-element.242.refs_2_, ...), custom_call_target="tpu_custom_call" | custom-call | flops 536870912 | bytes 4194304 | tf_op jit(solution)/shard_map/cond/branch_2_fun/step_early/pallas_call | solution.py:317
  39.8 0.0 collective-permute-done.2
  39.9 0.0 collective-permute-done.10.refs_2_
  39.9 4.9 %step_late.1 = bf16[2048,512]{1,0:T(8,128)(2,1)} custom-call(s32[16,32]{1,0:T(8,128)S(1)} %convert_convert_fusion.notes, s32[1]{0:T(128)} %bitcast.6.refs_0_, bf16[1552,128]{1,0:T(8,128)(2,1)S(1)} %collective-permute-done.8.refs_1_, bf16[512,128]{1,0:T(8,128)(2,1)S(1)} %collective-permute-done.10.refs_2_, ...), custom_call_target="tpu_custom_call", output_to_operand_aliasing={{}: (15, {})} | custom-call | flops 536870912 | bytes 4194304 | tf_op jit(solution)/shard_map/step_late/pallas_call | solution.py:317
  (7 shorter events, 0.0 us)
Async XLA Ops:
  0.0 5.2 %copy-start = (bf16[2048,512]{1,0:T(8,128)(2,1)S(1)}, bf16[2048,512]{1,0:T(8,128)(2,1)}, u32[]{:S(2)}) copy-start(bf16[2048,512]{1,0:T(8,128)(2,1)} %f_ref.3) | copy-start | bytes 6291460
  0.0 5.1 %copy-start.2 = (s32[32,1]{0,1:T(1,128)S(1)}, s32[32,1]{0,1:T(1,128)}, u32[]{:S(2)}) copy-start(s32[32,1]{0,1:T(1,128)} %param.14) | copy-start | bytes 388
  0.0 5.2 %copy-start.1 = (s32[32,8]{0,1:T(8,128)S(1)}, s32[32,8]{0,1:T(8,128)}, u32[]{:S(2)}) copy-start(s32[32,8]{0,1:T(8,128)} %param.13) | copy-start | bytes 3076
  1.2 13.6 %collective-permute-start.8 = (bf16[1552,128]{1,0:T(8,128)(2,1)S(1)}, bf16[1552,128]{1,0:T(8,128)(2,1)S(1)}, u32[]{:S(2)}, u32[]{:S(2)}) collective-permute-start(bf16[1552,128]{1,0:T(8,128)(2,1)S(1)} %leading_pieces.1), channel_id=1, source_target_pairs={{1,0},{2,1},{3,2},{0,3},{5,4},{6,5},{7,6},{4,7},{9,8},{10,9},{11,1... | collective-permute-start | bytes 1191944 | tf_op jit(solution)/shard_map/ppermute | solution.py:21
  7.4 25.9 %collective-permute-start.12 = (bf16[1536,512]{1,0:T(8,128)(2,1)}, bf16[1536,512]{1,0:T(8,128)(2,1)}, u32[]{:S(2)}, u32[]{:S(2)}) collective-permute-start(bf16[1536,512]{1,0:T(8,128)(2,1)} %refs_1_.1), channel_id=1, source_target_pairs={{4,0},{8,4},{12,8},{16,12},{20,16},{24,20},{28,24},{0,28},{5,1},{9... | collective-permute-start | bytes 4718600 | tf_op jit(solution)/shard_map/ppermute | solution.py:21
  10.2 23.1 %collective-permute-start.11 = (bf16[2560,128]{1,0:T(8,128)(2,1)S(1)}, bf16[2560,128]{1,0:T(8,128)(2,1)S(1)}, u32[]{:S(2)}, u32[]{:S(2)}) collective-permute-start(bf16[2560,128]{1,0:T(8,128)(2,1)S(1)} %get-tuple-element.357), channel_id=1, source_target_pairs={{1,0},{2,1},{3,2},{0,3},{5,4},{6,5},{7,6},{4,7},{9,8},{10,9},{11,1... | collective-permute-start | bytes 1966088 | tf_op jit(solution)/shard_map/ppermute | solution.py:21
  21.6 18.2 %collective-permute-start.10 = (bf16[512,128]{1,0:T(8,128)(2,1)S(1)}, bf16[512,128]{1,0:T(8,128)(2,1)S(1)}, u32[]{:S(2)}, u32[]{:S(2)}) collective-permute-start(bf16[512,128]{1,0:T(8,128)(2,1)S(1)} %get-tuple-element.356), channel_id=1, source_target_pairs={{1,0},{2,1},{3,2},{0,3},{5,4},{6,5},{7,6},{4,7},{9,8},{10,9},{11,1... | collective-permute-start | bytes 393224 | tf_op jit(solution)/shard_map/ppermute | solution.py:21
  29.1 3.6 %collective-permute-start.9 = (s32[]{:T(128)}, s32[]{:T(128)}, u32[]{:S(2)}, u32[]{:S(2)}) collective-permute-start(s32[]{:T(128)} %max.35), channel_id=1, source_target_pairs={{2,0},{3,1},{0,2},{1,3},{6,4},{7,5},{4,6},{5,7},{10,8},{11,9},{8,1... | collective-permute-start | bytes 20 | tf_op jit(solution)/shard_map/ppermute | solution.py:21
  33.4 6.5 %collective-permute-start.2 = (bf16[768,128]{1,0:T(8,128)(2,1)}, bf16[768,128]{1,0:T(8,128)(2,1)}, u32[]{:S(2)}, u32[]{:S(2)}) collective-permute-start(bf16[768,128]{1,0:T(8,128)(2,1)} %get-tuple-element.246), channel_id=1, source_target_pairs={{1,0},{2,1},{3,2},{0,3},{5,4},{6,5},{7,6},{4,7},{9,8},{10,9},{11,1... | collective-permute-start | bytes 589832 | tf_op jit(solution)/shard_map/cond/branch_2_fun/ppermute | solution.py:21

commit v9 on v8

--- a/solution.py
+++ b/solution.py
@@ -40,11 +40,6 @@
 def beyond(count):
     more = jnp.maximum(count - PAIR, 0)
     return more // PAIR, more % PAIR
-
-
-def pieces_of(counts):
-    full, single = beyond(counts)
-    return jnp.sum(full) + (jnp.sum(single) + 1) // PAIR
 
 
 def walk(counts, full_at, single_at, row_done):
@@ -58,6 +53,71 @@
         opened = jnp.where(opens, at + full, jnp.where(shares, -1, opened))
         at = at + full + opens.astype(jnp.int32)
         row_done(r, at, opened)
+
+
+def write_table(notes, slots, table):
+    nrows = notes.shape[1]
+
+    def full_at(r, at):
+        table[0, r] = at
+
+    def single_at(r, at, shares):
+        table[1, r] = at * 2 + shares.astype(jnp.int32)
+
+    def row_done(r, at, opened):
+        table[0, r + 1] = at
+        table[2, r + 1] = jnp.where(opened < 0, at, opened)
+
+    table[2, 0] = jnp.int32(0)
+    walk([notes[slots, r] for r in range(nrows)], full_at, single_at, row_done)
+
+
+def table_shape(nrows):
+    return jax.ShapeDtypeStruct((3, nrows + 1), jnp.int32)
+
+
+def read_kernel(slots, notes, notes_next, table, most_ref):
+    write_table(notes_next, slots, table)
+    nrows = notes.shape[1]
+    full, single = jnp.int32(0), jnp.int32(0)
+    for r in range(nrows):
+        more, rest = beyond(notes[slots, r])
+        full, single = full + more, single + rest
+    most = jnp.maximum(full + (single + 1) // PAIR, table[0, nrows])
+    most_ref[...] = jnp.full(most_ref.shape, most, jnp.int32)
+
+
+def read_notes(notes, notes_next, slots):
+    return pl.pallas_call(
+        functools.partial(read_kernel, slots),
+        in_specs=[SMEM, SMEM],
+        out_specs=[SMEM, pl.BlockSpec(memory_space=pltpu.VMEM)],
+        out_shape=[table_shape(notes.shape[1]), jax.ShapeDtypeStruct((8, 128), jnp.int32)],
+        cost_estimate=cost(20 << 30, 4096),
+        compiler_params=params(2),
+        name="read_notes",
+    )(notes, notes_next)
+
+
+def pick_kernel(ends, one_ref, other_ref, size):
+    most = jnp.max(jnp.maximum(one_ref[...], other_ref[...]))
+    index = jnp.int32(0)
+    for end in ends[:-1]:
+        index = index + (most > end).astype(jnp.int32)
+    size[0] = index
+
+
+def pick_size(ends, one, other):
+    vector = pl.BlockSpec(memory_space=pltpu.VMEM)
+    return pl.pallas_call(
+        functools.partial(pick_kernel, ends),
+        in_specs=[vector, vector],
+        out_specs=SMEM,
+        out_shape=jax.ShapeDtypeStruct((1,), jnp.int32),
+        cost_estimate=cost(0, 4096),
+        compiler_params=params(2),
+        name="pick_size",
+    )(one, other)
 
 
 def leading_kernel(f_ref, cols_ref, counts_ref, out_ref):
@@ -89,7 +149,7 @@
     )(f_blocks, cols, counts)
 
 
-def pack_kernel(edge, slots, notes, f_ref, out_ref, extra_ref, f_here, packed, sems):
+def pack_kernel(edge, slots, notes, f_ref, out_ref, extra_ref, table, f_here, packed, sems):
     nrows = notes.shape[1]
     parts = slots // PAIR
     fetched = []
@@ -125,6 +185,7 @@
     ]
     for copy in copies:
         copy.start()
+    write_table(notes, slots, table)
     for copy in copies:
         copy.wait()
 
@@ -136,7 +197,7 @@
     return pl.pallas_call(
         functools.partial(pack_kernel, edge, slots),
         in_specs=[SMEM, ANY],
-        out_specs=[ANY, ANY],
+        out_specs=[ANY, ANY, SMEM],
         scratch_shapes=[
             pltpu.VMEM(f_blocks.shape, f_blocks.dtype),
             pltpu.VMEM(shape, f_blocks.dtype),
@@ -145,6 +206,7 @@
         out_shape=[
             jax.ShapeDtypeStruct(shape, f_blocks.dtype),
             jax.ShapeDtypeStruct((always * edge, PAIR * edge), f_blocks.dtype),
+            table_shape(nrows),
         ],
         cost_estimate=cost(0, 4 * f_blocks.size),
         compiler_params=params(16),
@@ -179,18 +241,18 @@
     )(packed)
 
 
-def row_product(notes, slots, edge, row, starts, singles, held, p_ref):
+def row_product(notes, table, slots, edge, row, held, p_ref):
     nrows = notes.shape[1]
     zero = p_ref.shape[0] // edge - 1
     count = notes[slots, row]
     full, single = beyond(count)
-    code = singles[row]
+    code = table[1, row]
     second = code % 2
     left = [held[piece(edge, row), :]]
     picks = [notes[0, row], jnp.where(count > 1, notes[1, row], zero)]
     for p in range(slots // PAIR - 1):
         alone = jnp.logical_and(p == full, single == 1)
-        at = jnp.where(p < full, nrows + starts[row] + p, jnp.where(alone, nrows + code // 2, row))
+        at = jnp.where(p < full, nrows + table[0, row] + p, jnp.where(alone, nrows + code // 2, row))
         left.append(held[piece(edge, at), :])
         even, odd = notes[PAIR * (p + 1), row], notes[PAIR * (p + 1) + 1, row]
         picks.append(jnp.where(jnp.logical_or(p < full, jnp.logical_and(alone, second == 0)), even, zero))
@@ -201,7 +263,7 @@
     )
 
 
-def step_kernel(edge, slots, name, leading, places, notes, *refs):
+def step_kernel(edge, slots, name, leading, places, notes, table, *refs):
     size = None
     if name == "late":
         size, *refs = refs
@@ -212,7 +274,7 @@
         total_ref, *refs = refs
     if name == "late":
         _, *refs = refs
-    out_ref, starts, singles, opened, held, p_here, stage, sems, out_sems, *refs = refs
+    out_ref, held, p_here, stage, sems, out_sems, *refs = refs
     nrows = notes.shape[1]
     groups = nrows // GROUP
 
@@ -221,24 +283,12 @@
     p_copy.start()
     p_here[pl.ds(depth, edge), :] = jnp.zeros((edge, p_here.shape[1]), p_here.dtype)
 
-    def full_at(r, at):
-        starts[r] = at
-
-    def single_at(r, at, shares):
-        singles[r] = at * 2 + shares.astype(jnp.int32)
-
-    def row_done(r, at, still):
-        starts[r + 1] = at
-        opened[r + 1] = jnp.where(still < 0, at, still)
-
-    opened[0] = jnp.int32(0)
-    walk([notes[slots, r] for r in range(nrows)], full_at, single_at, row_done)
     low, high = 0, groups
     if name != "first":
         room = [count for kind, _, count in places if kind == "second"][0]
         done = jnp.int32(0)
         for g in range(leading // GROUP):
-            done = done + (starts[(g + 1) * GROUP] <= room).astype(jnp.int32)
+            done = done + (table[0, (g + 1) * GROUP] <= room).astype(jnp.int32)
         low, high = (0, done) if name == "early" else (done, groups)
 
     copies = []
@@ -251,7 +301,7 @@
             if name == "late" and kind == "first":
                 needed = low < leading // GROUP
             elif name == "late" and kind == "second":
-                needed = opened[low * GROUP] < first + step
+                needed = table[2, low * GROUP] < first + step
             elif not isinstance(kind, str):
                 needed = size[0] == kind
             tall = min(step, count - first) * edge
@@ -294,7 +344,7 @@
         for r in range(GROUP):
             row = g * GROUP + r
             here = piece(edge, row)
-            value = row_product(notes, slots, edge, row, starts, singles, held, p_here)
+            value = row_product(notes, table, slots, edge, row, held, p_here)
             if name != "first":
                 value = refs[0][here, :] + value
             stage[here, :] = value.astype(stage.dtype)
@@ -304,7 +354,7 @@
     over(lambda g: out_copy(g).wait())
 
 
-def step_product(name, notes, slots, leading, places, parts, p_tile, total=None, size=None, out=None):
+def step_product(name, notes, table, slots, leading, places, parts, p_tile, total=None, size=None, out=None):
     nrows = notes.shape[1]
     depth, width = p_tile.shape
     edge = parts[0].shape[1] // PAIR
@@ -316,12 +366,9 @@
     late = name == "late"
     return pl.pallas_call(
         functools.partial(step_kernel, edge, slots, name, leading, places),
-        in_specs=[SMEM] * (1 + late) + [ANY] * len(parts) + [HBM] * (1 + later + late),
+        in_specs=[SMEM] * (2 + late) + [ANY] * len(parts) + [HBM] * (1 + later + late),
         out_specs=HBM,
         scratch_shapes=[
-            pltpu.SMEM((nrows + 1,), jnp.int32),
-            pltpu.SMEM((nrows,), jnp.int32),
-            pltpu.SMEM((nrows + 1,), jnp.int32),
             pltpu.VMEM((room * edge, PAIR * edge), p_tile.dtype),
             pltpu.VMEM((depth + edge, width), p_tile.dtype),
             pltpu.VMEM((tall, width), dtype),
@@ -330,12 +377,13 @@
         ]
         + [pltpu.VMEM((tall, width), jnp.float32), pltpu.SemaphoreType.DMA((groups,))] * later,
         out_shape=pltpu.HBM((tall, width), dtype),
-        input_output_aliases={4 + len(parts): 0} if late else {},
-        cost_estimate=cost((1 if later else 20) * tall * width * slots * edge, 4 * tall * width),
+        input_output_aliases={5 + len(parts): 0} if late else {},
+        cost_estimate=cost(tall * width * slots * edge, 4 * tall * width),
         compiler_params=params(16),
         name="step_" + name,
     )(
         notes,
+        table,
         *([size] if late else []),
         *parts,
         in_hbm(p_tile),
@@ -344,9 +392,9 @@
     )
 
 
-def remainder(k, slots, leading, places, rests, unused, notes, lead, extra, p_second, total):
+def remainder(k, slots, leading, places, rests, unused, notes, table, lead, extra, p_second, total):
     rest = [shifted(part, "col", -1) if k == n else other for n, (part, other) in enumerate(zip(rests, unused))]
-    return step_product("early", notes, slots, leading, places, (lead, extra), p_second, total), rest
+    return step_product("early", notes, table, slots, leading, places, (lead, extra), p_second, total), rest
 
 
 def body(f_blocks, block_cols, block_counts, p_matrix):
@@ -362,32 +410,33 @@
 
     lead = shifted(leading_pieces(leading, f_blocks, cols, counts), "col", -1)
     notes = jnp.concatenate([cols, jnp.broadcast_to(counts, (slots, nrows))], axis=0)
-    packed, extra = packed_pieces(notes, slots, always, f_blocks)
+    packed, extra, table = packed_pieces(notes, slots, always, f_blocks)
     extra = shifted(extra, "col", -1)
     p_second, packed = lax.optimization_barrier((p_matrix, packed))
     p_second = shifted(p_second, "row", -1)
     rests = cut_pieces([(nrows + always, nrows + end) for end in ends] + [(leading, nrows)], packed)
     rests, later, unused = rests[: len(ends)], rests[len(ends)], rests[len(ends) + 1 : -1]
     every = packed.shape[0] // edge
+    total = step_product("first", notes, table, slots, leading, [("all", 0, every)], (packed,), p_matrix)
+    later, total, lead = lax.optimization_barrier((later, total, lead))
+    later = shifted(later, "col", -1)
+
     notes_next = lead[leading * edge :, :nrows].astype(jnp.float32).astype(jnp.int32)
-    packed, notes_next = lax.optimization_barrier((packed, notes_next))
-    total = step_product("first", notes, slots, leading, [("all", 0, every)], (packed,), p_matrix)
-    later, total = lax.optimization_barrier((later, total))
-    later = shifted(later, "col", -1)
-
-    most = jnp.maximum(pieces_of(counts), pieces_of(notes_next[slots]))
+    table_next, most = read_notes(notes, notes_next, slots)
+    other = most
     distance = 2
     while distance < lax.axis_size("col"):
-        most = jnp.maximum(most, shifted(most, "col", -distance))
+        most = jnp.maximum(most, other)
+        other = shifted(most, "col", -distance)
         distance *= 2
-    size = sum((most > end).astype(jnp.int32) for end in ends[:-1])
+    size = pick_size(ends, most, other)
     early = [("first", 0, leading), ("second", nrows, always)]
     late = [early[0], ("later", leading, nrows - leading), early[1]]
     late += [(k, nrows + always, end - always) for k, end in enumerate(ends)]
     branches = [functools.partial(remainder, k, slots, leading, early) for k in range(len(ends))]
-    out, rest = lax.switch(size, branches, rests, unused, notes_next, lead, extra, p_second, total)
+    out, rest = lax.switch(size[0], branches, rests, unused, notes_next, table_next, lead, extra, p_second, total)
     parts = (lead, later, extra, *rest)
-    return step_product("late", notes_next, slots, leading, late, parts, p_second, total, size.reshape(1), out)
+    return step_product("late", notes_next, table_next, slots, leading, late, parts, p_second, total, size, out)
 
 
 def solution(mesh):

time: 44.9 us -> 43.5 us (0.969)
  Pallas kernels: 22.7 us -> 26.2 us
  between operations: 3.36 us -> 0.64 us
  other arithmetic: 1.42 us -> 0.01 us
  waiting for transfers between devices: 4.26 us -> 3.43 us
    pallas_call x0 -> x2, Pallas kernels: none -> 2.54 us  [the longest x1 1.82 us: read_notes(): pl.pallas_call(functools.partial(read_kernel, slots), in_specs=[SMEM, SME...]
    reduce_sum x2 -> x0, other arithmetic: 1.41 us -> none  [pieces_of(): return jnp.sum(full) + (jnp.sum(single) + 1) // PAIR]
    pallas_call x1, Pallas kernels: 2.23 us -> 3.12 us  [packed_pieces(): pl.pallas_call(functools.partial(pack_kernel, edge, slots), in_specs=[SME...]
    ppermute x6, waiting for transfers between devices: 4.26 us -> 3.43 us  [shifted(): return lax.ppermute(block, axis, route)]
  transfers between devices with their start and end apart: 6 -> 6, of which waited for: 2 -> 3; matrix products, arithmetic and copies ran while one was open for 3% -> 0% of each run, Pallas kernels for 37% -> 47%
where the time goes in v9:
time: 43.5 us; the launch traced here: 43.3 us
  Pallas kernels  26.2 us (60%)
  starting transfers between devices  13 us (30%)
  waiting for transfers between devices  3.43 us (8%)
  between operations  0.64 us (1%)
    pallas_call x3, Pallas kernels, step_product(): pl.pallas_call(functools.partial(step_kernel, edge, slots, name, leading,...  17.9 us
    ppermute x6, starting transfers between devices, shifted(): return lax.ppermute(block, axis, route)  13 us
    ppermute x6, waiting for transfers between devices, shifted(): return lax.ppermute(block, axis, route)  3.43 us
    pallas_call x1, Pallas kernels, packed_pieces(): pl.pallas_call(functools.partial(pack_kernel, edge, slots), in_specs=[SME...  3.12 us
    pallas_call x1, Pallas kernels, read_notes(): pl.pallas_call(functools.partial(read_kernel, slots), in_specs=[SMEM, SME...  1.82 us
    pallas_call x1, Pallas kernels, cut_pieces(): pl.pallas_call(functools.partial(cut_kernel, rows), in_specs=[ANY], out_s...  1.51 us
    pallas_call x1, Pallas kernels, leading_pieces(): pl.pallas_call(leading_kernel, grid=(1,), in_specs=[pl.BlockSpec((rows *...  1.19 us
  transfers between devices with their start and end apart: 6, of which 3 were waited for; matrix products, arithmetic and copies ran while one was open for 0% of the time, Pallas kernels for 47%

profile of v9, /device:TPU:0, one launch (start us, length us, event | category | flops | bytes accessed | tf_op | source)
XLA Modules:
  0.0 43.3 jit_solution(11539206959260858765)
XLA Ops:
  0.0 1.2 %leading_pieces.1 = bf16[1552,128]{1,0:T(8,128)(2,1)S(1)} custom-call(bf16[2048,512]{1,0:T(8,128)(2,1)} %f_ref.3, s32[8,32]{1,0:T(8,128)} %bitcast.4, s32[1,32]{1,0:T(1,128)} %bitcast.6), custom_call_target="tpu_custom_call" | custom-call | bytes 786432 | tf_op jit(solution)/shard_map/leading_pieces/pallas_call | solution.py:136
  1.2 4.0 %collective-permute-start.8 = (bf16[1552,128]{1,0:T(8,128)(2,1)S(1)}, bf16[1552,128]{1,0:T(8,128)(2,1)S(1)}, u32[]{:S(2)}, u32[]{:S(2)}) collective-permute-start(bf16[1552,128]{1,0:T(8,128)(2,1)S(1)} %leading_pieces.1), channel_id=1, source_target_pairs={{1,0},{2,1},{3,2},{0,3},{5,4},{6,5},{7,6},{4,7},{9,8},{10,9},{11,1... | collective-permute-start | bytes 1191944 | tf_op jit(solution)/shard_map/ppermute | solution.py:21
  5.2 0.0 copy-done.3
  5.2 0.0 copy-done.2
  5.2 0.0 copy-done
  5.2 3.1 %pack_live_pieces.1 = (bf16[8192,128]{1,0:T(8,128)(2,1)S(1)}, bf16[2560,128]{1,0:T(8,128)(2,1)S(1)}, s32[3,33]{1,0:T(4,128)S(1)}) custom-call(s32[16,32]{1,0:T(8,128)S(1)} %pad_add_fusion.notes, bf16[2048,512]{1,0:T(8,128)(2,1)S(1)} %copy-done), custom_call_target="tpu_custom_call" | custom-call | bytes 4194304 | tf_op jit(solution)/shard_map/pack_live_pieces/pallas_call | solution.py:197
  8.3 0.8 %collective-permute-start.11 = (bf16[2560,128]{1,0:T(8,128)(2,1)S(1)}, bf16[2560,128]{1,0:T(8,128)(2,1)S(1)}, u32[]{:S(2)}, u32[]{:S(2)}) collective-permute-start(bf16[2560,128]{1,0:T(8,128)(2,1)S(1)} %get-tuple-element.385), channel_id=1, source_target_pairs={{1,0},{2,1},{3,2},{0,3},{5,4},{6,5},{7,6},{4,7},{9,8},{10,9},{11,1... | collective-permute-start | bytes 1966088 | tf_op jit(solution)/shard_map/ppermute | solution.py:21
  9.1 2.4 %collective-permute-start.12 = (bf16[1536,512]{1,0:T(8,128)(2,1)S(1)}, bf16[1536,512]{1,0:T(8,128)(2,1)}, u32[]{:S(2)}, u32[]{:S(2)}) collective-permute-start(bf16[1536,512]{1,0:T(8,128)(2,1)S(1)} %copy-done.1), channel_id=1, source_target_pairs={{4,0},{8,4},{12,8},{16,12},{20,16},{24,20},{28,24},{0,28},{5,1},{9... | collective-permute-start | bytes 4718600 | tf_op jit(solution)/shard_map/ppermute | solution.py:21
  11.5 1.5 %cut_pieces.1 = (bf16[256,128]{1,0:T(8,128)(2,1)S(1)}, bf16[512,128]{1,0:T(8,128)(2,1)S(1)}, bf16[768,128]{1,0:T(8,128)(2,1)S(1)}, bf16[1024,128]{1,0:T(8,128)(2...) custom-call(bf16[8192,128]{1,0:T(8,128)(2,1)S(1)} %get-tuple-element, ...), custom_call_target="tpu_custom_call" | custom-call | bytes 5898240 | tf_op jit(solution)/shard_map/cut_pieces/pallas_call | solution.py:232
  13.0 6.9 %step_first.1.refs_13_ = f32[2048,512]{1,0:T(8,128)} custom-call(s32[16,32]{1,0:T(8,128)S(1)} %pad_add_fusion.notes, s32[3,33]{1,0:T(4,128)S(1)} %get-tuple-element.380.table, bf16[8192,128]{1,0:T(8,128)(2,1)S(1)} %get-tuple-element.378.packed_ref.refs_0_, bf16[1536,512]{1,0:T(8,128)(2,1)} %refs_1_.1), custom_call_target="tpu_custom_call" | custom-call | flops 536870912 | bytes 4194304 | tf_op jit(solution)/shard_map/step_first/pallas_call | solution.py:367
  19.9 0.0 collective-permute-done.8.refs_1_
  19.9 1.5 %collective-permute-start.10 = (bf16[512,128]{1,0:T(8,128)(2,1)S(1)}, bf16[512,128]{1,0:T(8,128)(2,1)S(1)}, u32[]{:S(2)}, u32[]{:S(2)}) collective-permute-start(bf16[512,128]{1,0:T(8,128)(2,1)S(1)} %get-tuple-element.384), channel_id=1, source_target_pairs={{1,0},{2,1},{3,2},{0,3},{5,4},{6,5},{7,6},{4,7},{9,8},{10,9},{11,1... | collective-permute-start | bytes 393224 | tf_op jit(solution)/shard_map/ppermute | solution.py:21
  21.4 1.8 %read_notes.1 = (s32[3,33]{1,0:T(4,128)S(1)}, s32[8,128]{1,0:T(8,128)S(1)}) custom-call(s32[16,32]{1,0:T(8,128)S(1)} %pad_add_fusion.notes, s32[16,32]{1,0:T(8,128)S(1)} %convert_convert_fusion.notes_next.notes), custom_call_target="tpu_custom_call" | custom-call | flops 21474836480 | bytes 4096 | tf_op jit(solution)/shard_map/read_notes/pallas_call | solution.py:91
  23.2 1.5 %collective-permute-start.9 = (s32[8,128]{1,0:T(8,128)S(1)}, s32[8,128]{1,0:T(8,128)S(1)}, u32[]{:S(2)}, u32[]{:S(2)}) collective-permute-start(s32[8,128]{1,0:T(8,128)S(1)} %get-tuple-element.383.one_ref), channel_id=1, source_target_pairs={{2,0},{3,1},{0,2},{1,3},{6,4},{7,5},{4,6},{5,7},{10,8},{11,9},{8,1... | collective-permute-start | bytes 12296 | tf_op jit(solution)/shard_map/ppermute | solution.py:21
  24.7 2.1 %collective-permute-done.9.other_ref = s32[8,128]{1,0:T(8,128)S(1)} collective-permute-done((s32[8,128]{1,0:T(8,128)S(1)}, s32[8,128]{1,0:T(8,128)S(1)}, u32[]{:S(2)}, u32[]{:S(2)}) %collective-permute-start.9) | collective-permute-done | bytes 4128 | tf_op jit(solution)/shard_map/ppermute | solution.py:21
  26.9 0.7 %pick_size.1.refs_0_ = s32[1]{0:T(128)} custom-call(s32[8,128]{1,0:T(8,128)S(1)} %get-tuple-element.383.one_ref, s32[8,128]{1,0:T(8,128)S(1)} %collective-permute-done.9.other_ref), custom_call_target="tpu_custom_call" | custom-call | bytes 4096 | tf_op jit(solution)/shard_map/pick_size/pallas_call | solution.py:112
  28.1 0.7 %collective-permute-done.11.refs_3_ = bf16[2560,128]{1,0:T(8,128)(2,1)S(1)} collective-permute-done((bf16[2560,128]{1,0:T(8,128)(2,1)S(1)}, bf16[2560,128]{1,0:T(8,128)(2,1)S(1)}, u32[]{:S(2)}, u32[]{:S(2)}) %collective-permute-start.11) | collective-permute-done | bytes 655392 | tf_op jit(solution)/shard_map/ppermute | solution.py:21
  28.8 0.6 %collective-permute-done.12.refs_12_ = bf16[1536,512]{1,0:T(8,128)(2,1)} collective-permute-done((bf16[1536,512]{1,0:T(8,128)(2,1)S(1)}, bf16[1536,512]{1,0:T(8,128)(2,1)}, u32[]{:S(2)}, u32[]{:S(2)}) %collective-permute-start.12) | collective-permute-done | bytes 1572896 | tf_op jit(solution)/shard_map/ppermute | solution.py:21
  29.4 9.0 %conditional.1 = (bf16[2048,512]{1,0:T(8,128)(2,1)}, bf16[256,128]{1,0:T(8,128)(2,1)S(1)}, bf16[512,128]{1,0:T(8,128)(2,1)}, bf16[768,128]{1,0:T(8,128)(2,1)}, b...) conditional(s32[]{:T(128)} %bitcast.3, ...), branch_computations={%region_0.0_spmd, %region_1.0_spmd, %region_2.0_spmd, %region_3.0_... | conditional | flops 536870912 | bytes 7995504 | solution.py:437
  29.4 2.9 %collective-permute-start.1 = (bf16[512,128]{1,0:T(8,128)(2,1)S(1)}, bf16[512,128]{1,0:T(8,128)(2,1)}, u32[]{:S(2)}, u32[]{:S(2)}) collective-permute-start(bf16[512,128]{1,0:T(8,128)(2,1)S(1)} %get-tuple-element.250), channel_id=1, source_target_pairs={{1,0},{2,1},{3,2},{0,3},{5,4},{6,5},{7,6},{4,7},{9,8},{10,9},{11,1... | collective-permute-start | bytes 393224 | tf_op jit(solution)/shard_map/cond/branch_1_fun/ppermute | solution.py:21
  32.3 6.1 %step_early.9 = bf16[2048,512]{1,0:T(8,128)(2,1)} custom-call(s32[16,32]{1,0:T(8,128)S(1)} %get-tuple-element.243.notes, s32[3,33]{1,0:T(4,128)S(1)} %get-tuple-element.244.table, bf16[1552,128]{1,0:T(8,128)(2,1)S(1)} %get-tuple-element.245.refs_0_, bf16[2560,128]{1,0:T(8,128)(2,1)S(1)} %get-tuple-element.246.refs_1_, ...), custom_call_target="tpu_custom_call" | custom-call | flops 536870912 | bytes 4194304 | tf_op jit(solution)/shard_map/cond/branch_1_fun/step_early/pallas_call | solution.py:367
  38.4 0.0 collective-permute-done.1
  38.5 0.0 collective-permute-done.10.refs_2_
  38.5 4.9 %step_late.1 = bf16[2048,512]{1,0:T(8,128)(2,1)} custom-call(s32[16,32]{1,0:T(8,128)S(1)} %convert_convert_fusion.notes_next.notes, s32[3,33]{1,0:T(4,128)S(1)} %get-tuple-element.382.table, s32[1]{0:T(128)} %pick_size.1.refs_0_, bf16[1552,128]{1,0:T(8,128)(2,1)S(1)} %collective-permute-done.8.refs_1_, ...), custom_call_target="tpu_custom_call", output_to_operand_aliasing={{}: (16, {})} | custom-call | flops 536870912 | bytes 4194304 | tf_op jit(solution)/shard_map/step_late/pallas_call | solution.py:367
  (9 shorter events, 0.0 us)
Async XLA Ops:
  0.0 5.2 %copy-start = (bf16[2048,512]{1,0:T(8,128)(2,1)S(1)}, bf16[2048,512]{1,0:T(8,128)(2,1)}, u32[]{:S(2)}) copy-start(bf16[2048,512]{1,0:T(8,128)(2,1)} %f_ref.3) | copy-start | bytes 6291460
  0.0 5.2 %copy-start.3 = (s32[32,1]{0,1:T(1,128)S(1)}, s32[32,1]{0,1:T(1,128)}, u32[]{:S(2)}) copy-start(s32[32,1]{0,1:T(1,128)} %param.14) | copy-start | bytes 388
  0.0 5.2 %copy-start.2 = (s32[32,8]{0,1:T(8,128)S(1)}, s32[32,8]{0,1:T(8,128)}, u32[]{:S(2)}) copy-start(s32[32,8]{0,1:T(8,128)} %param.13) | copy-start | bytes 3076
  0.0 9.1 %copy-start.1 = (bf16[1536,512]{1,0:T(8,128)(2,1)S(1)}, bf16[1536,512]{1,0:T(8,128)(2,1)}, u32[]{:S(2)}) copy-start(bf16[1536,512]{1,0:T(8,128)(2,1)} %refs_1_.1) | copy-start | bytes 4718596
  1.2 18.7 %collective-permute-start.8 = (bf16[1552,128]{1,0:T(8,128)(2,1)S(1)}, bf16[1552,128]{1,0:T(8,128)(2,1)S(1)}, u32[]{:S(2)}, u32[]{:S(2)}) collective-permute-start(bf16[1552,128]{1,0:T(8,128)(2,1)S(1)} %leading_pieces.1), channel_id=1, source_target_pairs={{1,0},{2,1},{3,2},{0,3},{5,4},{6,5},{7,6},{4,7},{9,8},{10,9},{11,1... | collective-permute-start | bytes 1191944 | tf_op jit(solution)/shard_map/ppermute | solution.py:21
  8.3 20.5 %collective-permute-start.11 = (bf16[2560,128]{1,0:T(8,128)(2,1)S(1)}, bf16[2560,128]{1,0:T(8,128)(2,1)S(1)}, u32[]{:S(2)}, u32[]{:S(2)}) collective-permute-start(bf16[2560,128]{1,0:T(8,128)(2,1)S(1)} %get-tuple-element.385), channel_id=1, source_target_pairs={{1,0},{2,1},{3,2},{0,3},{5,4},{6,5},{7,6},{4,7},{9,8},{10,9},{11,1... | collective-permute-start | bytes 1966088 | tf_op jit(solution)/shard_map/ppermute | solution.py:21
  9.1 20.3 %collective-permute-start.12 = (bf16[1536,512]{1,0:T(8,128)(2,1)S(1)}, bf16[1536,512]{1,0:T(8,128)(2,1)}, u32[]{:S(2)}, u32[]{:S(2)}) collective-permute-start(bf16[1536,512]{1,0:T(8,128)(2,1)S(1)} %copy-done.1), channel_id=1, source_target_pairs={{4,0},{8,4},{12,8},{16,12},{20,16},{24,20},{28,24},{0,28},{5,1},{9... | collective-permute-start | bytes 4718600 | tf_op jit(solution)/shard_map/ppermute | solution.py:21
  19.9 18.6 %collective-permute-start.10 = (bf16[512,128]{1,0:T(8,128)(2,1)S(1)}, bf16[512,128]{1,0:T(8,128)(2,1)S(1)}, u32[]{:S(2)}, u32[]{:S(2)}) collective-permute-start(bf16[512,128]{1,0:T(8,128)(2,1)S(1)} %get-tuple-element.384), channel_id=1, source_target_pairs={{1,0},{2,1},{3,2},{0,3},{5,4},{6,5},{7,6},{4,7},{9,8},{10,9},{11,1... | collective-permute-start | bytes 393224 | tf_op jit(solution)/shard_map/ppermute | solution.py:21
  23.2 3.7 %collective-permute-start.9 = (s32[8,128]{1,0:T(8,128)S(1)}, s32[8,128]{1,0:T(8,128)S(1)}, u32[]{:S(2)}, u32[]{:S(2)}) collective-permute-start(s32[8,128]{1,0:T(8,128)S(1)} %get-tuple-element.383.one_ref), channel_id=1, source_target_pairs={{2,0},{3,1},{0,2},{1,3},{6,4},{7,5},{4,6},{5,7},{10,8},{11,9},{8,1... | collective-permute-start | bytes 12296 | tf_op jit(solution)/shard_map/ppermute | solution.py:21
  29.4 9.0 %collective-permute-start.1 = (bf16[512,128]{1,0:T(8,128)(2,1)S(1)}, bf16[512,128]{1,0:T(8,128)(2,1)}, u32[]{:S(2)}, u32[]{:S(2)}) collective-permute-start(bf16[512,128]{1,0:T(8,128)(2,1)S(1)} %get-tuple-element.250), channel_id=1, source_target_pairs={{1,0},{2,1},{3,2},{0,3},{5,4},{6,5},{7,6},{4,7},{9,8},{10,9},{11,1... | collective-permute-start | bytes 393224 | tf_op jit(solution)/shard_map/cond/branch_1_fun/ppermute | solution.py:21

commit v10 on v9

--- a/solution.py
+++ b/solution.py
@@ -55,35 +55,49 @@
         row_done(r, at, opened)
 
 
-def write_table(notes, slots, table):
+def write_table(notes, slots, zero, table):
     nrows = notes.shape[1]
+    others = slots // PAIR - 1
+    places = {}
 
     def full_at(r, at):
         table[0, r] = at
+        places[r] = at
 
     def single_at(r, at, shares):
-        table[1, r] = at * 2 + shares.astype(jnp.int32)
+        count = notes[slots, r]
+        full, single = beyond(count)
+        table[2 + others, r] = notes[0, r]
+        table[3 + others, r] = jnp.where(count > 1, notes[1, r], zero)
+        for p in range(others):
+            alone = jnp.logical_and(p == full, single == 1)
+            table[2 + p, r] = jnp.where(p < full, nrows + places[r] + p, jnp.where(alone, nrows + at, r))
+            even, odd = notes[PAIR * (p + 1), r], notes[PAIR * (p + 1) + 1, r]
+            first = jnp.logical_or(p < full, jnp.logical_and(alone, jnp.logical_not(shares)))
+            row = 2 + others + PAIR * (p + 1)
+            table[row, r] = jnp.where(first, even, zero)
+            table[row + 1, r] = jnp.where(p < full, odd, jnp.where(jnp.logical_and(alone, shares), even, zero))
 
     def row_done(r, at, opened):
         table[0, r + 1] = at
-        table[2, r + 1] = jnp.where(opened < 0, at, opened)
-
-    table[2, 0] = jnp.int32(0)
+        table[1, r + 1] = jnp.where(opened < 0, at, opened)
+
+    table[1, 0] = jnp.int32(0)
     walk([notes[slots, r] for r in range(nrows)], full_at, single_at, row_done)
 
 
-def table_shape(nrows):
-    return jax.ShapeDtypeStruct((3, nrows + 1), jnp.int32)
-
-
-def read_kernel(slots, notes, notes_next, table, most_ref):
-    write_table(notes_next, slots, table)
-    nrows = notes.shape[1]
-    full, single = jnp.int32(0), jnp.int32(0)
-    for r in range(nrows):
-        more, rest = beyond(notes[slots, r])
-        full, single = full + more, single + rest
-    most = jnp.maximum(full + (single + 1) // PAIR, table[0, nrows])
+def table_shape(nrows, slots):
+    return jax.ShapeDtypeStruct((2 + slots // PAIR - 1 + slots, nrows + 1), jnp.int32)
+
+
+def read_kernel(slots, notes, notes_next, most_ref):
+    most = jnp.int32(0)
+    for tile in (notes, notes_next):
+        full, single = jnp.int32(0), jnp.int32(0)
+        for r in range(tile.shape[1]):
+            more, rest = beyond(tile[slots, r])
+            full, single = full + more, single + rest
+        most = jnp.maximum(most, full + (single + 1) // PAIR)
     most_ref[...] = jnp.full(most_ref.shape, most, jnp.int32)
 
 
@@ -91,12 +105,24 @@
     return pl.pallas_call(
         functools.partial(read_kernel, slots),
         in_specs=[SMEM, SMEM],
-        out_specs=[SMEM, pl.BlockSpec(memory_space=pltpu.VMEM)],
-        out_shape=[table_shape(notes.shape[1]), jax.ShapeDtypeStruct((8, 128), jnp.int32)],
+        out_specs=pl.BlockSpec(memory_space=pltpu.VMEM),
+        out_shape=jax.ShapeDtypeStruct((8, 128), jnp.int32),
         cost_estimate=cost(20 << 30, 4096),
         compiler_params=params(2),
         name="read_notes",
     )(notes, notes_next)
+
+
+def table_of(notes, slots, zero):
+    return pl.pallas_call(
+        lambda notes, table: write_table(notes, slots, zero, table),
+        in_specs=[SMEM],
+        out_specs=SMEM,
+        out_shape=table_shape(notes.shape[1], slots),
+        cost_estimate=cost(0, 4096),
+        compiler_params=params(2),
+        name="make_table",
+    )(notes)
 
 
 def pick_kernel(ends, one_ref, other_ref, size):
@@ -149,7 +175,7 @@
     )(f_blocks, cols, counts)
 
 
-def pack_kernel(edge, slots, notes, f_ref, out_ref, extra_ref, table, f_here, packed, sems):
+def pack_kernel(edge, slots, notes, f_ref, out_ref, extra_ref, f_here, packed, sems):
     nrows = notes.shape[1]
     parts = slots // PAIR
     fetched = []
@@ -185,7 +211,6 @@
     ]
     for copy in copies:
         copy.start()
-    write_table(notes, slots, table)
     for copy in copies:
         copy.wait()
 
@@ -197,7 +222,7 @@
     return pl.pallas_call(
         functools.partial(pack_kernel, edge, slots),
         in_specs=[SMEM, ANY],
-        out_specs=[ANY, ANY, SMEM],
+        out_specs=[ANY, ANY],
         scratch_shapes=[
             pltpu.VMEM(f_blocks.shape, f_blocks.dtype),
             pltpu.VMEM(shape, f_blocks.dtype),
@@ -206,7 +231,6 @@
         out_shape=[
             jax.ShapeDtypeStruct(shape, f_blocks.dtype),
             jax.ShapeDtypeStruct((always * edge, PAIR * edge), f_blocks.dtype),
-            table_shape(nrows),
         ],
         cost_estimate=cost(0, 4 * f_blocks.size),
         compiler_params=params(16),
@@ -214,7 +238,7 @@
     )(notes, f_blocks)
 
 
-def cut_kernel(ranges, packed_ref, *refs):
+def cut_kernel(ranges, slots, zero, notes, packed_ref, table, *refs):
     out_refs, sems = refs[: len(ranges)], refs[-1]
     copies = [
         pltpu.make_async_copy(packed_ref.at[pl.ds(low, high - low)], out_ref, sems.at[k])
@@ -222,48 +246,38 @@
     ]
     for copy in copies:
         copy.start()
+    write_table(notes, slots, zero, table)
     for copy in copies:
         copy.wait()
 
 
-def cut_pieces(ranges, packed):
+def cut_pieces(ranges, notes, slots, zero, packed):
     edge = packed.shape[1] // PAIR
     rows = [(low * edge, high * edge) for low, high in ranges]
     return pl.pallas_call(
-        functools.partial(cut_kernel, rows),
-        in_specs=[ANY],
-        out_specs=[ANY] * (2 * len(rows)),
+        functools.partial(cut_kernel, rows, slots, zero),
+        in_specs=[SMEM, ANY],
+        out_specs=[SMEM] + [ANY] * (2 * len(rows)),
         scratch_shapes=[pltpu.SemaphoreType.DMA((len(rows),))],
-        out_shape=[jax.ShapeDtypeStruct((high - low, packed.shape[1]), packed.dtype) for low, high in rows] * 2,
+        out_shape=[table_shape(notes.shape[1], slots)]
+        + [jax.ShapeDtypeStruct((high - low, packed.shape[1]), packed.dtype) for low, high in rows] * 2,
         cost_estimate=cost(0, 4 * sum(high - low for low, high in rows) * packed.shape[1]),
         compiler_params=params(2),
         name="cut_pieces",
-    )(packed)
-
-
-def row_product(notes, table, slots, edge, row, held, p_ref):
-    nrows = notes.shape[1]
-    zero = p_ref.shape[0] // edge - 1
-    count = notes[slots, row]
-    full, single = beyond(count)
-    code = table[1, row]
-    second = code % 2
+    )(notes, packed)
+
+
+def row_product(table, slots, edge, row, held, p_ref):
+    others = slots // PAIR - 1
     left = [held[piece(edge, row), :]]
-    picks = [notes[0, row], jnp.where(count > 1, notes[1, row], zero)]
-    for p in range(slots // PAIR - 1):
-        alone = jnp.logical_and(p == full, single == 1)
-        at = jnp.where(p < full, nrows + table[0, row] + p, jnp.where(alone, nrows + code // 2, row))
-        left.append(held[piece(edge, at), :])
-        even, odd = notes[PAIR * (p + 1), row], notes[PAIR * (p + 1) + 1, row]
-        picks.append(jnp.where(jnp.logical_or(p < full, jnp.logical_and(alone, second == 0)), even, zero))
-        picks.append(jnp.where(p < full, odd, jnp.where(jnp.logical_and(alone, second == 1), even, zero)))
-    picked = [p_ref[piece(edge, pick), :] for pick in picks]
+    left += [held[piece(edge, table[2 + p, row]), :] for p in range(others)]
+    picked = [p_ref[piece(edge, table[2 + others + s, row]), :] for s in range(slots)]
     return jnp.dot(
         jnp.concatenate(left, axis=1), jnp.concatenate(picked, axis=0), preferred_element_type=jnp.float32
     )
 
 
-def step_kernel(edge, slots, name, leading, places, notes, table, *refs):
+def step_kernel(edge, slots, name, leading, places, table, *refs):
     size = None
     if name == "late":
         size, *refs = refs
@@ -275,7 +289,7 @@
     if name == "late":
         _, *refs = refs
     out_ref, held, p_here, stage, sems, out_sems, *refs = refs
-    nrows = notes.shape[1]
+    nrows = table.shape[1] - 1
     groups = nrows // GROUP
 
     depth = p_ref.shape[0]
@@ -301,7 +315,7 @@
             if name == "late" and kind == "first":
                 needed = low < leading // GROUP
             elif name == "late" and kind == "second":
-                needed = table[2, low * GROUP] < first + step
+                needed = table[1, low * GROUP] < first + step
             elif not isinstance(kind, str):
                 needed = size[0] == kind
             tall = min(step, count - first) * edge
@@ -344,7 +358,7 @@
         for r in range(GROUP):
             row = g * GROUP + r
             here = piece(edge, row)
-            value = row_product(notes, table, slots, edge, row, held, p_here)
+            value = row_product(table, slots, edge, row, held, p_here)
             if name != "first":
                 value = refs[0][here, :] + value
             stage[here, :] = value.astype(stage.dtype)
@@ -354,8 +368,8 @@
     over(lambda g: out_copy(g).wait())
 
 
-def step_product(name, notes, table, slots, leading, places, parts, p_tile, total=None, size=None, out=None):
-    nrows = notes.shape[1]
+def step_product(name, table, slots, leading, places, parts, p_tile, total=None, size=None, out=None):
+    nrows = table.shape[1] - 1
     depth, width = p_tile.shape
     edge = parts[0].shape[1] // PAIR
     groups = nrows // GROUP
@@ -366,7 +380,7 @@
     late = name == "late"
     return pl.pallas_call(
         functools.partial(step_kernel, edge, slots, name, leading, places),
-        in_specs=[SMEM] * (2 + late) + [ANY] * len(parts) + [HBM] * (1 + later + late),
+        in_specs=[SMEM] * (1 + late) + [ANY] * len(parts) + [HBM] * (1 + later + late),
         out_specs=HBM,
         scratch_shapes=[
             pltpu.VMEM((room * edge, PAIR * edge), p_tile.dtype),
@@ -377,12 +391,11 @@
         ]
         + [pltpu.VMEM((tall, width), jnp.float32), pltpu.SemaphoreType.DMA((groups,))] * later,
         out_shape=pltpu.HBM((tall, width), dtype),
-        input_output_aliases={5 + len(parts): 0} if late else {},
+        input_output_aliases={4 + len(parts): 0} if late else {},
         cost_estimate=cost(tall * width * slots * edge, 4 * tall * width),
         compiler_params=params(16),
         name="step_" + name,
     )(
-        notes,
         table,
         *([size] if late else []),
         *parts,
@@ -392,9 +405,9 @@
     )
 
 
-def remainder(k, slots, leading, places, rests, unused, notes, table, lead, extra, p_second, total):
+def remainder(k, slots, leading, places, rests, unused, table, lead, extra, p_second, total):
     rest = [shifted(part, "col", -1) if k == n else other for n, (part, other) in enumerate(zip(rests, unused))]
-    return step_product("early", notes, table, slots, leading, places, (lead, extra), p_second, total), rest
+    return step_product("early", table, slots, leading, places, (lead, extra), p_second, total), rest
 
 
 def body(f_blocks, block_cols, block_counts, p_matrix):
@@ -410,19 +423,23 @@
 
     lead = shifted(leading_pieces(leading, f_blocks, cols, counts), "col", -1)
     notes = jnp.concatenate([cols, jnp.broadcast_to(counts, (slots, nrows))], axis=0)
-    packed, extra, table = packed_pieces(notes, slots, always, f_blocks)
+    packed, extra = packed_pieces(notes, slots, always, f_blocks)
     extra = shifted(extra, "col", -1)
     p_second, packed = lax.optimization_barrier((p_matrix, packed))
     p_second = shifted(p_second, "row", -1)
-    rests = cut_pieces([(nrows + always, nrows + end) for end in ends] + [(leading, nrows)], packed)
+    zero = p_matrix.shape[0] // edge
+    ranges = [(nrows + always, nrows + end) for end in ends] + [(leading, nrows)]
+    table, *rests = cut_pieces(ranges, notes, slots, zero, packed)
     rests, later, unused = rests[: len(ends)], rests[len(ends)], rests[len(ends) + 1 : -1]
     every = packed.shape[0] // edge
-    total = step_product("first", notes, table, slots, leading, [("all", 0, every)], (packed,), p_matrix)
+    total = step_product("first", table, slots, leading, [("all", 0, every)], (packed,), p_matrix)
     later, total, lead = lax.optimization_barrier((later, total, lead))
     later = shifted(later, "col", -1)
 
     notes_next = lead[leading * edge :, :nrows].astype(jnp.float32).astype(jnp.int32)
-    table_next, most = read_notes(notes, notes_next, slots)
+    most = read_notes(notes, notes_next, slots)
+    notes_next, most = lax.optimization_barrier((notes_next, most))
+    table_next = table_of(notes_next, slots, zero)
     other = most
     distance = 2
     while distance < lax.axis_size("col"):
@@ -434,9 +451,9 @@
     late = [early[0], ("later", leading, nrows - leading), early[1]]
     late += [(k, nrows + always, end - always) for k, end in enumerate(ends)]
     branches = [functools.partial(remainder, k, slots, leading, early) for k in range(len(ends))]
-    out, rest = lax.switch(size[0], branches, rests, unused, notes_next, table_next, lead, extra, p_second, total)
+    out, rest = lax.switch(size[0], branches, rests, unused, table_next, lead, extra, p_second, total)
     parts = (lead, later, extra, *rest)
-    return step_product("late", notes_next, table_next, slots, leading, late, parts, p_second, total, size, out)
+    return step_product("late", table_next, slots, leading, late, parts, p_second, total, size, out)
 
 
 def solution(mesh):

time: 43.5 us -> 43.7 us (level)
  waiting for transfers between devices: 3.43 us -> 0.02 us
  Pallas kernels: 26.2 us -> 29.3 us
    pallas_call x1 -> x2, Pallas kernels: 1.51 us -> 6.18 us  [the longest x1 3.87 us: cut_pieces(): pl.pallas_call(functools.partial(cut_kernel, rows, slots, zero), in_specs...]
    ppermute x6, waiting for transfers between devices: 3.43 us -> 0.02 us  [shifted(): return lax.ppermute(block, axis, route)]
    pallas_call x1, Pallas kernels: 3.12 us -> 2.3 us  [packed_pieces(): pl.pallas_call(functools.partial(pack_kernel, edge, slots), in_specs=[SME...]
    pallas_call x1, Pallas kernels: 1.82 us -> 1.04 us  [read_notes(): pl.pallas_call(functools.partial(read_kernel, slots), in_specs=[SMEM, SME...]
  transfers between devices with their start and end apart: 6 -> 6, of which waited for: 3 -> 0; matrix products, arithmetic and copies ran while one was open for 0% -> 0% of each run, Pallas kernels for 47% -> 53%
where the time goes in v10:
time: 43.7 us; the launch traced here: 43.4 us
  Pallas kernels  29.3 us (67%)
  starting transfers between devices  13.2 us (30%)
  between operations  0.75 us (2%)
    pallas_call x3, Pallas kernels, step_product(): pl.pallas_call(functools.partial(step_kernel, edge, slots, name, leading,...  17.9 us
    ppermute x6, starting transfers between devices, shifted(): return lax.ppermute(block, axis, route)  13.2 us
    pallas_call x1, Pallas kernels, cut_pieces(): pl.pallas_call(functools.partial(cut_kernel, rows, slots, zero), in_specs...  3.87 us
    pallas_call x1, Pallas kernels, table_of(): pl.pallas_call(lambda notes, table: write_table(notes, slots, zero, table...  2.31 us
    pallas_call x1, Pallas kernels, packed_pieces(): pl.pallas_call(functools.partial(pack_kernel, edge, slots), in_specs=[SME...  2.3 us
    pallas_call x1, Pallas kernels, leading_pieces(): pl.pallas_call(leading_kernel, grid=(1,), in_specs=[pl.BlockSpec((rows *...  1.19 us
    pallas_call x1, Pallas kernels, read_notes(): pl.pallas_call(functools.partial(read_kernel, slots), in_specs=[SMEM, SME...  1.04 us
  transfers between devices with their start and end apart: 6, of which 0 were waited for; matrix products, arithmetic and copies ran while one was open for 0% of the time, Pallas kernels for 53%

profile of v10, /device:TPU:0, one launch (start us, length us, event | category | flops | bytes accessed | tf_op | source)
XLA Modules:
  0.0 43.4 jit_solution(2583444089580845178)
XLA Ops:
  0.0 1.2 %leading_pieces.1 = bf16[1552,128]{1,0:T(8,128)(2,1)S(1)} custom-call(bf16[2048,512]{1,0:T(8,128)(2,1)} %f_ref.3, s32[8,32]{1,0:T(8,128)} %bitcast.4, s32[1,32]{1,0:T(1,128)} %bitcast.6), custom_call_target="tpu_custom_call" | custom-call | bytes 786432 | tf_op jit(solution)/shard_map/leading_pieces/pallas_call | solution.py:162
  1.2 4.0 %collective-permute-start.8 = (bf16[1552,128]{1,0:T(8,128)(2,1)S(1)}, bf16[1552,128]{1,0:T(8,128)(2,1)S(1)}, u32[]{:S(2)}, u32[]{:S(2)}) collective-permute-start(bf16[1552,128]{1,0:T(8,128)(2,1)S(1)} %leading_pieces.1), channel_id=1, source_target_pairs={{1,0},{2,1},{3,2},{0,3},{5,4},{6,5},{7,6},{4,7},{9,8},{10,9},{11,1... | collective-permute-start | bytes 1191944 | tf_op jit(solution)/shard_map/ppermute | solution.py:21
  5.2 0.0 copy-done.3
  5.2 0.0 copy-done.2
  5.2 2.3 %pack_live_pieces.1 = (bf16[8192,128]{1,0:T(8,128)(2,1)S(1)}, bf16[2560,128]{1,0:T(8,128)(2,1)S(1)}) custom-call(s32[16,32]{1,0:T(8,128)S(1)} %pad_add_fusion.notes, bf16[2048,512]{1,0:T(8,128)(2,1)S(1)} %copy-done), custom_call_target="tpu_custom_call" | custom-call | bytes 4194304 | tf_op jit(solution)/shard_map/pack_live_pieces/pallas_call | solution.py:222
  7.5 0.4 collective-permute-start.11
  7.9 2.7 %collective-permute-start.12 = (bf16[1536,512]{1,0:T(8,128)(2,1)S(1)}, bf16[1536,512]{1,0:T(8,128)(2,1)}, u32[]{:S(2)}, u32[]{:S(2)}) collective-permute-start(bf16[1536,512]{1,0:T(8,128)(2,1)S(1)} %copy-done.1), channel_id=1, source_target_pairs={{4,0},{8,4},{12,8},{16,12},{20,16},{24,20},{28,24},{0,28},{5,1},{9... | collective-permute-start | bytes 4718600 | tf_op jit(solution)/shard_map/ppermute | solution.py:21
  10.7 3.9 %cut_pieces.1 = (s32[13,33]{1,0:T(8,128)S(1)}, bf16[256,128]{1,0:T(8,128)(2,1)S(1)}, bf16[512,128]{1,0:T(8,128)(2,1)S(1)}, bf16[768,128]{1,0:T(8,128)(2,1)S(1)},...) custom-call(s32[16,32]{1,0:T(8,128)S(1)} %pad_add_fusion.notes, ...), custom_call_target="tpu_custom_call" | custom-call | bytes 5898240 | tf_op jit(solution)/shard_map/cut_pieces/pallas_call | solution.py:257
  14.5 6.8 %step_first.1.refs_13_ = f32[2048,512]{1,0:T(8,128)} custom-call(s32[13,33]{1,0:T(8,128)S(1)} %get-tuple-element.356.table, bf16[8192,128]{1,0:T(8,128)(2,1)S(1)} %get-tuple-element.354.packed_ref.refs_0_, bf16[1536,512]{1,0:T(8,128)(2,1)} %refs_1_.1), custom_call_target="tpu_custom_call" | custom-call | flops 536870912 | bytes 4194304 | tf_op jit(solution)/shard_map/step_first/pallas_call | solution.py:381
  21.4 0.0 collective-permute-done.8.refs_1_
  21.4 1.3 %collective-permute-start.10 = (bf16[512,128]{1,0:T(8,128)(2,1)S(1)}, bf16[512,128]{1,0:T(8,128)(2,1)S(1)}, u32[]{:S(2)}, u32[]{:S(2)}) collective-permute-start(bf16[512,128]{1,0:T(8,128)(2,1)S(1)} %get-tuple-element.360), channel_id=1, source_target_pairs={{1,0},{2,1},{3,2},{0,3},{5,4},{6,5},{7,6},{4,7},{9,8},{10,9},{11,1... | collective-permute-start | bytes 393224 | tf_op jit(solution)/shard_map/ppermute | solution.py:21
  22.7 1.0 %read_notes.1.one_ref = s32[8,128]{1,0:T(8,128)S(1)} custom-call(s32[16,32]{1,0:T(8,128)S(1)} %pad_add_fusion.notes, s32[16,32]{1,0:T(8,128)S(1)} %convert_convert_fusion.notes_next.notes), custom_call_target="tpu_custom_call" | custom-call | flops 21474836480 | bytes 4096 | tf_op jit(solution)/shard_map/read_notes/pallas_call | solution.py:105
  23.8 1.6 %collective-permute-start.9 = (s32[8,128]{1,0:T(8,128)S(1)}, s32[8,128]{1,0:T(8,128)S(1)}, u32[]{:S(2)}, u32[]{:S(2)}) collective-permute-start(s32[8,128]{1,0:T(8,128)S(1)} %read_notes.1.one_ref), channel_id=1, source_target_pairs={{2,0},{3,1},{0,2},{1,3},{6,4},{7,5},{4,6},{5,7},{10,8},{11,9},{8,1... | collective-permute-start | bytes 12296 | tf_op jit(solution)/shard_map/ppermute | solution.py:21
  25.4 2.3 %make_table.1.table = s32[13,33]{1,0:T(8,128)S(1)} custom-call(s32[16,32]{1,0:T(8,128)S(1)} %convert_convert_fusion.notes_next.notes), custom_call_target="tpu_custom_call" | custom-call | bytes 4096 | tf_op jit(solution)/shard_map/make_table/pallas_call | solution.py:117
  27.7 0.0 collective-permute-done.9.other_ref
  27.7 0.7 %pick_size.1.refs_0_ = s32[1]{0:T(128)} custom-call(s32[8,128]{1,0:T(8,128)S(1)} %read_notes.1.one_ref, s32[8,128]{1,0:T(8,128)S(1)} %collective-permute-done.9.other_ref), custom_call_target="tpu_custom_call" | custom-call | bytes 4096 | tf_op jit(solution)/shard_map/pick_size/pallas_call | solution.py:138
  29.0 0.0 collective-permute-done.11.refs_3_
  29.1 0.0 collective-permute-done.12.refs_12_
  29.1 9.3 %conditional.1 = (bf16[2048,512]{1,0:T(8,128)(2,1)}, bf16[256,128]{1,0:T(8,128)(2,1)S(1)}, bf16[512,128]{1,0:T(8,128)(2,1)}, bf16[768,128]{1,0:T(8,128)(2,1)}, b...) conditional(s32[]{:T(128)} %bitcast.3, ...), branch_computations={%region_0.0_spmd, %region_1.0_spmd, %region_2.0_spmd, %region_3.0_... | conditional | flops 536870912 | bytes 7995504 | solution.py:454
  29.1 3.2 %collective-permute-start.3 = (bf16[1024,128]{1,0:T(8,128)(2,1)S(1)}, bf16[1024,128]{1,0:T(8,128)(2,1)}, u32[]{:S(2)}, u32[]{:S(2)}) collective-permute-start(bf16[1024,128]{1,0:T(8,128)(2,1)S(1)} %get-tuple-element.260), channel_id=1, source_target_pairs={{1,0},{2,1},{3,2},{0,3},{5,4},{6,5},{7,6},{4,7},{9,8},{10,9},{11,1... | collective-permute-start | bytes 786440 | tf_op jit(solution)/shard_map/cond/branch_3_fun/ppermute | solution.py:21
  32.3 6.1 %step_early.11 = bf16[2048,512]{1,0:T(8,128)(2,1)} custom-call(s32[13,33]{1,0:T(8,128)S(1)} %get-tuple-element.252.table, bf16[1552,128]{1,0:T(8,128)(2,1)S(1)} %get-tuple-element.253.refs_0_, bf16[2560,128]{1,0:T(8,128)(2,1)S(1)} %get-tuple-element.254.refs_1_, bf16[1536,512]{1,0:T(8,128)(2,1)} %get-tuple-element.255.refs_2_, ...), custom_call_target="tpu_custom_call" | custom-call | flops 536870912 | bytes 4194304 | tf_op jit(solution)/shard_map/cond/branch_3_fun/step_early/pallas_call | solution.py:381
  38.4 0.0 collective-permute-done.3
  38.4 0.0 collective-permute-done.10.refs_2_
  38.4 5.0 %step_late.1 = bf16[2048,512]{1,0:T(8,128)(2,1)} custom-call(s32[13,33]{1,0:T(8,128)S(1)} %make_table.1.table, s32[1]{0:T(128)} %pick_size.1.refs_0_, bf16[1552,128]{1,0:T(8,128)(2,1)S(1)} %collective-permute-done.8.refs_1_, bf16[512,128]{1,0:T(8,128)(2,1)S(1)} %collective-permute-done.10.refs_2_, ...), custom_call_target="tpu_custom_call", output_to_operand_aliasing={{}: (15, {})} | custom-call | flops 536870912 | bytes 4194304 | tf_op jit(solution)/shard_map/step_late/pallas_call | solution.py:381
  (10 shorter events, 0.0 us)
Async XLA Ops:
  0.0 5.2 %copy-start = (bf16[2048,512]{1,0:T(8,128)(2,1)S(1)}, bf16[2048,512]{1,0:T(8,128)(2,1)}, u32[]{:S(2)}) copy-start(bf16[2048,512]{1,0:T(8,128)(2,1)} %f_ref.3) | copy-start | bytes 6291460
  0.0 5.2 %copy-start.3 = (s32[32,1]{0,1:T(1,128)S(1)}, s32[32,1]{0,1:T(1,128)}, u32[]{:S(2)}) copy-start(s32[32,1]{0,1:T(1,128)} %param.14) | copy-start | bytes 388
  0.0 5.2 %copy-start.2 = (s32[32,8]{0,1:T(8,128)S(1)}, s32[32,8]{0,1:T(8,128)}, u32[]{:S(2)}) copy-start(s32[32,8]{0,1:T(8,128)} %param.13) | copy-start | bytes 3076
  0.0 7.9 %copy-start.1 = (bf16[1536,512]{1,0:T(8,128)(2,1)S(1)}, bf16[1536,512]{1,0:T(8,128)(2,1)}, u32[]{:S(2)}) copy-start(bf16[1536,512]{1,0:T(8,128)(2,1)} %refs_1_.1) | copy-start | bytes 4718596
  1.2 20.2 %collective-permute-start.8 = (bf16[1552,128]{1,0:T(8,128)(2,1)S(1)}, bf16[1552,128]{1,0:T(8,128)(2,1)S(1)}, u32[]{:S(2)}, u32[]{:S(2)}) collective-permute-start(bf16[1552,128]{1,0:T(8,128)(2,1)S(1)} %leading_pieces.1), channel_id=1, source_target_pairs={{1,0},{2,1},{3,2},{0,3},{5,4},{6,5},{7,6},{4,7},{9,8},{10,9},{11,1... | collective-permute-start | bytes 1191944 | tf_op jit(solution)/shard_map/ppermute | solution.py:21
  7.5 21.6 %collective-permute-start.11 = (bf16[2560,128]{1,0:T(8,128)(2,1)S(1)}, bf16[2560,128]{1,0:T(8,128)(2,1)S(1)}, u32[]{:S(2)}, u32[]{:S(2)}) collective-permute-start(bf16[2560,128]{1,0:T(8,128)(2,1)S(1)} %get-tuple-element.361), channel_id=1, source_target_pairs={{1,0},{2,1},{3,2},{0,3},{5,4},{6,5},{7,6},{4,7},{9,8},{10,9},{11,1... | collective-permute-start | bytes 1966088 | tf_op jit(solution)/shard_map/ppermute | solution.py:21
  7.9 21.1 %collective-permute-start.12 = (bf16[1536,512]{1,0:T(8,128)(2,1)S(1)}, bf16[1536,512]{1,0:T(8,128)(2,1)}, u32[]{:S(2)}, u32[]{:S(2)}) collective-permute-start(bf16[1536,512]{1,0:T(8,128)(2,1)S(1)} %copy-done.1), channel_id=1, source_target_pairs={{4,0},{8,4},{12,8},{16,12},{20,16},{24,20},{28,24},{0,28},{5,1},{9... | collective-permute-start | bytes 4718600 | tf_op jit(solution)/shard_map/ppermute | solution.py:21
  21.4 17.0 %collective-permute-start.10 = (bf16[512,128]{1,0:T(8,128)(2,1)S(1)}, bf16[512,128]{1,0:T(8,128)(2,1)S(1)}, u32[]{:S(2)}, u32[]{:S(2)}) collective-permute-start(bf16[512,128]{1,0:T(8,128)(2,1)S(1)} %get-tuple-element.360), channel_id=1, source_target_pairs={{1,0},{2,1},{3,2},{0,3},{5,4},{6,5},{7,6},{4,7},{9,8},{10,9},{11,1... | collective-permute-start | bytes 393224 | tf_op jit(solution)/shard_map/ppermute | solution.py:21
  23.8 3.9 %collective-permute-start.9 = (s32[8,128]{1,0:T(8,128)S(1)}, s32[8,128]{1,0:T(8,128)S(1)}, u32[]{:S(2)}, u32[]{:S(2)}) collective-permute-start(s32[8,128]{1,0:T(8,128)S(1)} %read_notes.1.one_ref), channel_id=1, source_target_pairs={{2,0},{3,1},{0,2},{1,3},{6,4},{7,5},{4,6},{5,7},{10,8},{11,9},{8,1... | collective-permute-start | bytes 12296 | tf_op jit(solution)/shard_map/ppermute | solution.py:21
  29.1 9.3 %collective-permute-start.3 = (bf16[1024,128]{1,0:T(8,128)(2,1)S(1)}, bf16[1024,128]{1,0:T(8,128)(2,1)}, u32[]{:S(2)}, u32[]{:S(2)}) collective-permute-start(bf16[1024,128]{1,0:T(8,128)(2,1)S(1)} %get-tuple-element.260), channel_id=1, source_target_pairs={{1,0},{2,1},{3,2},{0,3},{5,4},{6,5},{7,6},{4,7},{9,8},{10,9},{11,1... | collective-permute-start | bytes 786440 | tf_op jit(solution)/shard_map/cond/branch_3_fun/ppermute | solution.py:21

commit v11 on v10

--- a/solution.py
+++ b/solution.py
@@ -9,6 +9,8 @@
 
 GROUP = 4
 PAIR = 2
+SPLIT = 8
+BATCH = 8
 
 SMEM = pl.BlockSpec(memory_space=pltpu.SMEM)
 ANY = pl.BlockSpec(memory_space=pl.ANY)
@@ -293,8 +295,11 @@
     groups = nrows // GROUP
 
     depth = p_ref.shape[0]
-    p_copy = pltpu.make_async_copy(p_ref, p_here.at[pl.ds(0, depth)], sems.at[0])
-    p_copy.start()
+    p_copies = []
+    for k in range(SPLIT):
+        here = pl.ds(k * (depth // SPLIT), depth // SPLIT)
+        p_copies.append(pltpu.make_async_copy(p_ref.at[here], p_here.at[here], sems.at[k]))
+        p_copies[-1].start()
     p_here[pl.ds(depth, edge), :] = jnp.zeros((edge, p_here.shape[1]), p_here.dtype)
 
     low, high = 0, groups
@@ -307,21 +312,18 @@
 
     copies = []
     for (kind, at, count), part in zip(places, part_refs):
-        step = count
-        if name == "late" and kind == "second":
-            step = -(-count // 4)
-        for first in range(0, count, step):
+        for first in range(0, count, BATCH):
             needed = None
             if name == "late" and kind == "first":
                 needed = low < leading // GROUP
             elif name == "late" and kind == "second":
-                needed = table[1, low * GROUP] < first + step
+                needed = table[1, low * GROUP] < first + BATCH
             elif not isinstance(kind, str):
                 needed = size[0] == kind
-            tall = min(step, count - first) * edge
+            tall = min(BATCH, count - first) * edge
             source = part.at[pl.ds(first * edge, tall)]
             target = held.at[pl.ds((at + first) * edge, tall)]
-            copies.append((needed, pltpu.make_async_copy(source, target, sems.at[1 + len(copies)])))
+            copies.append((needed, pltpu.make_async_copy(source, target, sems.at[SPLIT + len(copies)])))
 
     def each(act):
         for needed, copy in copies:
@@ -336,9 +338,9 @@
         here = piece(edge, g * GROUP, GROUP)
         return pltpu.make_async_copy(total_ref.at[here], refs[0].at[here], refs[1].at[g])
 
-    def out_copy(g):
-        here = piece(edge, g * GROUP, GROUP)
-        return pltpu.make_async_copy(stage.at[here], out_ref.at[here], out_sems.at[g])
+    def out_copy(row):
+        here = piece(edge, row)
+        return pltpu.make_async_copy(stage.at[here], out_ref.at[here], out_sems.at[row])
 
     def over(act):
         def step(g, carry):
@@ -350,7 +352,8 @@
     if name != "first":
         over(lambda g: total_copy(g).start())
     each(lambda copy: copy.wait())
-    p_copy.wait()
+    for copy in p_copies:
+        copy.wait()
 
     def group(g):
         if name != "first":
@@ -362,10 +365,15 @@
             if name != "first":
                 value = refs[0][here, :] + value
             stage[here, :] = value.astype(stage.dtype)
-        out_copy(g).start()
+            out_copy(row).start()
 
     over(group)
-    over(lambda g: out_copy(g).wait())
+
+    def settle(g):
+        for r in range(GROUP):
+            out_copy(g * GROUP + r).wait()
+
+    over(settle)
 
 
 def step_product(name, table, slots, leading, places, parts, p_tile, total=None, size=None, out=None):
@@ -386,8 +394,8 @@
             pltpu.VMEM((room * edge, PAIR * edge), p_tile.dtype),
             pltpu.VMEM((depth + edge, width), p_tile.dtype),
             pltpu.VMEM((tall, width), dtype),
-            pltpu.SemaphoreType.DMA((len(parts) + 8,)),
-            pltpu.SemaphoreType.DMA((groups,)),
+            pltpu.SemaphoreType.DMA((SPLIT + sum(-(-count // BATCH) for _, _, count in places),)),
+            pltpu.SemaphoreType.DMA((nrows,)),
         ]
         + [pltpu.VMEM((tall, width), jnp.float32), pltpu.SemaphoreType.DMA((groups,))] * later,
         out_shape=pltpu.HBM((tall, width), dtype),

time: 43.7 us -> 45.2 us (1.034)
  Pallas kernels: 29.3 us -> 32.7 us
  starting transfers between devices: 13.2 us -> 11.7 us
    pallas_call x3, Pallas kernels: 17.9 us -> 21.3 us  [step_product(): pl.pallas_call(functools.partial(step_kernel, edge, slots, name, leading,...]
    ppermute x6, starting transfers between devices: 13.2 us -> 11.7 us  [shifted(): return lax.ppermute(block, axis, route)]
  transfers between devices with their start and end apart: 6 -> 6, of which waited for: 0 -> 0; matrix products, arithmetic and copies ran while one was open for 0% -> 0% of each run, Pallas kernels for 53% -> 56%
where the time goes in v11:
time: 45.2 us
  Pallas kernels  32.7 us (72%)
  starting transfers between devices  11.7 us (26%)
  between operations  0.75 us (2%)
    pallas_call x3, Pallas kernels, step_product(): pl.pallas_call(functools.partial(step_kernel, edge, slots, name, leading,...  21.3 us
    ppermute x6, starting transfers between devices, shifted(): return lax.ppermute(block, axis, route)  11.7 us
    pallas_call x1, Pallas kernels, cut_pieces(): pl.pallas_call(functools.partial(cut_kernel, rows, slots, zero), in_specs...  3.87 us
    pallas_call x1, Pallas kernels, table_of(): pl.pallas_call(lambda notes, table: write_table(notes, slots, zero, table...  2.31 us
    pallas_call x1, Pallas kernels, packed_pieces(): pl.pallas_call(functools.partial(pack_kernel, edge, slots), in_specs=[SME...  2.29 us
    pallas_call x1, Pallas kernels, leading_pieces(): pl.pallas_call(leading_kernel, grid=(1,), in_specs=[pl.BlockSpec((rows *...  1.19 us
    pallas_call x1, Pallas kernels, read_notes(): pl.pallas_call(functools.partial(read_kernel, slots), in_specs=[SMEM, SME...  1.04 us
  transfers between devices with their start and end apart: 6, of which 0 were waited for; matrix products, arithmetic and copies ran while one was open for 0% of the time, Pallas kernels for 56%

profile of v11, /device:TPU:0, one launch (start us, length us, event | category | flops | bytes accessed | tf_op | source)
XLA Modules:
  0.0 45.2 jit_solution(11817767459207727300)
XLA Ops:
  0.0 1.2 %leading_pieces.1 = bf16[1552,128]{1,0:T(8,128)(2,1)S(1)} custom-call(bf16[2048,512]{1,0:T(8,128)(2,1)} %f_ref.3, s32[8,32]{1,0:T(8,128)} %bitcast.4, s32[1,32]{1,0:T(1,128)} %bitcast.6), custom_call_target="tpu_custom_call" | custom-call | bytes 786432 | tf_op jit(solution)/shard_map/leading_pieces/pallas_call | solution.py:164
  1.2 4.0 %collective-permute-start.8 = (bf16[1552,128]{1,0:T(8,128)(2,1)S(1)}, bf16[1552,128]{1,0:T(8,128)(2,1)S(1)}, u32[]{:S(2)}, u32[]{:S(2)}) collective-permute-start(bf16[1552,128]{1,0:T(8,128)(2,1)S(1)} %leading_pieces.1), channel_id=1, source_target_pairs={{1,0},{2,1},{3,2},{0,3},{5,4},{6,5},{7,6},{4,7},{9,8},{10,9},{11,1... | collective-permute-start | bytes 1191944 | tf_op jit(solution)/shard_map/ppermute | solution.py:23
  5.2 0.0 copy-done.3
  5.2 0.0 copy-done.2
  5.2 2.3 %pack_live_pieces.1 = (bf16[8192,128]{1,0:T(8,128)(2,1)S(1)}, bf16[2560,128]{1,0:T(8,128)(2,1)S(1)}) custom-call(s32[16,32]{1,0:T(8,128)S(1)} %pad_add_fusion.notes, bf16[2048,512]{1,0:T(8,128)(2,1)S(1)} %copy-done), custom_call_target="tpu_custom_call" | custom-call | bytes 4194304 | tf_op jit(solution)/shard_map/pack_live_pieces/pallas_call | solution.py:224
  7.5 0.6 %collective-permute-start.11 = (bf16[2560,128]{1,0:T(8,128)(2,1)S(1)}, bf16[2560,128]{1,0:T(8,128)(2,1)S(1)}, u32[]{:S(2)}, u32[]{:S(2)}) collective-permute-start(bf16[2560,128]{1,0:T(8,128)(2,1)S(1)} %get-tuple-element.361), channel_id=1, source_target_pairs={{1,0},{2,1},{3,2},{0,3},{5,4},{6,5},{7,6},{4,7},{9,8},{10,9},{11,1... | collective-permute-start | bytes 1966088 | tf_op jit(solution)/shard_map/ppermute | solution.py:23
  8.1 2.8 %collective-permute-start.12 = (bf16[1536,512]{1,0:T(8,128)(2,1)S(1)}, bf16[1536,512]{1,0:T(8,128)(2,1)}, u32[]{:S(2)}, u32[]{:S(2)}) collective-permute-start(bf16[1536,512]{1,0:T(8,128)(2,1)S(1)} %copy-done.1), channel_id=1, source_target_pairs={{4,0},{8,4},{12,8},{16,12},{20,16},{24,20},{28,24},{0,28},{5,1},{9... | collective-permute-start | bytes 4718600 | tf_op jit(solution)/shard_map/ppermute | solution.py:23
  10.9 3.9 %cut_pieces.1 = (s32[13,33]{1,0:T(8,128)S(1)}, bf16[256,128]{1,0:T(8,128)(2,1)S(1)}, bf16[512,128]{1,0:T(8,128)(2,1)S(1)}, bf16[768,128]{1,0:T(8,128)(2,1)S(1)},...) custom-call(s32[16,32]{1,0:T(8,128)S(1)} %pad_add_fusion.notes, ...), custom_call_target="tpu_custom_call" | custom-call | bytes 5898240 | tf_op jit(solution)/shard_map/cut_pieces/pallas_call | solution.py:259
  14.8 8.4 %step_first.1.refs_13_ = f32[2048,512]{1,0:T(8,128)} custom-call(s32[13,33]{1,0:T(8,128)S(1)} %get-tuple-element.356.table, bf16[8192,128]{1,0:T(8,128)(2,1)S(1)} %get-tuple-element.354.packed_ref.refs_0_, bf16[1536,512]{1,0:T(8,128)(2,1)} %refs_1_.1), custom_call_target="tpu_custom_call" | custom-call | flops 536870912 | bytes 4194304 | tf_op jit(solution)/shard_map/step_first/pallas_call | solution.py:389
  23.2 0.0 collective-permute-done.8.refs_1_
  23.2 1.1 %collective-permute-start.10 = (bf16[512,128]{1,0:T(8,128)(2,1)S(1)}, bf16[512,128]{1,0:T(8,128)(2,1)S(1)}, u32[]{:S(2)}, u32[]{:S(2)}) collective-permute-start(bf16[512,128]{1,0:T(8,128)(2,1)S(1)} %get-tuple-element.360), channel_id=1, source_target_pairs={{1,0},{2,1},{3,2},{0,3},{5,4},{6,5},{7,6},{4,7},{9,8},{10,9},{11,1... | collective-permute-start | bytes 393224 | tf_op jit(solution)/shard_map/ppermute | solution.py:23
  24.3 1.0 %read_notes.1.one_ref = s32[8,128]{1,0:T(8,128)S(1)} custom-call(s32[16,32]{1,0:T(8,128)S(1)} %pad_add_fusion.notes, s32[16,32]{1,0:T(8,128)S(1)} %convert_convert_fusion.notes_next.notes), custom_call_target="tpu_custom_call" | custom-call | flops 21474836480 | bytes 4096 | tf_op jit(solution)/shard_map/read_notes/pallas_call | solution.py:107
  25.3 1.6 %collective-permute-start.9 = (s32[8,128]{1,0:T(8,128)S(1)}, s32[8,128]{1,0:T(8,128)S(1)}, u32[]{:S(2)}, u32[]{:S(2)}) collective-permute-start(s32[8,128]{1,0:T(8,128)S(1)} %read_notes.1.one_ref), channel_id=1, source_target_pairs={{2,0},{3,1},{0,2},{1,3},{6,4},{7,5},{4,6},{5,7},{10,8},{11,9},{8,1... | collective-permute-start | bytes 12296 | tf_op jit(solution)/shard_map/ppermute | solution.py:23
  26.9 2.3 %make_table.1.table = s32[13,33]{1,0:T(8,128)S(1)} custom-call(s32[16,32]{1,0:T(8,128)S(1)} %convert_convert_fusion.notes_next.notes), custom_call_target="tpu_custom_call" | custom-call | bytes 4096 | tf_op jit(solution)/shard_map/make_table/pallas_call | solution.py:119
  29.2 0.0 collective-permute-done.9.other_ref
  29.2 0.7 %pick_size.1.refs_0_ = s32[1]{0:T(128)} custom-call(s32[8,128]{1,0:T(8,128)S(1)} %read_notes.1.one_ref, s32[8,128]{1,0:T(8,128)S(1)} %collective-permute-done.9.other_ref), custom_call_target="tpu_custom_call" | custom-call | bytes 4096 | tf_op jit(solution)/shard_map/pick_size/pallas_call | solution.py:140
  30.6 0.0 collective-permute-done.11.refs_3_
  30.6 0.0 collective-permute-done.12.refs_12_
  30.6 8.3 %conditional.1 = (bf16[2048,512]{1,0:T(8,128)(2,1)}, bf16[256,128]{1,0:T(8,128)(2,1)S(1)}, bf16[512,128]{1,0:T(8,128)(2,1)}, bf16[768,128]{1,0:T(8,128)(2,1)}, b...) conditional(s32[]{:T(128)} %bitcast.3, ...), branch_computations={%region_0.0_spmd, %region_1.0_spmd, %region_2.0_spmd, %region_3.0_... | conditional | flops 536870912 | bytes 7995504 | solution.py:462
  30.7 1.6 %collective-permute-start.4 = (bf16[1280,128]{1,0:T(8,128)(2,1)S(1)}, bf16[1280,128]{1,0:T(8,128)(2,1)}, u32[]{:S(2)}, u32[]{:S(2)}) collective-permute-start(bf16[1280,128]{1,0:T(8,128)(2,1)S(1)} %get-tuple-element.274), channel_id=1, source_target_pairs={{1,0},{2,1},{3,2},{0,3},{5,4},{6,5},{7,6},{4,7},{9,8},{10,9},{11,1... | collective-permute-start | bytes 983048 | tf_op jit(solution)/shard_map/cond/branch_4_fun/ppermute | solution.py:23
  32.3 6.6 %step_early.12 = bf16[2048,512]{1,0:T(8,128)(2,1)} custom-call(s32[13,33]{1,0:T(8,128)S(1)} %get-tuple-element.265.table, bf16[1552,128]{1,0:T(8,128)(2,1)S(1)} %get-tuple-element.266.refs_0_, bf16[2560,128]{1,0:T(8,128)(2,1)S(1)} %get-tuple-element.267.refs_1_, bf16[1536,512]{1,0:T(8,128)(2,1)} %get-tuple-element.268.refs_2_, ...), custom_call_target="tpu_custom_call" | custom-call | flops 536870912 | bytes 4194304 | tf_op jit(solution)/shard_map/cond/branch_4_fun/step_early/pallas_call | solution.py:389
  38.9 0.0 collective-permute-done.4
  39.0 0.0 collective-permute-done.10.refs_2_
  39.0 6.2 %step_late.1 = bf16[2048,512]{1,0:T(8,128)(2,1)} custom-call(s32[13,33]{1,0:T(8,128)S(1)} %make_table.1.table, s32[1]{0:T(128)} %pick_size.1.refs_0_, bf16[1552,128]{1,0:T(8,128)(2,1)S(1)} %collective-permute-done.8.refs_1_, bf16[512,128]{1,0:T(8,128)(2,1)S(1)} %collective-permute-done.10.refs_2_, ...), custom_call_target="tpu_custom_call", output_to_operand_aliasing={{}: (15, {})} | custom-call | flops 536870912 | bytes 4194304 | tf_op jit(solution)/shard_map/step_late/pallas_call | solution.py:389
  (10 shorter events, 0.0 us)
Async XLA Ops:
  0.0 5.2 %copy-start = (bf16[2048,512]{1,0:T(8,128)(2,1)S(1)}, bf16[2048,512]{1,0:T(8,128)(2,1)}, u32[]{:S(2)}) copy-start(bf16[2048,512]{1,0:T(8,128)(2,1)} %f_ref.3) | copy-start | bytes 6291460
  0.0 5.2 %copy-start.3 = (s32[32,1]{0,1:T(1,128)S(1)}, s32[32,1]{0,1:T(1,128)}, u32[]{:S(2)}) copy-start(s32[32,1]{0,1:T(1,128)} %param.14) | copy-start | bytes 388
  0.0 5.2 %copy-start.2 = (s32[32,8]{0,1:T(8,128)S(1)}, s32[32,8]{0,1:T(8,128)}, u32[]{:S(2)}) copy-start(s32[32,8]{0,1:T(8,128)} %param.13) | copy-start | bytes 3076
  0.0 8.1 %copy-start.1 = (bf16[1536,512]{1,0:T(8,128)(2,1)S(1)}, bf16[1536,512]{1,0:T(8,128)(2,1)}, u32[]{:S(2)}) copy-start(bf16[1536,512]{1,0:T(8,128)(2,1)} %refs_1_.1) | copy-start | bytes 4718596
  1.2 22.0 %collective-permute-start.8 = (bf16[1552,128]{1,0:T(8,128)(2,1)S(1)}, bf16[1552,128]{1,0:T(8,128)(2,1)S(1)}, u32[]{:S(2)}, u32[]{:S(2)}) collective-permute-start(bf16[1552,128]{1,0:T(8,128)(2,1)S(1)} %leading_pieces.1), channel_id=1, source_target_pairs={{1,0},{2,1},{3,2},{0,3},{5,4},{6,5},{7,6},{4,7},{9,8},{10,9},{11,1... | collective-permute-start | bytes 1191944 | tf_op jit(solution)/shard_map/ppermute | solution.py:23
  7.5 23.1 %collective-permute-start.11 = (bf16[2560,128]{1,0:T(8,128)(2,1)S(1)}, bf16[2560,128]{1,0:T(8,128)(2,1)S(1)}, u32[]{:S(2)}, u32[]{:S(2)}) collective-permute-start(bf16[2560,128]{1,0:T(8,128)(2,1)S(1)} %get-tuple-element.361), channel_id=1, source_target_pairs={{1,0},{2,1},{3,2},{0,3},{5,4},{6,5},{7,6},{4,7},{9,8},{10,9},{11,1... | collective-permute-start | bytes 1966088 | tf_op jit(solution)/shard_map/ppermute | solution.py:23
  8.1 22.6 %collective-permute-start.12 = (bf16[1536,512]{1,0:T(8,128)(2,1)S(1)}, bf16[1536,512]{1,0:T(8,128)(2,1)}, u32[]{:S(2)}, u32[]{:S(2)}) collective-permute-start(bf16[1536,512]{1,0:T(8,128)(2,1)S(1)} %copy-done.1), channel_id=1, source_target_pairs={{4,0},{8,4},{12,8},{16,12},{20,16},{24,20},{28,24},{0,28},{5,1},{9... | collective-permute-start | bytes 4718600 | tf_op jit(solution)/shard_map/ppermute | solution.py:23
  23.2 15.8 %collective-permute-start.10 = (bf16[512,128]{1,0:T(8,128)(2,1)S(1)}, bf16[512,128]{1,0:T(8,128)(2,1)S(1)}, u32[]{:S(2)}, u32[]{:S(2)}) collective-permute-start(bf16[512,128]{1,0:T(8,128)(2,1)S(1)} %get-tuple-element.360), channel_id=1, source_target_pairs={{1,0},{2,1},{3,2},{0,3},{5,4},{6,5},{7,6},{4,7},{9,8},{10,9},{11,1... | collective-permute-start | bytes 393224 | tf_op jit(solution)/shard_map/ppermute | solution.py:23
  25.3 3.9 %collective-permute-start.9 = (s32[8,128]{1,0:T(8,128)S(1)}, s32[8,128]{1,0:T(8,128)S(1)}, u32[]{:S(2)}, u32[]{:S(2)}) collective-permute-start(s32[8,128]{1,0:T(8,128)S(1)} %read_notes.1.one_ref), channel_id=1, source_target_pairs={{2,0},{3,1},{0,2},{1,3},{6,4},{7,5},{4,6},{5,7},{10,8},{11,9},{8,1... | collective-permute-start | bytes 12296 | tf_op jit(solution)/shard_map/ppermute | solution.py:23
  30.7 8.3 %collective-permute-start.4 = (bf16[1280,128]{1,0:T(8,128)(2,1)S(1)}, bf16[1280,128]{1,0:T(8,128)(2,1)}, u32[]{:S(2)}, u32[]{:S(2)}) collective-permute-start(bf16[1280,128]{1,0:T(8,128)(2,1)S(1)} %get-tuple-element.274), channel_id=1, source_target_pairs={{1,0},{2,1},{3,2},{0,3},{5,4},{6,5},{7,6},{4,7},{9,8},{10,9},{11,1... | collective-permute-start | bytes 983048 | tf_op jit(solution)/shard_map/cond/branch_4_fun/ppermute | solution.py:23

commit v12 on v9

--- a/solution.py
+++ b/solution.py
@@ -333,19 +333,19 @@
 
         lax.fori_loop(low, high, step, 0)
 
+    each(lambda copy: copy.wait())
+    p_copy.wait()
     if name != "first":
         over(lambda g: total_copy(g).start())
-    each(lambda copy: copy.wait())
-    p_copy.wait()
 
     def group(g):
-        if name != "first":
-            total_copy(g).wait()
         for r in range(GROUP):
             row = g * GROUP + r
             here = piece(edge, row)
             value = row_product(notes, table, slots, edge, row, held, p_here)
             if name != "first":
+                if r == 0:
+                    total_copy(g).wait()
                 value = refs[0][here, :] + value
             stage[here, :] = value.astype(stage.dtype)
         out_copy(g).start()

time: 43.5 us -> 45.9 us (1.055)
  Pallas kernels: 26.2 us -> 28.7 us
    pallas_call x3, Pallas kernels: 17.9 us -> 20.3 us  [step_product(): pl.pallas_call(functools.partial(step_kernel, edge, slots, name, leading,...]
where the time goes in v12:
time: 45.9 us; the launch traced here: 45.8 us
  Pallas kernels  28.7 us (63%)
  starting transfers between devices  13 us (28%)
  waiting for transfers between devices  3.44 us (7%)
  between operations  0.64 us (1%)
    pallas_call x3, Pallas kernels, step_product(): pl.pallas_call(functools.partial(step_kernel, edge, slots, name, leading,...  20.3 us
    ppermute x6, starting transfers between devices, shifted(): return lax.ppermute(block, axis, route)  13 us
    ppermute x6, waiting for transfers between devices, shifted(): return lax.ppermute(block, axis, route)  3.44 us
    pallas_call x1, Pallas kernels, packed_pieces(): pl.pallas_call(functools.partial(pack_kernel, edge, slots), in_specs=[SME...  3.13 us
    pallas_call x1, Pallas kernels, read_notes(): pl.pallas_call(functools.partial(read_kernel, slots), in_specs=[SMEM, SME...  1.82 us
    pallas_call x1, Pallas kernels, cut_pieces(): pl.pallas_call(functools.partial(cut_kernel, rows), in_specs=[ANY], out_s...  1.51 us
    pallas_call x1, Pallas kernels, leading_pieces(): pl.pallas_call(leading_kernel, grid=(1,), in_specs=[pl.BlockSpec((rows *...  1.19 us
  transfers between devices with their start and end apart: 6, of which 3 were waited for; matrix products, arithmetic and copies ran while one was open for 0% of the time, Pallas kernels for 47%

profile of v12, /device:TPU:0, one launch (start us, length us, event | category | flops | bytes accessed | tf_op | source)
XLA Modules:
  0.0 45.8 jit_solution(11021045511683620327)
XLA Ops:
  0.0 1.2 %leading_pieces.1 = bf16[1552,128]{1,0:T(8,128)(2,1)S(1)} custom-call(bf16[2048,512]{1,0:T(8,128)(2,1)} %f_ref.3, s32[8,32]{1,0:T(8,128)} %bitcast.4, s32[1,32]{1,0:T(1,128)} %bitcast.6), custom_call_target="tpu_custom_call" | custom-call | bytes 786432 | tf_op jit(solution)/shard_map/leading_pieces/pallas_call | solution.py:136
  1.2 4.0 %collective-permute-start.8 = (bf16[1552,128]{1,0:T(8,128)(2,1)S(1)}, bf16[1552,128]{1,0:T(8,128)(2,1)S(1)}, u32[]{:S(2)}, u32[]{:S(2)}) collective-permute-start(bf16[1552,128]{1,0:T(8,128)(2,1)S(1)} %leading_pieces.1), channel_id=1, source_target_pairs={{1,0},{2,1},{3,2},{0,3},{5,4},{6,5},{7,6},{4,7},{9,8},{10,9},{11,1... | collective-permute-start | bytes 1191944 | tf_op jit(solution)/shard_map/ppermute | solution.py:21
  5.2 0.0 copy-done.3
  5.2 0.0 copy-done.2
  5.2 3.1 %pack_live_pieces.1 = (bf16[8192,128]{1,0:T(8,128)(2,1)S(1)}, bf16[2560,128]{1,0:T(8,128)(2,1)S(1)}, s32[3,33]{1,0:T(4,128)S(1)}) custom-call(s32[16,32]{1,0:T(8,128)S(1)} %pad_add_fusion.notes, bf16[2048,512]{1,0:T(8,128)(2,1)S(1)} %copy-done), custom_call_target="tpu_custom_call" | custom-call | bytes 4194304 | tf_op jit(solution)/shard_map/pack_live_pieces/pallas_call | solution.py:197
  8.3 0.7 %collective-permute-start.11 = (bf16[2560,128]{1,0:T(8,128)(2,1)S(1)}, bf16[2560,128]{1,0:T(8,128)(2,1)S(1)}, u32[]{:S(2)}, u32[]{:S(2)}) collective-permute-start(bf16[2560,128]{1,0:T(8,128)(2,1)S(1)} %get-tuple-element.385), channel_id=1, source_target_pairs={{1,0},{2,1},{3,2},{0,3},{5,4},{6,5},{7,6},{4,7},{9,8},{10,9},{11,1... | collective-permute-start | bytes 1966088 | tf_op jit(solution)/shard_map/ppermute | solution.py:21
  9.0 0.0 copy-done.1
  9.0 2.6 %collective-permute-start.12 = (bf16[1536,512]{1,0:T(8,128)(2,1)S(1)}, bf16[1536,512]{1,0:T(8,128)(2,1)}, u32[]{:S(2)}, u32[]{:S(2)}) collective-permute-start(bf16[1536,512]{1,0:T(8,128)(2,1)S(1)} %copy-done.1), channel_id=1, source_target_pairs={{4,0},{8,4},{12,8},{16,12},{20,16},{24,20},{28,24},{0,28},{5,1},{9... | collective-permute-start | bytes 4718600 | tf_op jit(solution)/shard_map/ppermute | solution.py:21
  11.6 1.5 %cut_pieces.1 = (bf16[256,128]{1,0:T(8,128)(2,1)S(1)}, bf16[512,128]{1,0:T(8,128)(2,1)S(1)}, bf16[768,128]{1,0:T(8,128)(2,1)S(1)}, bf16[1024,128]{1,0:T(8,128)(2...) custom-call(bf16[8192,128]{1,0:T(8,128)(2,1)S(1)} %get-tuple-element, ...), custom_call_target="tpu_custom_call" | custom-call | bytes 5898240 | tf_op jit(solution)/shard_map/cut_pieces/pallas_call | solution.py:232
  13.2 6.9 %step_first.1.refs_13_ = f32[2048,512]{1,0:T(8,128)} custom-call(s32[16,32]{1,0:T(8,128)S(1)} %pad_add_fusion.notes, s32[3,33]{1,0:T(4,128)S(1)} %get-tuple-element.380.table, bf16[8192,128]{1,0:T(8,128)(2,1)S(1)} %get-tuple-element.378.packed_ref.refs_0_, bf16[1536,512]{1,0:T(8,128)(2,1)} %refs_1_.1), custom_call_target="tpu_custom_call" | custom-call | flops 536870912 | bytes 4194304 | tf_op jit(solution)/shard_map/step_first/pallas_call | solution.py:367
  20.0 0.0 collective-permute-done.8.refs_1_
  20.0 1.2 %collective-permute-start.10 = (bf16[512,128]{1,0:T(8,128)(2,1)S(1)}, bf16[512,128]{1,0:T(8,128)(2,1)S(1)}, u32[]{:S(2)}, u32[]{:S(2)}) collective-permute-start(bf16[512,128]{1,0:T(8,128)(2,1)S(1)} %get-tuple-element.384), channel_id=1, source_target_pairs={{1,0},{2,1},{3,2},{0,3},{5,4},{6,5},{7,6},{4,7},{9,8},{10,9},{11,1... | collective-permute-start | bytes 393224 | tf_op jit(solution)/shard_map/ppermute | solution.py:21
  21.2 1.8 %read_notes.1 = (s32[3,33]{1,0:T(4,128)S(1)}, s32[8,128]{1,0:T(8,128)S(1)}) custom-call(s32[16,32]{1,0:T(8,128)S(1)} %pad_add_fusion.notes, s32[16,32]{1,0:T(8,128)S(1)} %convert_convert_fusion.notes_next.notes), custom_call_target="tpu_custom_call" | custom-call | flops 21474836480 | bytes 4096 | tf_op jit(solution)/shard_map/read_notes/pallas_call | solution.py:91
  23.0 1.8 %collective-permute-start.9 = (s32[8,128]{1,0:T(8,128)S(1)}, s32[8,128]{1,0:T(8,128)S(1)}, u32[]{:S(2)}, u32[]{:S(2)}) collective-permute-start(s32[8,128]{1,0:T(8,128)S(1)} %get-tuple-element.383.one_ref), channel_id=1, source_target_pairs={{2,0},{3,1},{0,2},{1,3},{6,4},{7,5},{4,6},{5,7},{10,8},{11,9},{8,1... | collective-permute-start | bytes 12296 | tf_op jit(solution)/shard_map/ppermute | solution.py:21
  24.9 1.9 %collective-permute-done.9.other_ref = s32[8,128]{1,0:T(8,128)S(1)} collective-permute-done((s32[8,128]{1,0:T(8,128)S(1)}, s32[8,128]{1,0:T(8,128)S(1)}, u32[]{:S(2)}, u32[]{:S(2)}) %collective-permute-start.9) | collective-permute-done | bytes 4128 | tf_op jit(solution)/shard_map/ppermute | solution.py:21
  26.7 0.7 %pick_size.1.refs_0_ = s32[1]{0:T(128)} custom-call(s32[8,128]{1,0:T(8,128)S(1)} %get-tuple-element.383.one_ref, s32[8,128]{1,0:T(8,128)S(1)} %collective-permute-done.9.other_ref), custom_call_target="tpu_custom_call" | custom-call | bytes 4096 | tf_op jit(solution)/shard_map/pick_size/pallas_call | solution.py:112
  28.0 0.9 %collective-permute-done.11.refs_3_ = bf16[2560,128]{1,0:T(8,128)(2,1)S(1)} collective-permute-done((bf16[2560,128]{1,0:T(8,128)(2,1)S(1)}, bf16[2560,128]{1,0:T(8,128)(2,1)S(1)}, u32[]{:S(2)}, u32[]{:S(2)}) %collective-permute-start.11) | collective-permute-done | bytes 655392 | tf_op jit(solution)/shard_map/ppermute | solution.py:21
  28.8 0.7 %collective-permute-done.12.refs_12_ = bf16[1536,512]{1,0:T(8,128)(2,1)} collective-permute-done((bf16[1536,512]{1,0:T(8,128)(2,1)S(1)}, bf16[1536,512]{1,0:T(8,128)(2,1)}, u32[]{:S(2)}, u32[]{:S(2)}) %collective-permute-start.12) | collective-permute-done | bytes 1572896 | tf_op jit(solution)/shard_map/ppermute | solution.py:21
  29.6 10.2 %conditional.1 = (bf16[2048,512]{1,0:T(8,128)(2,1)}, bf16[256,128]{1,0:T(8,128)(2,1)S(1)}, bf16[512,128]{1,0:T(8,128)(2,1)}, bf16[768,128]{1,0:T(8,128)(2,1)}, b...) conditional(s32[]{:T(128)} %bitcast.3, ...), branch_computations={%region_0.0_spmd, %region_1.0_spmd, %region_2.0_spmd, %region_3.0_... | conditional | flops 536870912 | bytes 7995504 | solution.py:437
  29.6 2.7 %collective-permute-start.2 = (bf16[768,128]{1,0:T(8,128)(2,1)S(1)}, bf16[768,128]{1,0:T(8,128)(2,1)}, u32[]{:S(2)}, u32[]{:S(2)}) collective-permute-start(bf16[768,128]{1,0:T(8,128)(2,1)S(1)} %get-tuple-element.265), channel_id=1, source_target_pairs={{1,0},{2,1},{3,2},{0,3},{5,4},{6,5},{7,6},{4,7},{9,8},{10,9},{11,1... | collective-permute-start | bytes 589832 | tf_op jit(solution)/shard_map/cond/branch_2_fun/ppermute | solution.py:21
  32.3 7.5 %step_early.10 = bf16[2048,512]{1,0:T(8,128)(2,1)} custom-call(s32[16,32]{1,0:T(8,128)S(1)} %get-tuple-element.257.notes, s32[3,33]{1,0:T(4,128)S(1)} %get-tuple-element.258.table, bf16[1552,128]{1,0:T(8,128)(2,1)S(1)} %get-tuple-element.259.refs_0_, bf16[2560,128]{1,0:T(8,128)(2,1)S(1)} %get-tuple-element.260.refs_1_, ...), custom_call_target="tpu_custom_call" | custom-call | flops 536870912 | bytes 4194304 | tf_op jit(solution)/shard_map/cond/branch_2_fun/step_early/pallas_call | solution.py:367
  39.8 0.0 collective-permute-done.2
  39.8 0.0 collective-permute-done.10.refs_2_
  39.8 6.0 %step_late.1 = bf16[2048,512]{1,0:T(8,128)(2,1)} custom-call(s32[16,32]{1,0:T(8,128)S(1)} %convert_convert_fusion.notes_next.notes, s32[3,33]{1,0:T(4,128)S(1)} %get-tuple-element.382.table, s32[1]{0:T(128)} %pick_size.1.refs_0_, bf16[1552,128]{1,0:T(8,128)(2,1)S(1)} %collective-permute-done.8.refs_1_, ...), custom_call_target="tpu_custom_call", output_to_operand_aliasing={{}: (16, {})} | custom-call | flops 536870912 | bytes 4194304 | tf_op jit(solution)/shard_map/step_late/pallas_call | solution.py:367
  (9 shorter events, 0.0 us)
Async XLA Ops:
  0.0 5.2 %copy-start = (bf16[2048,512]{1,0:T(8,128)(2,1)S(1)}, bf16[2048,512]{1,0:T(8,128)(2,1)}, u32[]{:S(2)}) copy-start(bf16[2048,512]{1,0:T(8,128)(2,1)} %f_ref.3) | copy-start | bytes 6291460
  0.0 5.2 %copy-start.3 = (s32[32,1]{0,1:T(1,128)S(1)}, s32[32,1]{0,1:T(1,128)}, u32[]{:S(2)}) copy-start(s32[32,1]{0,1:T(1,128)} %param.14) | copy-start | bytes 388
  0.0 5.2 %copy-start.2 = (s32[32,8]{0,1:T(8,128)S(1)}, s32[32,8]{0,1:T(8,128)}, u32[]{:S(2)}) copy-start(s32[32,8]{0,1:T(8,128)} %param.13) | copy-start | bytes 3076
  0.0 9.0 %copy-start.1 = (bf16[1536,512]{1,0:T(8,128)(2,1)S(1)}, bf16[1536,512]{1,0:T(8,128)(2,1)}, u32[]{:S(2)}) copy-start(bf16[1536,512]{1,0:T(8,128)(2,1)} %refs_1_.1) | copy-start | bytes 4718596
  1.2 18.8 %collective-permute-start.8 = (bf16[1552,128]{1,0:T(8,128)(2,1)S(1)}, bf16[1552,128]{1,0:T(8,128)(2,1)S(1)}, u32[]{:S(2)}, u32[]{:S(2)}) collective-permute-start(bf16[1552,128]{1,0:T(8,128)(2,1)S(1)} %leading_pieces.1), channel_id=1, source_target_pairs={{1,0},{2,1},{3,2},{0,3},{5,4},{6,5},{7,6},{4,7},{9,8},{10,9},{11,1... | collective-permute-start | bytes 1191944 | tf_op jit(solution)/shard_map/ppermute | solution.py:21
  8.3 20.5 %collective-permute-start.11 = (bf16[2560,128]{1,0:T(8,128)(2,1)S(1)}, bf16[2560,128]{1,0:T(8,128)(2,1)S(1)}, u32[]{:S(2)}, u32[]{:S(2)}) collective-permute-start(bf16[2560,128]{1,0:T(8,128)(2,1)S(1)} %get-tuple-element.385), channel_id=1, source_target_pairs={{1,0},{2,1},{3,2},{0,3},{5,4},{6,5},{7,6},{4,7},{9,8},{10,9},{11,1... | collective-permute-start | bytes 1966088 | tf_op jit(solution)/shard_map/ppermute | solution.py:21
  9.0 20.6 %collective-permute-start.12 = (bf16[1536,512]{1,0:T(8,128)(2,1)S(1)}, bf16[1536,512]{1,0:T(8,128)(2,1)}, u32[]{:S(2)}, u32[]{:S(2)}) collective-permute-start(bf16[1536,512]{1,0:T(8,128)(2,1)S(1)} %copy-done.1), channel_id=1, source_target_pairs={{4,0},{8,4},{12,8},{16,12},{20,16},{24,20},{28,24},{0,28},{5,1},{9... | collective-permute-start | bytes 4718600 | tf_op jit(solution)/shard_map/ppermute | solution.py:21
  20.0 19.7 %collective-permute-start.10 = (bf16[512,128]{1,0:T(8,128)(2,1)S(1)}, bf16[512,128]{1,0:T(8,128)(2,1)S(1)}, u32[]{:S(2)}, u32[]{:S(2)}) collective-permute-start(bf16[512,128]{1,0:T(8,128)(2,1)S(1)} %get-tuple-element.384), channel_id=1, source_target_pairs={{1,0},{2,1},{3,2},{0,3},{5,4},{6,5},{7,6},{4,7},{9,8},{10,9},{11,1... | collective-permute-start | bytes 393224 | tf_op jit(solution)/shard_map/ppermute | solution.py:21
  23.0 3.7 %collective-permute-start.9 = (s32[8,128]{1,0:T(8,128)S(1)}, s32[8,128]{1,0:T(8,128)S(1)}, u32[]{:S(2)}, u32[]{:S(2)}) collective-permute-start(s32[8,128]{1,0:T(8,128)S(1)} %get-tuple-element.383.one_ref), channel_id=1, source_target_pairs={{2,0},{3,1},{0,2},{1,3},{6,4},{7,5},{4,6},{5,7},{10,8},{11,9},{8,1... | collective-permute-start | bytes 12296 | tf_op jit(solution)/shard_map/ppermute | solution.py:21
  29.6 10.2 %collective-permute-start.2 = (bf16[768,128]{1,0:T(8,128)(2,1)S(1)}, bf16[768,128]{1,0:T(8,128)(2,1)}, u32[]{:S(2)}, u32[]{:S(2)}) collective-permute-start(bf16[768,128]{1,0:T(8,128)(2,1)S(1)} %get-tuple-element.265), channel_id=1, source_target_pairs={{1,0},{2,1},{3,2},{0,3},{5,4},{6,5},{7,6},{4,7},{9,8},{10,9},{11,1... | collective-permute-start | bytes 589832 | tf_op jit(solution)/shard_map/cond/branch_2_fun/ppermute | solution.py:21
